TPU v7x, 32 devices: a whole 2x2x4 slice. The times are simulated.
32 devices in a mesh: replica: 2 (over y), tensor: 16 (over z, x, core).
Axes of the slice: x: 2, y: 2, z: 4, core: 2. Of those that a mesh axis runs over, the one named last changes fastest.
Arguments:
- activations: bfloat16 [8192, 832], P(('replica', 'tensor')), may hold values from -6 to 6
- out_grad: bfloat16 [8192, 7168], P('replica', 'tensor'), may hold values from -0.09375 to 0.09375
- master_weights: float32 [1664, 7168], P('replica', 'tensor'), may hold values from -6 to 6
- first_moment: float32 [1664, 7168], P('replica', 'tensor'), may hold values from -0.6 to 0.6
- second_moment: float32 [1664, 7168], P('replica', 'tensor'), may hold values from 0.01 to 1
- anchor: float32 [832, 7168], P(None, 'tensor'), may hold values from -6 to 6
- outer_momentum: float32 [832, 7168], P(None, 'tensor'), may hold values from -3 to 3
Outputs:
- rebuilt_weights: bfloat16 [832, 7168], P(None, 'tensor')
- new_momentum: float32 [832, 7168], P(None, 'tensor')
All inputs are finite; a program needn't handle non-finite values.
Results may differ from a plain program's by a relative error of at most 0.001.
Values may be sent and summed in bfloat16 or wider, within the bound.
No kernel may reach another device: no remote copies, remote signals or barrier semaphores. Data moves between devices by JAX's collectives and lax.ppermute only.
A program may use at most 128 MiB of HBM per device.

v0:
```python
import jax
import jax.numpy as jnp
from jax import lax
from jax.sharding import PartitionSpec as P

BETA_ONE = 0.9
BETA_TWO = 0.95
BIAS_ONE = 0.9999734386
BIAS_TWO = 0.9940794708
EPSILON = 1e-08
INNER_RATE = 0.25
DECAY_RATE = 0.1
OUTER_RATE = 0.7
NESTEROV = 0.9


def outer_update(pseudo_mean, anchor_rows, momentum_rows):
    new_momentum = NESTEROV * momentum_rows + pseudo_mean
    rebuilt = anchor_rows - OUTER_RATE * (pseudo_mean + NESTEROV * new_momentum)
    return (rebuilt.astype(jnp.bfloat16), new_momentum)


def on_device(
    activations, out_grad, master_weights, first_moment, second_moment, anchor, outer_momentum
):
    numbers = (((0,), (0,)), ((), ()))
    gathered = lax.all_gather(activations, "tensor", axis=0, tiled=True)
    gradient = lax.dot_general(gathered, out_grad, numbers, preferred_element_type=jnp.float32)
    moment_one = BETA_ONE * first_moment + (1.0 - BETA_ONE) * gradient
    moment_two = BETA_TWO * second_moment + (1.0 - BETA_TWO) * gradient * gradient
    step_size = moment_one / BIAS_ONE / (jnp.sqrt(moment_two / BIAS_TWO) + EPSILON)
    updated = master_weights - INNER_RATE * (step_size + DECAY_RATE * master_weights)
    pseudo = anchor - updated
    groups = lax.axis_size("replica")
    summed = lax.psum(pseudo, "replica")
    return outer_update(summed / groups, anchor, outer_momentum)


def solution(mesh):
    placed = (
        P(("replica", "tensor"), None),
        P("replica", "tensor"),
        P("replica", "tensor"),
        P("replica", "tensor"),
        P("replica", "tensor"),
        P(None, "tensor"),
        P(None, "tensor"),
    )
    return jax.shard_map(
        on_device,
        mesh=mesh,
        in_specs=placed,
        out_specs=(P(None, "tensor"), P(None, "tensor")),
        check_vma=False,
    )
```

profile of v0, /device:TPU:0, one launch (start us, length us, event | category | flops | bytes accessed | tf_op | source)
XLA Modules:
  0.0 154.4 jit_solution(15599914343387089846)
XLA Ops:
  7.2 0.0 all-gather.2.cloned.1.call-start
  7.2 0.7 all-gather.2.cloned.1.call-update
  7.9 0.0 all-reduce.2.cloned.1.call-start
  7.9 73.7 %all-gather.2.cloned.1.call-done = bf16[4096,832]{0,1:T(8,128)(2,1)} async-done(((bf16[256,832]{0,1:T(8,128)(2,1)}), bf16[4096,832]{0,1:T(8,128)(2,1)}) %all-gather.2.cloned.1.call-update) | async-done | bytes 6815760 | tf_op jit(solution)/shard_map/all_gather | solution.py:27
  81.7 0.0 copy-start.1
  81.7 12.1 %subtract_subtract_fusion = f32[832,448]{0,1:T(8,128)} fusion(f32[832,448]{0,1:T(8,128)} %param.12, f32[832,448]{0,1:T(8,128)} %param.9, f32[832,448]{0,1:T(8,128)} %param.11, f32[832,448]{0,1:T(8,128)} %param.10, bf16[4096,832]{0,1:T(8,128)(2,1)} %all-gather.2.cloned.1.call-done, bf16[4096,448]{0,1:T(8,128)(2,1)} %param.8), kind=kOutput, calls=%fused_computation.9 | convolution fusion | flops 3059417088 | bytes 17940480 | tf_op jit(solution)/shard_map/dot_general | solution.py:28
  93.8 0.0 copy-start
  93.8 0.0 all-reduce.2.cloned.1.call-update
  93.8 50.5 %all-reduce.2.cloned.1.call-done = f32[832,448]{0,1:T(8,128)} async-done(((f32[832,448]{0,1:T(8,128)}), f32[832,448]{0,1:T(8,128)}) %all-reduce.2.cloned.1.call-update) | async-done | bytes 1490960 | tf_op jit(solution)/shard_map/psum | solution.py:35
  144.4 0.0 copy-done.1
  144.4 0.0 copy-done
  144.4 3.2 %subtract_convert_fusion = (bf16[832,448]{0,1:T(8,128)(2,1)}, f32[832,448]{0,1:T(8,128)}) fusion(f32[832,448]{0,1:T(8,128)S(1)} %copy-done, f32[832,448]{0,1:T(8,128)} %all-reduce.2.cloned.1.call-done, f32[832,448]{0,1:T(8,128)S(1)} %copy-done.1), kind=kLoop, calls=%fused_computation.7 | loop fusion | flops 2981888 | bytes 6709248 | tf_op jit(solution)/shard_map/convert_element_type | solution.py:20
Async XLA Ops:
  7.2 74.5 %all-gather.2.cloned.1.call-start = ((), (), s32[]{:S(2)}) async-start(), calls=%async_computation | async-start | bytes 7241728 | tf_op jit(solution)/shard_map/all_gather | solution.py:27
  7.9 136.5 %all-reduce.2.cloned.1.call-start = ((), (), s32[]{:S(2)}) async-start(), calls=%async_computation.1 | async-start | bytes 3211264 | tf_op jit(solution)/shard_map/psum | solution.py:35
  81.7 62.7 %copy-start.1 = (f32[832,448]{0,1:T(8,128)S(1)}, f32[832,448]{0,1:T(8,128)}, u32[]{:S(2)}) copy-start(f32[832,448]{0,1:T(8,128)} %param.13) | copy-start | bytes 4472836
  93.8 50.6 %copy-start = (f32[832,448]{0,1:T(8,128)S(1)}, f32[832,448]{0,1:T(8,128)}, u32[]{:S(2)}) copy-start(f32[832,448]{0,1:T(8,128)} %param.12) | copy-start | bytes 4472836
Sparse Core Ops, SparseCore 0:
  10.2 71.4 all-gather.1
  94.0 50.3 all-reduce.1
where the time goes:
time: 155 us; the launch traced here: 154 us
  waiting for transfers between devices  125 us (81%)
  between operations  14 us (9%)
  matrix products  12.1 us (8%)
  other arithmetic  3.25 us (2%)
    all_gather x1, waiting for transfers between devices, on_device(): gathered = lax.all_gather(activations, 'tensor', axis=0, tiled=True)  73.7 us
    psum x1, waiting for transfers between devices, on_device(): summed = lax.psum(pseudo, 'replica')  50.5 us
    dot_general x1, matrix products, on_device(): lax.dot_general(gathered, out_grad, numbers, preferred_element_type=jnp.f...  12.1 us
    convert_element_type x1, other arithmetic, outer_update(): return (rebuilt.astype(jnp.bfloat16), new_momentum)  3.25 us
  transfers between devices with their start and end apart: 2, of which 2 were waited for; matrix products, arithmetic and copies ran while one was open for 0% of the time, Pallas kernels for 0%

commit v1 on v0

v1 whole, which is shorter than its diff:
```python
import functools

import jax
import jax.numpy as jnp
import numpy as np
from jax import lax
from jax.experimental import pallas as pl
from jax.experimental.pallas import tpu as pltpu
from jax.sharding import PartitionSpec as P

BETA_ONE = 0.9
BETA_TWO = 0.95
BIAS_ONE = 0.9999734386
BIAS_TWO = 0.9940794708
EPSILON = 1e-08
INNER_RATE = 0.25
DECAY_RATE = 0.1
OUTER_RATE = 0.7
NESTEROV = 0.9
CORES = 2
LANES = 128


def chip_ring(chips):
    return list(range(0, chips, 2)) + list(range(chips - 1, 0, -2))


def neighbour_exchange(size):
    ring = chip_ring(size // CORES)
    chips = len(ring)
    partner = [[0] * size for _ in range(2)]
    for kind in range(2):
        for core in range(CORES):
            for at in range(chips):
                other = at + 1 if (at + kind + core) % 2 == 0 else at - 1
                partner[kind][ring[at] * CORES + core] = ring[other % chips] * CORES + core
    held = [[d] for d in range(size)]
    sent = [[d] for d in range(size)]
    for step in range(chips // 2):
        came = [sent[partner[step % 2][d]] for d in range(size)]
        held = [h + c for h, c in zip(held, came)]
        sent = [h[:2] for h in held] if step == 0 else came
    pairs = [[(d, p) for d, p in enumerate(kind)] for kind in partner]
    return pairs, np.array(held, np.int32)


def feature_cuts(features):
    tiles = features // LANES
    return [0, LANES * ((tiles + 1) // 2), LANES * (tiles - 1), features]


def gradient_kernel(low, tokens, starts_ref, mine_ref, theirs_ref, own_ref, first_ref, *refs):
    later, (keep_ref, give_ref, grad, acts, sems) = refs[:-5], refs[-5:]
    count = keep_ref.shape[1]
    columns = keep_ref.shape[0]
    blocks = starts_ref.shape[1]
    halves = [[], []]

    def begin(half, source, target):
        copy = pltpu.make_async_copy(source, target, sems.at[sum(map(len, halves))])
        copy.start()
        halves[half].append(copy)

    for at in range(blocks):
        half = at * 2 // blocks
        here = pl.ds(at * tokens, tokens)
        there = pl.ds(pl.multiple_of(starts_ref[0, at] * tokens, LANES), tokens)
        begin(half, mine_ref.at[:, there], grad.at[pl.ds(0, columns), here])
        begin(half, theirs_ref.at[:, there], grad.at[pl.ds(columns, columns), here])
        if at < 2:
            begin(half, (own_ref, first_ref)[at].at[pl.ds(low, count), :], acts.at[:, here])
        elif at % 2 == 0:
            begin(half, later[at // 2 - 1], acts.at[:, pl.ds(at * tokens, 2 * tokens)])
    cut = (blocks // 2) * tokens
    for half, span in enumerate((slice(0, cut), slice(cut, blocks * tokens))):
        for copy in halves[half]:
            copy.wait()
        for at, out in enumerate((keep_ref, give_ref)):
            product = lax.dot_general(
                grad[at * columns : (at + 1) * columns, span],
                acts[:, span],
                (((1,), (1,)), ((), ())),
                preferred_element_type=jnp.float32,
            )
            out[...] = product if half == 0 else out[...] + product


def partial_gradient(low, high, starts, mine, theirs, own, first, later):
    tokens, columns, blocks = own.shape[1], mine.shape[0], starts.shape[1]
    count = high - low
    out = jax.ShapeDtypeStruct((columns, count), jnp.float32)
    return pl.pallas_call(
        functools.partial(gradient_kernel, low, tokens),
        out_shape=(out, out),
        in_specs=[pl.BlockSpec(memory_space=pltpu.SMEM)]
        + [pl.BlockSpec(memory_space=pl.ANY)] * (4 + len(later)),
        out_specs=(pl.BlockSpec(memory_space=pltpu.VMEM),) * 2,
        scratch_shapes=[
            pltpu.VMEM((CORES * columns, blocks * tokens), mine.dtype),
            pltpu.VMEM((count, blocks * tokens), own.dtype),
            pltpu.SemaphoreType.DMA((3 * blocks,)),
        ],
        compiler_params=pltpu.CompilerParams(vmem_limit_bytes=32 * 2**20),
        cost_estimate=pl.CostEstimate(
            flops=2 * CORES * columns * count * blocks * tokens,
            bytes_accessed=2 * (CORES * columns + count) * blocks * tokens + 8 * columns * count,
            transcendentals=0,
        ),
        name="gradient",
    )(starts, mine, theirs, own, first, *later)


def start_to_half(anchor, weights):
    exact = anchor - (1.0 - INNER_RATE * DECAY_RATE) * weights
    return exact, lax.reduce_precision(exact, 5, 10)


def late_part(gradient, first_moment, second_moment, weights, anchor):
    moment_one = BETA_ONE * first_moment + (1.0 - BETA_ONE) * gradient
    moment_two = BETA_TWO * second_moment + (1.0 - BETA_TWO) * gradient * gradient
    step = moment_one / BIAS_ONE / (jnp.sqrt(moment_two / BIAS_TWO) + EPSILON)
    exact, half = start_to_half(anchor, weights)
    return ((exact - half) + INNER_RATE * step).astype(jnp.float16)


def on_device(
    activations, out_grad, master_weights, first_moment, second_moment, anchor, outer_momentum
):
    size = lax.axis_size("tensor")
    groups = lax.axis_size("replica")
    pairs, held = neighbour_exchange(size)
    swap = [(d, d ^ 1) for d in range(size)]
    own, mine = activations.T, out_grad.T
    weights, one, two = master_weights.T, first_moment.T, second_moment.T
    anchor, momentum = anchor.T, outer_momentum.T
    cuts = feature_cuts(own.shape[0])
    spans = list(zip(cuts[:-1], cuts[1:]))
    starts = lax.dynamic_slice_in_dim(jnp.asarray(held), lax.axis_index("tensor"), 1, 0)

    def other_groups_sum(value):
        total = None
        for hop in range(1, groups):
            there = [(g, (g + hop) % groups) for g in range(groups)]
            came = lax.ppermute(value, "replica", there).astype(jnp.float32)
            total = came if total is None else total + came
        return total

    first = lax.ppermute(own, "tensor", pairs[0])
    theirs = lax.ppermute(mine, "tensor", swap)
    early = start_to_half(anchor, weights)[1]
    early_others = other_groups_sum(early.astype(jnp.float16))

    rebuilt = jnp.zeros(anchor.shape, jnp.bfloat16)
    new_momentum = jnp.zeros(anchor.shape, jnp.float32)
    for low, high in spans:
        block = jnp.concatenate([own[low:high], first[low:high]], axis=1)
        later = []
        for step in range(1, held.shape[1] // 2):
            block = lax.ppermute(block, "tensor", pairs[step % 2])
            later.append(block)
        keep, give = partial_gradient(low, high, starts, mine, theirs, own, first, later)
        gradient = keep + lax.ppermute(give, "tensor", swap)
        here = lambda x: x[:, low:high]
        late = late_part(gradient, here(one), here(two), here(weights), here(anchor))
        late_others = other_groups_sum(late)
        mean = ((here(early) + here(early_others)) + (late.astype(jnp.float32) + late_others)) / groups
        moved = NESTEROV * here(momentum) + mean
        weight = here(anchor) - OUTER_RATE * (mean + NESTEROV * moved)
        rebuilt = lax.dynamic_update_slice(rebuilt, weight.astype(jnp.bfloat16), (0, low))
        new_momentum = lax.dynamic_update_slice(new_momentum, moved, (0, low))
    return rebuilt.T, new_momentum.T


def solution(mesh):
    placed = (
        P(("replica", "tensor"), None),
        P("replica", "tensor"),
        P("replica", "tensor"),
        P("replica", "tensor"),
        P("replica", "tensor"),
        P(None, "tensor"),
        P(None, "tensor"),
    )
    return jax.shard_map(
        on_device,
        mesh=mesh,
        in_specs=placed,
        out_specs=(P(None, "tensor"), P(None, "tensor")),
        check_vma=False,
    )
```

time: 155 us -> 92.5 us (0.60)
  waiting for transfers between devices: 125 us -> 45.5 us
  starting transfers between devices: 0.08 us -> 22 us
  between operations: 14 us -> 0.93 us
  matrix products: 12.1 us -> 0 us
  Pallas kernels: 0 us -> 11.5 us
  local copies, waits for them, and re-layouts: 0.01 us -> 5.24 us
  other arithmetic: 3.25 us -> 7.04 us
    all_gather x1 -> x0, waiting for transfers between devices: 73.7 us -> none  [on_device(): gathered = lax.all_gather(activations, 'tensor', axis=0, tiled=True)]
    psum x1 -> x0, waiting for transfers between devices: 50.5 us -> none  [on_device(): summed = lax.psum(pseudo, 'replica')]
    ppermute x0 -> x18, waiting for transfers between devices: none -> 45.5 us  [the longest x9 25.5 us: on_device(): block = lax.ppermute(block, 'tensor', pairs[step % 2])]
    ppermute x0 -> x18, starting transfers between devices: none -> 22 us  [the longest x9 12.8 us: on_device(): block = lax.ppermute(block, 'tensor', pairs[step % 2])]
    dot_general x1 -> x0, matrix products: 12.1 us -> none  [on_device(): lax.dot_general(gathered, out_grad, numbers, preferred_element_type=jnp.f...]
    pallas_call x0 -> x3, Pallas kernels: none -> 11.5 us  [partial_gradient(): pl.pallas_call(functools.partial(gradient_kernel, low, tokens), out_shape...]
    unnamed x4 -> x22, local copies, waits for them, and re-layouts: 0.01 us -> 3.35 us
    convert_element_type x1 -> x5, other arithmetic: 3.25 us -> 6.04 us  [the longest x1 3.76 us: on_device(): early_others = other_groups_sum(early.astype(jnp.float16))]
  transfers between devices with their start and end apart: 2 -> 18, of which waited for: 2 -> 9; matrix products, arithmetic and copies ran while one was open for 0% -> 9% of each run, Pallas kernels for 0% -> 12%
where the time goes in v1:
time: 92.5 us; the launch traced here: 92.2 us
  waiting for transfers between devices  45.5 us (49%)
  starting transfers between devices  22 us (24%)
  Pallas kernels  11.5 us (12%)
  other arithmetic  7.04 us (8%)
  local copies, waits for them, and re-layouts  5.24 us (6%)
  between operations  0.93 us (1%)
    ppermute x9, waiting for transfers between devices, on_device(): block = lax.ppermute(block, 'tensor', pairs[step % 2])  25.5 us
    ppermute x4, waiting for transfers between devices, other_groups_sum(): came = lax.ppermute(value, 'replica', there).astype(jnp.float32)  14.6 us
    ppermute x9, starting transfers between devices, on_device(): block = lax.ppermute(block, 'tensor', pairs[step % 2])  12.8 us
    pallas_call x3, Pallas kernels, partial_gradient(): pl.pallas_call(functools.partial(gradient_kernel, low, tokens), out_shape...  11.5 us
    ppermute x4, starting transfers between devices, other_groups_sum(): came = lax.ppermute(value, 'replica', there).astype(jnp.float32)  5.78 us
    ppermute x1, waiting for transfers between devices, on_device(): first = lax.ppermute(own, 'tensor', pairs[0])  5.34 us
    convert_element_type x1, other arithmetic, on_device(): early_others = other_groups_sum(early.astype(jnp.float16))  3.76 us
    unnamed x22, local copies, waits for them, and re-layouts  3.35 us
  transfers between devices with their start and end apart: 18, of which 9 were waited for; matrix products, arithmetic and copies ran while one was open for 9% of the time, Pallas kernels for 12%

profile of v1, /device:TPU:0, one launch (start us, length us, event | category | flops | bytes accessed | tf_op | source)
XLA Modules:
  0.0 92.2 jit_solution(337801223331624499)
XLA Ops:
  0.6 0.0 copy-start.2
  0.7 0.5 collective-permute-start.1
  1.2 2.7 %collective-permute-start.2 = (bf16[832,256]{1,0:T(8,128)(2,1)}, bf16[832,256]{1,0:T(8,128)(2,1)S(1)}, u32[]{:S(2)}, u32[]{:S(2)}) collective-permute-start(bf16[832,256]{1,0:T(8,128)(2,1)} %bitcast.17), channel_id=1, source_target_pairs={{0,4},{1,3},{2,6},{3,1},{4,0},{5,9},{6,2},{7,11},{8,12},{9,5},{10,... | collective-permute-start | bytes 1277960 | tf_op jit(solution)/shard_map/ppermute | solution.py:148
  3.8 1.0 %slice.116 = bf16[384,256]{1,0:T(8,128)(2,1)S(1)} slice(bf16[832,256]{1,0:T(8,128)(2,1)} %bitcast.18), slice={[0:384], [0:256]} | slice | bytes 393216 | tf_op jit(solution)/shard_map/slice | solution.py:156
  4.8 5.3 %collective-permute-done.2.first_ref = bf16[832,256]{1,0:T(8,128)(2,1)S(1)} collective-permute-done((bf16[832,256]{1,0:T(8,128)(2,1)}, bf16[832,256]{1,0:T(8,128)(2,1)S(1)}, u32[]{:S(2)}, u32[]{:S(2)}) %collective-permute-start.2) | collective-permute-done | bytes 426016 | tf_op jit(solution)/shard_map/ppermute | solution.py:148
  10.2 2.0 %collective-permute-start.3 = (bf16[384,512]{1,0:T(8,128)(2,1)S(1)}, bf16[384,512]{1,0:T(8,128)(2,1)S(1)}, u32[]{:S(2)}, u32[]{:S(2)}) collective-permute-start(bf16[384,512]{1,0:T(8,128)(2,1)S(1)} %pad_maximum_fusion), channel_id=1, source_target_pairs={{0,2},{1,5},{2,0},{3,7},{4,8},{5,1},{6,10},{7,3},{8,4},{9,13},{10,... | collective-permute-start | bytes 1179656 | tf_op jit(solution)/shard_map/ppermute | solution.py:159
  12.2 5.8 %collective-permute-done.3.refs_0_ = bf16[384,512]{1,0:T(8,128)(2,1)S(1)} collective-permute-done((bf16[384,512]{1,0:T(8,128)(2,1)S(1)}, bf16[384,512]{1,0:T(8,128)(2,1)S(1)}, u32[]{:S(2)}, u32[]{:S(2)}) %collective-permute-start.3) | collective-permute-done | bytes 393248 | tf_op jit(solution)/shard_map/ppermute | solution.py:159
  18.0 2.0 %collective-permute-start.4 = (bf16[384,512]{1,0:T(8,128)(2,1)S(1)}, bf16[384,512]{1,0:T(8,128)(2,1)S(1)}, u32[]{:S(2)}, u32[]{:S(2)}) collective-permute-start(bf16[384,512]{1,0:T(8,128)(2,1)S(1)} %collective-permute-done.3.refs_0_), channel_id=1, source_target_pairs={{0,4},{1,3},{2,6},{3,1},{4,0},{5,9},{6,2},{7,11},{8,12},{9,5},{10,... | collective-permute-start | bytes 1179656 | tf_op jit(solution)/shard_map/ppermute | solution.py:159
  20.1 1.6 %collective-permute-start.8 = (bf16[256,512]{1,0:T(8,128)(2,1)S(1)}, bf16[256,512]{1,0:T(8,128)(2,1)S(1)}, u32[]{:S(2)}, u32[]{:S(2)}) collective-permute-start(bf16[256,512]{1,0:T(8,128)(2,1)S(1)} %pad_maximum_fusion.1), channel_id=1, source_target_pairs={{0,2},{1,5},{2,0},{3,7},{4,8},{5,1},{6,10},{7,3},{8,4},{9,13},{10,... | collective-permute-start | bytes 786440 | tf_op jit(solution)/shard_map/ppermute | solution.py:159
  21.7 7.4 %collective-permute-done.4.refs_1_ = bf16[384,512]{1,0:T(8,128)(2,1)S(1)} collective-permute-done((bf16[384,512]{1,0:T(8,128)(2,1)S(1)}, bf16[384,512]{1,0:T(8,128)(2,1)S(1)}, u32[]{:S(2)}, u32[]{:S(2)}) %collective-permute-start.4) | collective-permute-done | bytes 393248 | tf_op jit(solution)/shard_map/ppermute | solution.py:159
  29.1 1.3 %collective-permute-start.5 = (bf16[384,512]{1,0:T(8,128)(2,1)S(1)}, bf16[384,512]{1,0:T(8,128)(2,1)S(1)}, u32[]{:S(2)}, u32[]{:S(2)}) collective-permute-start(bf16[384,512]{1,0:T(8,128)(2,1)S(1)} %collective-permute-done.4.refs_1_), channel_id=1, source_target_pairs={{0,2},{1,5},{2,0},{3,7},{4,8},{5,1},{6,10},{7,3},{8,4},{9,13},{10,... | collective-permute-start | bytes 1179656 | tf_op jit(solution)/shard_map/ppermute | solution.py:159
  30.4 3.8 %fusion.46 = (f16[448,832]{1,0:T(8,128)(2,1)}, f32[448,832]{1,0:T(8,128)}) fusion(f32[832,448]{0,1:T(8,128)} %param.10, f32[832,448]{0,1:T(8,128)S(1)} %copy-done.2), kind=kLoop, calls=%fused_computation.75 | loop fusion | flops 1490944 | bytes 5218304 | tf_op jit(solution)/shard_map/convert_element_type | solution.py:151
  34.1 1.5 %collective-permute-start = (f16[448,832]{1,0:T(8,128)(2,1)}, f16[448,832]{1,0:T(8,128)(2,1)S(1)}, u32[]{:S(2)}, u32[]{:S(2)}) collective-permute-start(f16[448,832]{1,0:T(8,128)(2,1)} %get-tuple-element.14), channel_id=1, source_target_pairs={{0,16},{16,0},{1,17},{17,1},{2,18},{18,2},{3,19},{19,3},{4,20},{20... | collective-permute-start | bytes 2236424 | tf_op jit(solution)/shard_map/ppermute | solution.py:144
  35.7 0.7 constant_dynamic-slice_fusion.starts_ref
  36.4 0.9 collective-permute-start.9
  37.3 1.9 %collective-permute-done.5.refs_2_ = bf16[384,512]{1,0:T(8,128)(2,1)S(1)} collective-permute-done((bf16[384,512]{1,0:T(8,128)(2,1)S(1)}, bf16[384,512]{1,0:T(8,128)(2,1)S(1)}, u32[]{:S(2)}, u32[]{:S(2)}) %collective-permute-start.5) | collective-permute-done | bytes 393248 | tf_op jit(solution)/shard_map/ppermute | solution.py:159
  39.2 2.0 %copy-done = bf16[4096,448]{0,1:T(8,128)(2,1)S(1)} copy-done((bf16[4096,448]{0,1:T(8,128)(2,1)S(1)}, bf16[4096,448]{0,1:T(8,128)(2,1)}, u32[]{:S(2)}) %copy-start) | copy-done | bytes 3670040
  41.2 4.4 %gradient.3 = (f32[448,384]{1,0:T(8,128)S(1)}, f32[448,384]{1,0:T(8,128)S(1)}) custom-call(s32[1,8]{1,0:T(1,128)S(1)} %constant_dynamic-slice_fusion.starts_ref, bf16[448,4096]{1,0:T(8,128)(2,1)S(1)} %bitcast.14, bf16[448,4096]{1,0:T(8,128)(2,1)} %collective-permute-done.1.theirs_ref, bf16[832,256]{1,0:T(8,128)(2,1)S(1)} %bitcast.21, ...), custom_call_target="tpu_custom_call" | custom-call | flops 1409286144 | bytes 6619136 | tf_op jit(solution)/shard_map/gradient/pallas_call | solution.py:92
  45.6 0.1 collective-permute-start.6
  45.7 1.3 %collective-permute-start.13 = (bf16[192,512]{1,0:T(8,128)(2,1)S(1)}, bf16[192,512]{1,0:T(8,128)(2,1)S(1)}, u32[]{:S(2)}, u32[]{:S(2)}) collective-permute-start(bf16[192,512]{1,0:T(8,128)(2,1)S(1)} %pad_maximum_fusion.2), channel_id=1, source_target_pairs={{0,2},{1,5},{2,0},{3,7},{4,8},{5,1},{6,10},{7,3},{8,4},{9,13},{10,... | collective-permute-start | bytes 589832 | tf_op jit(solution)/shard_map/ppermute | solution.py:159
  46.9 4.5 %collective-permute-done.13.refs_0_ = bf16[192,512]{1,0:T(8,128)(2,1)S(1)} collective-permute-done((bf16[192,512]{1,0:T(8,128)(2,1)S(1)}, bf16[192,512]{1,0:T(8,128)(2,1)S(1)}, u32[]{:S(2)}, u32[]{:S(2)}) %collective-permute-start.13) | collective-permute-done | bytes 196640 | tf_op jit(solution)/shard_map/ppermute | solution.py:159
  51.4 1.1 %collective-permute-start.14 = (bf16[192,512]{1,0:T(8,128)(2,1)S(1)}, bf16[192,512]{1,0:T(8,128)(2,1)S(1)}, u32[]{:S(2)}, u32[]{:S(2)}) collective-permute-start(bf16[192,512]{1,0:T(8,128)(2,1)S(1)} %collective-permute-done.13.refs_0_), channel_id=1, source_target_pairs={{0,4},{1,3},{2,6},{3,1},{4,0},{5,9},{6,2},{7,11},{8,12},{9,5},{10,... | collective-permute-start | bytes 589832 | tf_op jit(solution)/shard_map/ppermute | solution.py:159
  52.5 1.5 %collective-permute-start.10 = (bf16[256,512]{1,0:T(8,128)(2,1)S(1)}, bf16[256,512]{1,0:T(8,128)(2,1)S(1)}, u32[]{:S(2)}, u32[]{:S(2)}) collective-permute-start(bf16[256,512]{1,0:T(8,128)(2,1)S(1)} %collective-permute-done.9.refs_1_), channel_id=1, source_target_pairs={{0,2},{1,5},{2,0},{3,7},{4,8},{5,1},{6,10},{7,3},{8,4},{9,13},{10,... | collective-permute-start | bytes 786440 | tf_op jit(solution)/shard_map/ppermute | solution.py:159
  54.0 5.1 %collective-permute-done.14.refs_1_ = bf16[192,512]{1,0:T(8,128)(2,1)S(1)} collective-permute-done((bf16[192,512]{1,0:T(8,128)(2,1)S(1)}, bf16[192,512]{1,0:T(8,128)(2,1)S(1)}, u32[]{:S(2)}, u32[]{:S(2)}) %collective-permute-start.14) | collective-permute-done | bytes 196640 | tf_op jit(solution)/shard_map/ppermute | solution.py:159
  59.1 1.2 %collective-permute-start.15 = (bf16[192,512]{1,0:T(8,128)(2,1)S(1)}, bf16[192,512]{1,0:T(8,128)(2,1)S(1)}, u32[]{:S(2)}, u32[]{:S(2)}) collective-permute-start(bf16[192,512]{1,0:T(8,128)(2,1)S(1)} %collective-permute-done.14.refs_1_), channel_id=1, source_target_pairs={{0,2},{1,5},{2,0},{3,7},{4,8},{5,1},{6,10},{7,3},{8,4},{9,13},{10,... | collective-permute-start | bytes 589832 | tf_op jit(solution)/shard_map/ppermute | solution.py:159
  60.4 0.1 convert_element_type.43
  60.5 3.4 %gradient.4 = (f32[448,256]{1,0:T(8,128)S(1)}, f32[448,256]{1,0:T(8,128)S(1)}) custom-call(s32[1,8]{1,0:T(1,128)S(1)} %constant_dynamic-slice_fusion.starts_ref, bf16[448,4096]{1,0:T(8,128)(2,1)S(1)} %bitcast.15, bf16[448,4096]{1,0:T(8,128)(2,1)} %collective-permute-done.1.theirs_ref, bf16[832,256]{1,0:T(8,128)(2,1)S(1)} %bitcast.22, ...), custom_call_target="tpu_custom_call" | custom-call | flops 939524096 | bytes 5636096 | tf_op jit(solution)/shard_map/gradient/pallas_call | solution.py:92
  63.9 0.1 collective-permute-start.11
  64.0 0.8 collective-permute-done.15.refs_2_
  64.8 3.8 %gradient.5 = (f32[448,192]{1,0:T(8,128)S(1)}, f32[448,192]{1,0:T(8,128)S(1)}) custom-call(s32[1,8]{1,0:T(1,128)S(1)} %constant_dynamic-slice_fusion.starts_ref, bf16[448,4096]{1,0:T(8,128)(2,1)S(1)} %bitcast.16, bf16[448,4096]{1,0:T(8,128)(2,1)} %collective-permute-done.1.theirs_ref, bf16[832,256]{1,0:T(8,128)(2,1)S(1)} %bitcast.23, ...), custom_call_target="tpu_custom_call" | custom-call | flops 704643072 | bytes 5144576 | tf_op jit(solution)/shard_map/gradient/pallas_call | solution.py:92
  68.6 0.1 collective-permute-start.16
  68.7 0.9 %fusion.1 = f16[448,384]{1,0:T(8,128)(2,1)S(1)} fusion(f32[448,832]{1,0:T(8,128)S(1)} %bitcast.38, f32[448,832]{1,0:T(8,128)S(1)} %bitcast.41, f32[448,832]{1,0:T(8,128)S(1)} %bitcast.30, f32[448,384]{1,0:T(8,128)S(1)} %get-tuple-element.8, f32[448,384]{1,0:T(8,128)S(1)} %collective-permute-done.6, f32[448,832]{1,0:T(8,128)S(1)} %bitcast.24), kind=kLoop, calls=%fused_computation.4 | loop fusion | flops 3268608 | bytes 4472832 | tf_op jit(solution)/shard_map/convert_element_type | solution.py:123
  69.6 2.1 %collective-permute-start.7 = (f16[448,384]{1,0:T(8,128)(2,1)S(1)}, f16[448,384]{1,0:T(8,128)(2,1)S(1)}, u32[]{:S(2)}, u32[]{:S(2)}) collective-permute-start(f16[448,384]{1,0:T(8,128)(2,1)S(1)} %fusion.1), channel_id=1, source_target_pairs={{0,16},{16,0},{1,17},{17,1},{2,18},{18,2},{3,19},{19,3},{4,20},{20... | collective-permute-start | bytes 1032200 | tf_op jit(solution)/shard_map/ppermute | solution.py:144
  71.7 0.6 fusion.23
  72.4 0.8 collective-permute-start.17
  73.2 0.6 fusion.15
  73.8 1.3 %collective-permute-start.12 = (f16[448,256]{1,0:T(8,128)(2,1)S(1)}, f16[448,256]{1,0:T(8,128)(2,1)S(1)}, u32[]{:S(2)}, u32[]{:S(2)}) collective-permute-start(f16[448,256]{1,0:T(8,128)(2,1)S(1)} %fusion.15), channel_id=1, source_target_pairs={{0,16},{16,0},{1,17},{17,1},{2,18},{18,2},{3,19},{19,3},{4,20},{20... | collective-permute-start | bytes 688136 | tf_op jit(solution)/shard_map/ppermute | solution.py:144
  75.2 5.5 %collective-permute-done.7 = f16[448,384]{1,0:T(8,128)(2,1)S(1)} collective-permute-done((f16[448,384]{1,0:T(8,128)(2,1)S(1)}, f16[448,384]{1,0:T(8,128)(2,1)S(1)}, u32[]{:S(2)}, u32[]{:S(2)}) %collective-permute-start.7) | collective-permute-done | bytes 344096 | tf_op jit(solution)/shard_map/ppermute | solution.py:144
  80.7 0.3 fusion.8
  81.0 0.1 dynamic_update_slice.18
  81.0 0.1 dynamic_update_slice.21
  81.1 9.1 %collective-permute-done.12 = f16[448,256]{1,0:T(8,128)(2,1)S(1)} collective-permute-done((f16[448,256]{1,0:T(8,128)(2,1)S(1)}, f16[448,256]{1,0:T(8,128)(2,1)S(1)}, u32[]{:S(2)}, u32[]{:S(2)}) %collective-permute-start.12) | collective-permute-done | bytes 229408 | tf_op jit(solution)/shard_map/ppermute | solution.py:144
  90.3 0.2 fusion.42
  90.5 0.1 fusion.45
  90.6 0.2 fusion.43
  90.8 0.1 fusion.44
  91.0 0.7 copy-done.10
  91.7 0.5 copy-done.9
  (35 shorter events, 0.2 us)
Async XLA Ops:
  0.6 19.4 %copy-start.1 = (bf16[256,832]{0,1:T(8,128)(2,1)S(1)}, bf16[256,832]{0,1:T(8,128)(2,1)}, u32[]{:S(2)}) copy-start(bf16[256,832]{0,1:T(8,128)(2,1)} %param.8) | copy-start | bytes 1277956
  0.6 29.8 %copy-start.2 = (f32[832,448]{0,1:T(8,128)S(1)}, f32[832,448]{0,1:T(8,128)}, u32[]{:S(2)}) copy-start(f32[832,448]{0,1:T(8,128)} %param.13) | copy-start | bytes 4472836
  0.7 38.5 %collective-permute-start.1 = (bf16[448,4096]{1,0:T(8,128)(2,1)}, bf16[448,4096]{1,0:T(8,128)(2,1)}, u32[]{:S(2)}, u32[]{:S(2)}) collective-permute-start(bf16[448,4096]{1,0:T(8,128)(2,1)} %bitcast.13), channel_id=1, source_target_pairs={{0,1},{1,0},{2,3},{3,2},{4,5},{5,4},{6,7},{7,6},{8,9},{9,8},{10,11... | collective-permute-start | bytes 11010056 | tf_op jit(solution)/shard_map/ppermute | solution.py:149
  1.2 9.0 %collective-permute-start.2 = (bf16[832,256]{1,0:T(8,128)(2,1)}, bf16[832,256]{1,0:T(8,128)(2,1)S(1)}, u32[]{:S(2)}, u32[]{:S(2)}) collective-permute-start(bf16[832,256]{1,0:T(8,128)(2,1)} %bitcast.17), channel_id=1, source_target_pairs={{0,4},{1,3},{2,6},{3,1},{4,0},{5,9},{6,2},{7,11},{8,12},{9,5},{10,... | collective-permute-start | bytes 1277960 | tf_op jit(solution)/shard_map/ppermute | solution.py:148
  10.2 7.8 %collective-permute-start.3 = (bf16[384,512]{1,0:T(8,128)(2,1)S(1)}, bf16[384,512]{1,0:T(8,128)(2,1)S(1)}, u32[]{:S(2)}, u32[]{:S(2)}) collective-permute-start(bf16[384,512]{1,0:T(8,128)(2,1)S(1)} %pad_maximum_fusion), channel_id=1, source_target_pairs={{0,2},{1,5},{2,0},{3,7},{4,8},{5,1},{6,10},{7,3},{8,4},{9,13},{10,... | collective-permute-start | bytes 1179656 | tf_op jit(solution)/shard_map/ppermute | solution.py:159
  18.0 11.0 %collective-permute-start.4 = (bf16[384,512]{1,0:T(8,128)(2,1)S(1)}, bf16[384,512]{1,0:T(8,128)(2,1)S(1)}, u32[]{:S(2)}, u32[]{:S(2)}) collective-permute-start(bf16[384,512]{1,0:T(8,128)(2,1)S(1)} %collective-permute-done.3.refs_0_), channel_id=1, source_target_pairs={{0,4},{1,3},{2,6},{3,1},{4,0},{5,9},{6,2},{7,11},{8,12},{9,5},{10,... | collective-permute-start | bytes 1179656 | tf_op jit(solution)/shard_map/ppermute | solution.py:159
  20.1 16.3 %collective-permute-start.8 = (bf16[256,512]{1,0:T(8,128)(2,1)S(1)}, bf16[256,512]{1,0:T(8,128)(2,1)S(1)}, u32[]{:S(2)}, u32[]{:S(2)}) collective-permute-start(bf16[256,512]{1,0:T(8,128)(2,1)S(1)} %pad_maximum_fusion.1), channel_id=1, source_target_pairs={{0,2},{1,5},{2,0},{3,7},{4,8},{5,1},{6,10},{7,3},{8,4},{9,13},{10,... | collective-permute-start | bytes 786440 | tf_op jit(solution)/shard_map/ppermute | solution.py:159
  29.1 10.1 %collective-permute-start.5 = (bf16[384,512]{1,0:T(8,128)(2,1)S(1)}, bf16[384,512]{1,0:T(8,128)(2,1)S(1)}, u32[]{:S(2)}, u32[]{:S(2)}) collective-permute-start(bf16[384,512]{1,0:T(8,128)(2,1)S(1)} %collective-permute-done.4.refs_1_), channel_id=1, source_target_pairs={{0,2},{1,5},{2,0},{3,7},{4,8},{5,1},{6,10},{7,3},{8,4},{9,13},{10,... | collective-permute-start | bytes 1179656 | tf_op jit(solution)/shard_map/ppermute | solution.py:159
  34.1 26.2 %collective-permute-start = (f16[448,832]{1,0:T(8,128)(2,1)}, f16[448,832]{1,0:T(8,128)(2,1)S(1)}, u32[]{:S(2)}, u32[]{:S(2)}) collective-permute-start(f16[448,832]{1,0:T(8,128)(2,1)} %get-tuple-element.14), channel_id=1, source_target_pairs={{0,16},{16,0},{1,17},{17,1},{2,18},{18,2},{3,19},{19,3},{4,20},{20... | collective-permute-start | bytes 2236424 | tf_op jit(solution)/shard_map/ppermute | solution.py:144
  36.4 16.1 %collective-permute-start.9 = (bf16[256,512]{1,0:T(8,128)(2,1)S(1)}, bf16[256,512]{1,0:T(8,128)(2,1)S(1)}, u32[]{:S(2)}, u32[]{:S(2)}) collective-permute-start(bf16[256,512]{1,0:T(8,128)(2,1)S(1)} %collective-permute-done.8.refs_0_), channel_id=1, source_target_pairs={{0,4},{1,3},{2,6},{3,1},{4,0},{5,9},{6,2},{7,11},{8,12},{9,5},{10,... | collective-permute-start | bytes 786440 | tf_op jit(solution)/shard_map/ppermute | solution.py:159
  39.2 2.0 %copy-start = (bf16[4096,448]{0,1:T(8,128)(2,1)S(1)}, bf16[4096,448]{0,1:T(8,128)(2,1)}, u32[]{:S(2)}) copy-start(bf16[4096,448]{0,1:T(8,128)(2,1)} %param.9) | copy-start | bytes 11010052
  45.6 23.1 %collective-permute-start.6 = (f32[448,384]{1,0:T(8,128)S(1)}, f32[448,384]{1,0:T(8,128)S(1)}, u32[]{:S(2)}, u32[]{:S(2)}) collective-permute-start(f32[448,384]{1,0:T(8,128)S(1)} %get-tuple-element.9), channel_id=1, source_target_pairs={{0,1},{1,0},{2,3},{3,2},{4,5},{5,4},{6,7},{7,6},{8,9},{9,8},{10,11... | collective-permute-start | bytes 2064392 | tf_op jit(solution)/shard_map/ppermute | solution.py:162
  45.7 5.7 %collective-permute-start.13 = (bf16[192,512]{1,0:T(8,128)(2,1)S(1)}, bf16[192,512]{1,0:T(8,128)(2,1)S(1)}, u32[]{:S(2)}, u32[]{:S(2)}) collective-permute-start(bf16[192,512]{1,0:T(8,128)(2,1)S(1)} %pad_maximum_fusion.2), channel_id=1, source_target_pairs={{0,2},{1,5},{2,0},{3,7},{4,8},{5,1},{6,10},{7,3},{8,4},{9,13},{10,... | collective-permute-start | bytes 589832 | tf_op jit(solution)/shard_map/ppermute | solution.py:159
  51.4 7.7 %collective-permute-start.14 = (bf16[192,512]{1,0:T(8,128)(2,1)S(1)}, bf16[192,512]{1,0:T(8,128)(2,1)S(1)}, u32[]{:S(2)}, u32[]{:S(2)}) collective-permute-start(bf16[192,512]{1,0:T(8,128)(2,1)S(1)} %collective-permute-done.13.refs_0_), channel_id=1, source_target_pairs={{0,4},{1,3},{2,6},{3,1},{4,0},{5,9},{6,2},{7,11},{8,12},{9,5},{10,... | collective-permute-start | bytes 589832 | tf_op jit(solution)/shard_map/ppermute | solution.py:159
  52.5 8.0 %collective-permute-start.10 = (bf16[256,512]{1,0:T(8,128)(2,1)S(1)}, bf16[256,512]{1,0:T(8,128)(2,1)S(1)}, u32[]{:S(2)}, u32[]{:S(2)}) collective-permute-start(bf16[256,512]{1,0:T(8,128)(2,1)S(1)} %collective-permute-done.9.refs_1_), channel_id=1, source_target_pairs={{0,2},{1,5},{2,0},{3,7},{4,8},{5,1},{6,10},{7,3},{8,4},{9,13},{10,... | collective-permute-start | bytes 786440 | tf_op jit(solution)/shard_map/ppermute | solution.py:159
  59.1 5.7 %collective-permute-start.15 = (bf16[192,512]{1,0:T(8,128)(2,1)S(1)}, bf16[192,512]{1,0:T(8,128)(2,1)S(1)}, u32[]{:S(2)}, u32[]{:S(2)}) collective-permute-start(bf16[192,512]{1,0:T(8,128)(2,1)S(1)} %collective-permute-done.14.refs_1_), channel_id=1, source_target_pairs={{0,2},{1,5},{2,0},{3,7},{4,8},{5,1},{6,10},{7,3},{8,4},{9,13},{10,... | collective-permute-start | bytes 589832 | tf_op jit(solution)/shard_map/ppermute | solution.py:159
  63.8 4.8 %copy-start.3 = (f32[832,448]{0,1:T(8,128)S(1)}, f32[832,448]{0,1:T(8,128)}, u32[]{:S(2)}) copy-start(f32[832,448]{0,1:T(8,128)} %param.13) | copy-start | bytes 4472836
  63.9 4.8 %copy-start.5 = (f32[832,448]{0,1:T(8,128)S(1)}, f32[832,448]{0,1:T(8,128)}, u32[]{:S(2)}) copy-start(f32[832,448]{0,1:T(8,128)} %param.10) | copy-start | bytes 4472836
  63.9 4.8 %copy-start.7 = (f32[832,448]{0,1:T(8,128)S(1)}, f32[832,448]{0,1:T(8,128)}, u32[]{:S(2)}) copy-start(f32[832,448]{0,1:T(8,128)} %param.12) | copy-start | bytes 4472836
  63.9 4.8 %copy-start.8 = (f32[832,448]{0,1:T(8,128)S(1)}, f32[832,448]{0,1:T(8,128)}, u32[]{:S(2)}) copy-start(f32[832,448]{0,1:T(8,128)} %param.11) | copy-start | bytes 4472836
  63.9 9.3 %collective-permute-start.11 = (f32[448,256]{1,0:T(8,128)S(1)}, f32[448,256]{1,0:T(8,128)S(1)}, u32[]{:S(2)}, u32[]{:S(2)}) collective-permute-start(f32[448,256]{1,0:T(8,128)S(1)} %get-tuple-element.11), channel_id=1, source_target_pairs={{0,1},{1,0},{2,3},{3,2},{4,5},{5,4},{6,7},{7,6},{8,9},{9,8},{10,11... | collective-permute-start | bytes 1376264 | tf_op jit(solution)/shard_map/ppermute | solution.py:162
  68.6 3.2 %collective-permute-start.16 = (f32[448,192]{1,0:T(8,128)S(1)}, f32[448,192]{1,0:T(8,128)S(1)}, u32[]{:S(2)}, u32[]{:S(2)}) collective-permute-start(f32[448,192]{1,0:T(8,128)S(1)} %get-tuple-element.13), channel_id=1, source_target_pairs={{0,1},{1,0},{2,3},{3,2},{4,5},{5,4},{6,7},{7,6},{8,9},{9,8},{10,11... | collective-permute-start | bytes 1032200 | tf_op jit(solution)/shard_map/ppermute | solution.py:162
  69.6 11.0 %collective-permute-start.7 = (f16[448,384]{1,0:T(8,128)(2,1)S(1)}, f16[448,384]{1,0:T(8,128)(2,1)S(1)}, u32[]{:S(2)}, u32[]{:S(2)}) collective-permute-start(f16[448,384]{1,0:T(8,128)(2,1)S(1)} %fusion.1), channel_id=1, source_target_pairs={{0,16},{16,0},{1,17},{17,1},{2,18},{18,2},{3,19},{19,3},{4,20},{20... | collective-permute-start | bytes 1032200 | tf_op jit(solution)/shard_map/ppermute | solution.py:144
  71.7 8.9 %copy-start.6 = (f32[832,448]{0,1:T(8,128)S(1)}, f32[832,448]{0,1:T(8,128)}, u32[]{:S(2)}) copy-start(f32[832,448]{0,1:T(8,128)} %param.14) | copy-start | bytes 4472836
  72.4 8.3 %copy-start.4 = (f32[448,832]{1,0:T(8,128)S(1)}, f32[448,832]{1,0:T(8,128)}, u32[]{:S(2)}) copy-start(f32[448,832]{1,0:T(8,128)} %get-tuple-element.15) | copy-start | bytes 4472836
  72.4 18.2 %collective-permute-start.17 = (f16[448,192]{1,0:T(8,128)(2,1)S(1)}, f16[448,192]{1,0:T(8,128)(2,1)S(1)}, u32[]{:S(2)}, u32[]{:S(2)}) collective-permute-start(f16[448,192]{1,0:T(8,128)(2,1)S(1)} %fusion.23), channel_id=1, source_target_pairs={{0,16},{16,0},{1,17},{17,1},{2,18},{18,2},{3,19},{19,3},{4,20},{20... | collective-permute-start | bytes 516104 | tf_op jit(solution)/shard_map/ppermute | solution.py:144
  73.8 16.4 %collective-permute-start.12 = (f16[448,256]{1,0:T(8,128)(2,1)S(1)}, f16[448,256]{1,0:T(8,128)(2,1)S(1)}, u32[]{:S(2)}, u32[]{:S(2)}) collective-permute-start(f16[448,256]{1,0:T(8,128)(2,1)S(1)} %fusion.15), channel_id=1, source_target_pairs={{0,16},{16,0},{1,17},{17,1},{2,18},{18,2},{3,19},{19,3},{4,20},{20... | collective-permute-start | bytes 688136 | tf_op jit(solution)/shard_map/ppermute | solution.py:144
  90.8 0.9 copy-start.10
  91.0 1.3 %copy-start.9 = (f32[448,832]{1,0:T(8,128)}, f32[448,832]{1,0:T(8,128)S(1)}, u32[]{:S(2)}) copy-start(f32[448,832]{1,0:T(8,128)S(1)} %fusion.44) | copy-start | bytes 4472836

commit v2 on v0

v2 whole, which is shorter than its diff:
```python
import functools

import jax
import jax.numpy as jnp
from jax import lax
from jax.experimental import pallas as pl
from jax.experimental.pallas import tpu as pltpu
from jax.sharding import PartitionSpec as P

BETA_ONE = 0.9
BETA_TWO = 0.95
BIAS_ONE = 0.9999734386
BIAS_TWO = 0.9940794708
EPSILON = 1e-08
INNER_RATE = 0.25
DECAY_RATE = 0.1
OUTER_RATE = 0.7
NESTEROV = 0.9
CORES = 2
LANES = 128


def chip_ring(chips):
    return list(range(0, chips, 2)) + list(range(chips - 1, 0, -2))


def arrivals(chips):
    return [[0]] + [[-hop, hop] for hop in range(1, chips // 2)] + [[chips // 2]]


def ring_step(size, hop):
    ring = chip_ring(size // CORES)
    return [
        (chip * CORES + core, ring[(at + hop) % len(ring)] * CORES + core)
        for at, chip in enumerate(ring)
        for core in range(CORES)
    ]


def feature_cuts(features):
    tiles = features // LANES
    return [0, tiles // 3 * LANES, 2 * (tiles // 3) * LANES, features]

def in_vmem(limit):
    return pltpu.CompilerParams(vmem_limit_bytes=limit)


def sort_kernel(chips, grad_ref, sorted_ref, sems):
    index = lax.axis_index("tensor")
    at, core = index // CORES, index % CORES
    tokens = sorted_ref.shape[1] // (CORES * chips)
    ring = chip_ring(chips)
    place = sum(jnp.where(at == chip, spot, 0) for spot, chip in enumerate(ring))
    copies = []
    for hops in arrivals(chips):
        for side in range(CORES):
            for hop in hops:
                there = lax.rem(place + hop + chips, chips)
                chip = sum(jnp.where(there == s, c, 0) for s, c in enumerate(ring))
                block = chip * CORES + (core if side == 0 else 1 - core)
                copy = pltpu.make_async_copy(
                    grad_ref.at[:, pl.ds(pl.multiple_of(block * tokens, LANES), tokens)],
                    sorted_ref.at[:, pl.ds(len(copies) * tokens, tokens)],
                    sems.at[len(copies)],
                )
                copy.start()
                copies.append(copy)
    for copy in copies:
        copy.wait()


def sort_tokens(grad, chips):
    return pl.pallas_call(
        functools.partial(sort_kernel, chips),
        out_shape=pltpu.VMEM(grad.shape, grad.dtype),
        in_specs=[pl.BlockSpec(memory_space=pl.ANY)],
        out_specs=pl.BlockSpec(memory_space=pltpu.VMEM),
        scratch_shapes=[pltpu.SemaphoreType.DMA((CORES * chips,))],
        compiler_params=in_vmem(2**20),
        cost_estimate=pl.CostEstimate(flops=0, bytes_accessed=4 * grad.size, transcendentals=0),
        name="sort_tokens",
    )(grad)


def place_kernel(low, *refs):
    parts, outs, sems = refs[:2], refs[-3:-1], refs[-1]
    copies = [
        pltpu.make_async_copy(part, out.at[:, pl.ds(low, part.shape[1])], sems.at[at])
        for at, (part, out) in enumerate(zip(parts, outs))
    ]
    for copy in copies:
        copy.start()
    for copy in copies:
        copy.wait()


def place(low, width, parts, outs):
    return pl.pallas_call(
        functools.partial(place_kernel, low),
        out_shape=tuple(jax.ShapeDtypeStruct((p.shape[0], width), p.dtype) for p in parts),
        in_specs=[pl.BlockSpec(memory_space=pl.ANY)] * (2 + len(outs)),
        out_specs=(pl.BlockSpec(memory_space=pl.ANY),) * 2,
        scratch_shapes=[pltpu.SemaphoreType.DMA((2,))],
        input_output_aliases={2 + at: at for at in range(len(outs))},
        compiler_params=in_vmem(2**20),
        cost_estimate=pl.CostEstimate(
            flops=0, bytes_accessed=12 * parts[0].size, transcendentals=0
        ),
        name="place",
    )(*parts, *outs)


def gradient_kernel(low, skip, tops, grad_ref, *refs):
    count = len(tops)
    blocks, so_far, (out_ref, acts, sems) = refs[:count], refs[count:-3], refs[-3:]
    tokens, high = blocks[0].shape[1], low + out_ref.shape[1]
    at, copies = 0, []
    for block, (top, ends) in zip(blocks, tops):
        first, after = max(low, top), min(high, top + block.shape[0])
        if first < after:
            copy = pltpu.make_async_copy(
                block.at[pl.ds(first - top, after - first)],
                acts.at[pl.ds(first - low, after - first), pl.ds(at * tokens, tokens)],
                sems.at[len(copies)],
            )
            copy.start()
            copies.append(copy)
        at += ends
    for copy in copies:
        copy.wait()
    product = lax.dot_general(
        grad_ref[:, skip * tokens : (skip + at) * tokens],
        acts[...],
        (((1,), (1,)), ((), ())),
        preferred_element_type=jnp.float32,
    )
    for ref in so_far:
        product = ref[:, low:high] + product
    out_ref[...] = product


def gradient_part(low, high, skip, grad, blocks, so_far=()):
    rows, tokens = grad.shape[0], blocks[0][0].shape[1]
    arrays = [b[0] for b in blocks]
    depth = tokens * sum(b[2] for b in blocks)
    return pl.pallas_call(
        functools.partial(gradient_kernel, low, skip, [b[1:] for b in blocks]),
        out_shape=jax.ShapeDtypeStruct((rows, high - low), jnp.float32),
        in_specs=[pl.BlockSpec(memory_space=pltpu.VMEM)]
        + [pl.BlockSpec(memory_space=pl.ANY)] * len(arrays)
        + [pl.BlockSpec(memory_space=pltpu.VMEM)] * len(so_far),
        out_specs=pl.BlockSpec(memory_space=pltpu.VMEM),
        scratch_shapes=[
            pltpu.VMEM((high - low, depth), arrays[0].dtype),
            pltpu.SemaphoreType.DMA((len(arrays),)),
        ],
        compiler_params=in_vmem(16 * 2**20),
        cost_estimate=pl.CostEstimate(
            flops=2 * rows * (high - low) * depth, bytes_accessed=8 * rows * (high - low), transcendentals=0
        ),
        name="gradient",
    )(grad, *arrays, *so_far)


def start_to_half(anchor, weights):
    exact = anchor - (1.0 - INNER_RATE * DECAY_RATE) * weights
    return exact, lax.reduce_precision(exact, 5, 10)


def late_part(gradient, first_moment, second_moment, weights, anchor):
    moment_one = BETA_ONE * first_moment + (1.0 - BETA_ONE) * gradient
    moment_two = BETA_TWO * second_moment + (1.0 - BETA_TWO) * gradient * gradient
    step = moment_one / BIAS_ONE / (jnp.sqrt(moment_two / BIAS_TWO) + EPSILON)
    exact, half = start_to_half(anchor, weights)
    return ((exact - half) + INNER_RATE * step).astype(jnp.float16)


def on_device(
    activations, out_grad, master_weights, first_moment, second_moment, anchor, outer_momentum
):
    size = lax.axis_size("tensor")
    groups = lax.axis_size("replica")
    chips = size // CORES
    half = chips // 2
    pairs = {hop: ring_step(size, hop) for hop in (1, -1)}
    swap = [(d, d ^ 1) for d in range(size)]
    own, mine = activations.T, out_grad.T
    weights, one, two = master_weights.T, first_moment.T, second_moment.T
    anchor, momentum = anchor.T, outer_momentum.T
    cuts = feature_cuts(own.shape[0])
    spans = list(zip(cuts[:-1], cuts[1:]))

    def other_groups_sum(value):
        total = None
        for hop in range(1, groups):
            there = [(g, (g + hop) % groups) for g in range(groups)]
            came = lax.ppermute(value, "replica", there).astype(jnp.float32)
            total = came if total is None else total + came
        return total

    def behind(value, *boxes):
        if not boxes:
            return value
        value, *contents = lax.optimization_barrier((value, *[b[0] for b in boxes]))
        for box, content in zip(boxes, contents):
            box[0] = content
        return value

    def send(blocks, *boxes):
        blocks = [behind(b, *boxes) for b in blocks] if boxes else blocks
        return [lax.ppermute(b, "tensor", pairs[hop]) for b, hop in zip(blocks, (1, -1))]

    def to_other_core(blocks, *boxes):
        return [lax.ppermute(behind(b, *boxes) if boxes else b, "tensor", swap) for b in blocks]

    def with_other(mine, theirs):
        return [(b, 0, 1) for b in mine + theirs]


    features = own.shape[0]
    first = send([own, own])
    early = start_to_half(anchor, weights)[1]
    early16 = [early.astype(jnp.float16)]
    early_others = [other_groups_sum(early16[0])]
    grad = sort_tokens(behind(mine, [first[0]]), chips)
    came = [with_other([own], to_other_core([own])), with_other(first, to_other_core(first))]
    newest = first
    for step in range(2, half - 1):
        newest = send(newest)
        came.append(with_other(newest, to_other_core(newest)))
    head = sum(came[:2], [])
    newest = send(newest, early_others)
    sums = [gradient_part(0, features, 0, grad, head)]
    middle = sum(came[2:], [])
    sums2 = [gradient_part(0, features, len(head), grad, middle, (sums[0],))]
    skip = len(head) + len(middle)
    top = cuts[1]
    final = send([newest[0][:top], newest[1][top:]], sums)
    third = [[b] for b in newest]
    theirs = to_other_core(newest)
    theirs_final = to_other_core(final, sums2)
    tail = with_other(newest, theirs) + [(final[0], 0, 0), (final[1], top, 1), (theirs_final[0], 0, 0), (theirs_final[1], top, 1)]
    so_far = (sums2[0],)
    outs = ()
    rest = []
    for low, high in spans:
        tied = [behind(b[0], *rest) for b in tail]
        tail = [(t, *b[1:]) for t, b in zip(tied, tail)]
        gradient = gradient_part(low, high, skip, grad, tail, so_far)
        here = lambda x: x[:, low:high]
        late = late_part(gradient, *map(here, (one, two, weights, anchor)))
        late_others = other_groups_sum(late)
        rest = [[late]] if True else []
        mean = ((here(early) + here(early_others[0])) + (late.astype(jnp.float32) + late_others)) / groups
        moved = NESTEROV * here(momentum) + mean
        weight = here(anchor) - OUTER_RATE * (mean + NESTEROV * moved)
        outs = place(low, cuts[-1], (weight.astype(jnp.bfloat16), moved), outs)
    rebuilt, new_momentum = outs
    return rebuilt.T, new_momentum.T


def solution(mesh):
    placed = (
        P(("replica", "tensor"), None),
        P("replica", "tensor"),
        P("replica", "tensor"),
        P("replica", "tensor"),
        P("replica", "tensor"),
        P(None, "tensor"),
        P(None, "tensor"),
    )
    return jax.shard_map(
        on_device,
        mesh=mesh,
        in_specs=placed,
        out_specs=(P(None, "tensor"), P(None, "tensor")),
        check_vma=False,
    )
```

time: 155 us -> 71.1 us (0.46)
  waiting for transfers between devices: 125 us -> 38.3 us
  starting transfers between devices: 0.08 us -> 16.5 us
  between operations: 14 us -> 0.87 us
  matrix products: 12.1 us -> 0 us
  Pallas kernels: 0 us -> 9.4 us
  other arithmetic: 3.25 us -> 5.87 us
    all_gather x1 -> x0, waiting for transfers between devices: 73.7 us -> none  [on_device(): gathered = lax.all_gather(activations, 'tensor', axis=0, tiled=True)]
    psum x1 -> x0, waiting for transfers between devices: 50.5 us -> none  [on_device(): summed = lax.psum(pseudo, 'replica')]
    ppermute x0 -> x21, waiting for transfers between devices: none -> 38.3 us  [the longest x4 21.2 us: other_groups_sum(): came = lax.ppermute(value, 'replica', there).astype(jnp.float32)]
    ppermute x0 -> x21, starting transfers between devices: none -> 16.5 us  [the longest x8 9.17 us: send(): lax.ppermute(b, 'tensor', pairs[hop])]
    dot_general x1 -> x0, matrix products: 12.1 us -> none  [on_device(): lax.dot_general(gathered, out_grad, numbers, preferred_element_type=jnp.f...]
    pallas_call x0 -> x9, Pallas kernels: none -> 9.4 us  [the longest x5 5.77 us: gradient_part(): pl.pallas_call(functools.partial(gradient_kernel, low, skip, [b[1:] for b...]
    convert_element_type x1 -> x6, other arithmetic: 3.25 us -> 5.58 us  [the longest x1 2.97 us: on_device(): early16 = [early.astype(jnp.float16)]]
  transfers between devices with their start and end apart: 2 -> 21, of which waited for: 2 -> 8; matrix products, arithmetic and copies ran while one was open for 0% -> 7% of each run, Pallas kernels for 0% -> 11%
where the time goes in v2:
time: 71.1 us; the launch traced here: 70.9 us
  waiting for transfers between devices  38.3 us (54%)
  starting transfers between devices  16.5 us (23%)
  Pallas kernels  9.4 us (13%)
  other arithmetic  5.87 us (8%)
  between operations  0.87 us (1%)
    ppermute x4, waiting for transfers between devices, other_groups_sum(): came = lax.ppermute(value, 'replica', there).astype(jnp.float32)  21.2 us
    ppermute x8, waiting for transfers between devices, send(): lax.ppermute(b, 'tensor', pairs[hop])  15.7 us
    ppermute x8, starting transfers between devices, send(): lax.ppermute(b, 'tensor', pairs[hop])  9.17 us
    pallas_call x5, Pallas kernels, gradient_part(): pl.pallas_call(functools.partial(gradient_kernel, low, skip, [b[1:] for b...  5.77 us
    ppermute x4, starting transfers between devices, other_groups_sum(): came = lax.ppermute(value, 'replica', there).astype(jnp.float32)  5.77 us
    convert_element_type x1, other arithmetic, on_device(): early16 = [early.astype(jnp.float16)]  2.97 us
    pallas_call x3, Pallas kernels, place(): pl.pallas_call(functools.partial(place_kernel, low), out_shape=tuple((jax...  2.71 us
    convert_element_type x3, other arithmetic, late_part(): return (exact - half + INNER_RATE * step).astype(jnp.float16)  2.12 us
  transfers between devices with their start and end apart: 21, of which 8 were waited for; matrix products, arithmetic and copies ran while one was open for 7% of the time, Pallas kernels for 11%

profile of v2, /device:TPU:0, one launch (start us, length us, event | category | flops | bytes accessed | tf_op | source)
XLA Modules:
  0.0 70.9 jit_solution(549301056628781997)
XLA Ops:
  0.6 3.1 %collective-permute-start.2 = (bf16[832,256]{1,0:T(8,128)(2,1)}, bf16[832,256]{1,0:T(8,128)(2,1)S(1)}, u32[]{:S(2)}, u32[]{:S(2)}) collective-permute-start(bf16[832,256]{1,0:T(8,128)(2,1)} %bitcast.14), channel_id=1, source_target_pairs={{0,4},{1,5},{4,8},{5,9},{8,12},{9,13},{12,14},{13,15},{14,10},{15,... | collective-permute-start | bytes 1277960 | tf_op jit(solution)/shard_map/ppermute | solution.py:211
  3.7 3.0 %fusion.42 = (f16[448,832]{1,0:T(8,128)(2,1)S(1)}, f32[448,832]{1,0:T(8,128)S(1)}) fusion(f32[832,448]{0,1:T(8,128)} %param.9, f32[832,448]{0,1:T(8,128)} %param.12), kind=kLoop, calls=%fused_computation.67 | loop fusion | flops 1490944 | bytes 5218304 | tf_op jit(solution)/shard_map/convert_element_type | solution.py:223
  6.7 2.0 %collective-permute-start.4 = (f16[448,832]{1,0:T(8,128)(2,1)S(1)}, f16[448,832]{1,0:T(8,128)(2,1)S(1)}, u32[]{:S(2)}, u32[]{:S(2)}) collective-permute-start(f16[448,832]{1,0:T(8,128)(2,1)S(1)} %get-tuple-element.38), channel_id=1, source_target_pairs={{0,16},{16,0},{1,17},{17,1},{2,18},{18,2},{3,19},{19,3},{4,20},{20... | collective-permute-start | bytes 2236424 | tf_op jit(solution)/shard_map/ppermute | solution.py:197
  8.7 4.9 %collective-permute-done.2.refs_2_ = bf16[832,256]{1,0:T(8,128)(2,1)S(1)} collective-permute-done((bf16[832,256]{1,0:T(8,128)(2,1)}, bf16[832,256]{1,0:T(8,128)(2,1)S(1)}, u32[]{:S(2)}, u32[]{:S(2)}) %collective-permute-start.2) | collective-permute-done | bytes 426016 | tf_op jit(solution)/shard_map/ppermute | solution.py:211
  13.7 1.8 %collective-permute-start.3 = (bf16[832,256]{1,0:T(8,128)(2,1)S(1)}, bf16[832,256]{1,0:T(8,128)(2,1)S(1)}, u32[]{:S(2)}, u32[]{:S(2)}) collective-permute-start(bf16[832,256]{1,0:T(8,128)(2,1)S(1)} %collective-permute-done.2.refs_2_), channel_id=1, source_target_pairs={{0,4},{1,5},{4,8},{5,9},{8,12},{9,13},{12,14},{13,15},{14,10},{15,... | collective-permute-start | bytes 1277960 | tf_op jit(solution)/shard_map/ppermute | solution.py:211
  15.5 0.0 collective-permute-done.refs_3_
  15.5 0.2 collective-permute-start.1
  15.7 0.0 collective-permute-start.9
  15.7 10.4 %collective-permute-done.4 = f16[448,832]{1,0:T(8,128)(2,1)S(1)} collective-permute-done((f16[448,832]{1,0:T(8,128)(2,1)S(1)}, f16[448,832]{1,0:T(8,128)(2,1)S(1)}, u32[]{:S(2)}, u32[]{:S(2)}) %collective-permute-start.4) | collective-permute-done | bytes 745504 | tf_op jit(solution)/shard_map/ppermute | solution.py:197
  26.1 0.1 convert_element_type.43
  26.2 0.0 collective-permute-done.3.refs_0_
  26.2 0.0 collective-permute-done.1.refs_1_
  26.2 1.7 %collective-permute-start.6 = (bf16[832,256]{1,0:T(8,128)(2,1)S(1)}, bf16[832,256]{1,0:T(8,128)(2,1)S(1)}, u32[]{:S(2)}, u32[]{:S(2)}) collective-permute-start(bf16[832,256]{1,0:T(8,128)(2,1)S(1)} %collective-permute-done.1.refs_1_), channel_id=1, source_target_pairs={{0,2},{1,3},{4,0},{5,1},{8,4},{9,5},{12,8},{13,9},{14,12},{15,13},... | collective-permute-start | bytes 1277960 | tf_op jit(solution)/shard_map/ppermute | solution.py:211
  27.9 0.5 collective-permute-start.11
  28.5 0.4 collective-permute-start.5
  28.8 7.8 %collective-permute-done.6.refs_1_ = bf16[832,256]{1,0:T(8,128)(2,1)S(1)} collective-permute-done((bf16[832,256]{1,0:T(8,128)(2,1)S(1)}, bf16[832,256]{1,0:T(8,128)(2,1)S(1)}, u32[]{:S(2)}, u32[]{:S(2)}) %collective-permute-start.6) | collective-permute-done | bytes 426016 | tf_op jit(solution)/shard_map/ppermute | solution.py:211
  36.7 0.0 collective-permute-done.10.refs_4_
  36.7 1.4 %collective-permute-start.13 = (bf16[576,256]{1,0:T(8,128)(2,1)S(1)}, bf16[576,256]{1,0:T(8,128)(2,1)S(1)}, u32[]{:S(2)}, u32[]{:S(2)}) collective-permute-start(bf16[576,256]{1,0:T(8,128)(2,1)S(1)} %slice.103), channel_id=1, source_target_pairs={{0,2},{1,3},{4,0},{5,1},{8,4},{9,5},{12,8},{13,9},{14,12},{15,13},... | collective-permute-start | bytes 884744 | tf_op jit(solution)/shard_map/ppermute | solution.py:211
  38.1 0.9 %sort_tokens.1.grad_ref = bf16[448,4096]{1,0:T(8,128)(2,1)S(1)} custom-call(bf16[448,4096]{1,0:T(8,128)(2,1)S(1)} %bitcast.13), custom_call_target="tpu_custom_call" | custom-call | bytes 7340032 | tf_op jit(solution)/shard_map/sort_tokens/pallas_call | solution.py:73
  39.0 1.9 %gradient.5.refs_4_ = f32[448,832]{1,0:T(8,128)S(1)} custom-call(bf16[448,4096]{1,0:T(8,128)(2,1)S(1)} %sort_tokens.1.grad_ref, bf16[832,256]{1,0:T(8,128)(2,1)S(1)} %bitcast.17, bf16[832,256]{1,0:T(8,128)(2,1)S(1)} %collective-permute-done.9.refs_1_, bf16[832,256]{1,0:T(8,128)(2,1)S(1)} %collective-permute-done.2.refs_2_, ...), custom_call_target="tpu_custom_call" | custom-call | flops 1145044992 | bytes 2981888 | tf_op jit(solution)/shard_map/gradient/pallas_call | solution.py:146
  41.0 0.6 collective-permute-start.12
  41.5 0.5 collective-permute-start.8
  42.1 1.4 %gradient.6.refs_8_ = f32[448,832]{1,0:T(8,128)S(1)} custom-call(bf16[448,4096]{1,0:T(8,128)(2,1)S(1)} %sort_tokens.1.grad_ref, bf16[832,256]{1,0:T(8,128)(2,1)S(1)} %collective-permute-done.3.refs_0_, bf16[832,256]{1,0:T(8,128)(2,1)S(1)} %collective-permute-done.1.refs_1_, bf16[832,256]{1,0:T(8,128)(2,1)S(1)} %collective-permute-done.14.refs_2_, ...), custom_call_target="tpu_custom_call" | custom-call | flops 763363328 | bytes 2981888 | tf_op jit(solution)/shard_map/gradient/pallas_call | solution.py:146
  43.5 0.0 copy-start.2
  43.5 0.0 copy-start.3
  43.5 0.0 copy-start.4
  43.5 0.0 copy-start.5
  43.5 3.0 %collective-permute-done.12.refs_4_ = bf16[256,256]{1,0:T(8,128)(2,1)S(1)} collective-permute-done((bf16[256,256]{1,0:T(8,128)(2,1)S(1)}, bf16[256,256]{1,0:T(8,128)(2,1)S(1)}, u32[]{:S(2)}, u32[]{:S(2)}) %collective-permute-start.12) | collective-permute-done | bytes 131104 | tf_op jit(solution)/shard_map/ppermute | solution.py:211
  46.5 0.5 collective-permute-start.16
  47.0 1.3 %collective-permute-done.16.refs_6_ = bf16[256,256]{1,0:T(8,128)(2,1)S(1)} collective-permute-done((bf16[256,256]{1,0:T(8,128)(2,1)S(1)}, bf16[256,256]{1,0:T(8,128)(2,1)S(1)}, u32[]{:S(2)}, u32[]{:S(2)}) %collective-permute-start.16) | collective-permute-done | bytes 131104 | tf_op jit(solution)/shard_map/ppermute | solution.py:214
  48.3 0.7 gradient.7
  49.0 0.6 fusion.15
  49.7 1.6 %collective-permute-start.20 = (f16[448,256]{1,0:T(8,128)(2,1)S(1)}, f16[448,256]{1,0:T(8,128)(2,1)S(1)}, u32[]{:S(2)}, u32[]{:S(2)}) collective-permute-start(f16[448,256]{1,0:T(8,128)(2,1)S(1)} %fusion.15), channel_id=1, source_target_pairs={{0,16},{16,0},{1,17},{17,1},{2,18},{18,2},{3,19},{19,3},{4,20},{20... | collective-permute-start | bytes 688136 | tf_op jit(solution)/shard_map/ppermute | solution.py:197
  51.2 0.7 gradient.8
  51.9 0.6 fusion.23
  52.5 0.6 collective-permute-start.19
  53.1 1.1 %gradient.9 = f32[448,320]{1,0:T(8,128)S(1)} custom-call(bf16[448,4096]{1,0:T(8,128)(2,1)S(1)} %sort_tokens.1.grad_ref, bf16[832,256]{1,0:T(8,128)(2,1)S(1)} %collective-permute-done.5.refs_0_, bf16[832,256]{1,0:T(8,128)(2,1)S(1)} %collective-permute-done.6.refs_1_, bf16[832,256]{1,0:T(8,128)(2,1)S(1)} %collective-permute-done.7.refs_2_, ...), custom_call_target="tpu_custom_call" | custom-call | flops 440401920 | bytes 1146880 | tf_op jit(solution)/shard_map/gradient/pallas_call | solution.py:146
  54.2 0.0 copy-start.6
  54.2 0.9 %fusion.1 = f16[448,320]{1,0:T(8,128)(2,1)S(1)} fusion(f32[448,320]{1,0:T(8,128)S(1)} %gradient.9, f32[448,832]{1,0:T(8,128)S(1)} %bitcast.30, f32[448,832]{1,0:T(8,128)S(1)} %bitcast.33, f32[448,832]{1,0:T(8,128)S(1)} %bitcast.25, f32[448,832]{1,0:T(8,128)S(1)} %bitcast.20), kind=kLoop, calls=%fused_computation.4 | loop fusion | flops 2580480 | bytes 3153920 | tf_op jit(solution)/shard_map/convert_element_type | solution.py:175
  55.1 1.6 %collective-permute-start.18 = (f16[448,320]{1,0:T(8,128)(2,1)S(1)}, f16[448,320]{1,0:T(8,128)(2,1)S(1)}, u32[]{:S(2)}, u32[]{:S(2)}) collective-permute-start(f16[448,320]{1,0:T(8,128)(2,1)S(1)} %fusion.1), channel_id=1, source_target_pairs={{0,16},{16,0},{1,17},{17,1},{2,18},{18,2},{3,19},{19,3},{4,20},{20... | collective-permute-start | bytes 860168 | tf_op jit(solution)/shard_map/ppermute | solution.py:197
  56.7 1.5 %collective-permute-done.20 = f16[448,256]{1,0:T(8,128)(2,1)S(1)} collective-permute-done((f16[448,256]{1,0:T(8,128)(2,1)S(1)}, f16[448,256]{1,0:T(8,128)(2,1)S(1)}, u32[]{:S(2)}, u32[]{:S(2)}) %collective-permute-start.20) | collective-permute-done | bytes 229408 | tf_op jit(solution)/shard_map/ppermute | solution.py:197
  58.2 4.9 %collective-permute-done.19 = f16[448,256]{1,0:T(8,128)(2,1)S(1)} collective-permute-done((f16[448,256]{1,0:T(8,128)(2,1)S(1)}, f16[448,256]{1,0:T(8,128)(2,1)S(1)}, u32[]{:S(2)}, u32[]{:S(2)}) %collective-permute-start.19) | collective-permute-done | bytes 229408 | tf_op jit(solution)/shard_map/ppermute | solution.py:197
  63.1 0.4 subtract_convert_fusion.1
  63.5 0.9 %place.3 = (bf16[448,832]{1,0:T(8,128)(2,1)}, f32[448,832]{1,0:T(8,128)}) custom-call(bf16[448,256]{1,0:T(8,128)(2,1)S(1)} %get-tuple-element.40.refs_0_, f32[448,256]{1,0:T(8,128)S(1)} %get-tuple-element.45.refs_1_), custom_call_target="tpu_custom_call" | custom-call | bytes 1376256 | tf_op jit(solution)/shard_map/place/pallas_call | solution.py:98
  64.3 0.9 %place.4 = (bf16[448,832]{1,0:T(8,128)(2,1)}, f32[448,832]{1,0:T(8,128)}) custom-call(bf16[448,256]{1,0:T(8,128)(2,1)S(1)} %get-tuple-element.41.refs_0_, f32[448,256]{1,0:T(8,128)S(1)} %get-tuple-element.44.refs_1_, bf16[448,832]{1,0:T(8,128)(2,1)} %get-tuple-element.32.refs_2_, ...), custom_call_target="tpu_custom_call", output_to_operand_aliasing={{0}: (2, {}), {1}: (3, {})} | custom-call | bytes 1376256 | tf_op jit(solution)/shard_map/place/pallas_call | solution.py:98
  65.2 4.4 %collective-permute-done.18 = f16[448,320]{1,0:T(8,128)(2,1)S(1)} collective-permute-done((f16[448,320]{1,0:T(8,128)(2,1)S(1)}, f16[448,320]{1,0:T(8,128)(2,1)S(1)}, u32[]{:S(2)}, u32[]{:S(2)}) %collective-permute-start.18) | collective-permute-done | bytes 286752 | tf_op jit(solution)/shard_map/ppermute | solution.py:197
  69.7 0.3 fusion.8
  70.0 1.0 %place.5 = (bf16[448,832]{1,0:T(8,128)(2,1)}, f32[448,832]{1,0:T(8,128)}) custom-call(bf16[448,320]{1,0:T(8,128)(2,1)S(1)} %get-tuple-element.43.refs_0_, f32[448,320]{1,0:T(8,128)S(1)} %get-tuple-element.42.refs_1_, bf16[448,832]{1,0:T(8,128)(2,1)} %get-tuple-element.34.refs_2_, ...), custom_call_target="tpu_custom_call", output_to_operand_aliasing={{0}: (2, {}), {1}: (3, {})} | custom-call | bytes 1720320 | tf_op jit(solution)/shard_map/place/pallas_call | solution.py:98
  (26 shorter events, 0.1 us)
Async XLA Ops:
  0.6 15.1 %copy-start.1 = (bf16[256,832]{0,1:T(8,128)(2,1)S(1)}, bf16[256,832]{0,1:T(8,128)(2,1)}, u32[]{:S(2)}) copy-start(bf16[256,832]{0,1:T(8,128)(2,1)} %param.7) | copy-start | bytes 1277956
  0.6 13.0 %collective-permute-start.2 = (bf16[832,256]{1,0:T(8,128)(2,1)}, bf16[832,256]{1,0:T(8,128)(2,1)S(1)}, u32[]{:S(2)}, u32[]{:S(2)}) collective-permute-start(bf16[832,256]{1,0:T(8,128)(2,1)} %bitcast.14), channel_id=1, source_target_pairs={{0,4},{1,5},{4,8},{5,9},{8,12},{9,13},{12,14},{13,15},{14,10},{15,... | collective-permute-start | bytes 1277960 | tf_op jit(solution)/shard_map/ppermute | solution.py:211
  3.7 11.8 %collective-permute-start = (bf16[832,256]{1,0:T(8,128)(2,1)}, bf16[832,256]{1,0:T(8,128)(2,1)S(1)}, u32[]{:S(2)}, u32[]{:S(2)}) collective-permute-start(bf16[832,256]{1,0:T(8,128)(2,1)} %bitcast.15), channel_id=1, source_target_pairs={{0,2},{1,3},{4,0},{5,1},{8,4},{9,5},{12,8},{13,9},{14,12},{15,13},... | collective-permute-start | bytes 1277960 | tf_op jit(solution)/shard_map/ppermute | solution.py:211
  3.7 34.4 %copy-start = (bf16[4096,448]{0,1:T(8,128)(2,1)S(1)}, bf16[4096,448]{0,1:T(8,128)(2,1)}, u32[]{:S(2)}) copy-start(bf16[4096,448]{0,1:T(8,128)(2,1)} %param.8) | copy-start | bytes 11010052
  6.7 19.4 %collective-permute-start.4 = (f16[448,832]{1,0:T(8,128)(2,1)S(1)}, f16[448,832]{1,0:T(8,128)(2,1)S(1)}, u32[]{:S(2)}, u32[]{:S(2)}) collective-permute-start(f16[448,832]{1,0:T(8,128)(2,1)S(1)} %get-tuple-element.38), channel_id=1, source_target_pairs={{0,16},{16,0},{1,17},{17,1},{2,18},{18,2},{3,19},{19,3},{4,20},{20... | collective-permute-start | bytes 2236424 | tf_op jit(solution)/shard_map/ppermute | solution.py:197
  13.7 12.6 %collective-permute-start.3 = (bf16[832,256]{1,0:T(8,128)(2,1)S(1)}, bf16[832,256]{1,0:T(8,128)(2,1)S(1)}, u32[]{:S(2)}, u32[]{:S(2)}) collective-permute-start(bf16[832,256]{1,0:T(8,128)(2,1)S(1)} %collective-permute-done.2.refs_2_), channel_id=1, source_target_pairs={{0,4},{1,5},{4,8},{5,9},{8,12},{9,13},{12,14},{13,15},{14,10},{15,... | collective-permute-start | bytes 1277960 | tf_op jit(solution)/shard_map/ppermute | solution.py:211
  15.5 10.7 %collective-permute-start.1 = (bf16[832,256]{1,0:T(8,128)(2,1)S(1)}, bf16[832,256]{1,0:T(8,128)(2,1)S(1)}, u32[]{:S(2)}, u32[]{:S(2)}) collective-permute-start(bf16[832,256]{1,0:T(8,128)(2,1)S(1)} %collective-permute-done.refs_3_), channel_id=1, source_target_pairs={{0,2},{1,3},{4,0},{5,1},{8,4},{9,5},{12,8},{13,9},{14,12},{15,13},... | collective-permute-start | bytes 1277960 | tf_op jit(solution)/shard_map/ppermute | solution.py:211
  15.7 13.1 %collective-permute-start.9 = (bf16[832,256]{1,0:T(8,128)(2,1)S(1)}, bf16[832,256]{1,0:T(8,128)(2,1)S(1)}, u32[]{:S(2)}, u32[]{:S(2)}) collective-permute-start(bf16[832,256]{1,0:T(8,128)(2,1)S(1)} %bitcast.16), channel_id=1, source_target_pairs={{0,1},{1,0},{2,3},{3,2},{4,5},{5,4},{6,7},{7,6},{8,9},{9,8},{10,11... | collective-permute-start | bytes 1277960 | tf_op jit(solution)/shard_map/ppermute | solution.py:214
  26.2 10.4 %collective-permute-start.6 = (bf16[832,256]{1,0:T(8,128)(2,1)S(1)}, bf16[832,256]{1,0:T(8,128)(2,1)S(1)}, u32[]{:S(2)}, u32[]{:S(2)}) collective-permute-start(bf16[832,256]{1,0:T(8,128)(2,1)S(1)} %collective-permute-done.1.refs_1_), channel_id=1, source_target_pairs={{0,2},{1,3},{4,0},{5,1},{8,4},{9,5},{12,8},{13,9},{14,12},{15,13},... | collective-permute-start | bytes 1277960 | tf_op jit(solution)/shard_map/ppermute | solution.py:211
  27.9 8.7 %collective-permute-start.10 = (bf16[832,256]{1,0:T(8,128)(2,1)S(1)}, bf16[832,256]{1,0:T(8,128)(2,1)S(1)}, u32[]{:S(2)}, u32[]{:S(2)}) collective-permute-start(bf16[832,256]{1,0:T(8,128)(2,1)S(1)} %collective-permute-done.2.refs_2_), channel_id=1, source_target_pairs={{0,1},{1,0},{2,3},{3,2},{4,5},{5,4},{6,7},{7,6},{8,9},{9,8},{10,11... | collective-permute-start | bytes 1277960 | tf_op jit(solution)/shard_map/ppermute | solution.py:214
  27.9 11.1 %collective-permute-start.11 = (bf16[832,256]{1,0:T(8,128)(2,1)S(1)}, bf16[832,256]{1,0:T(8,128)(2,1)S(1)}, u32[]{:S(2)}, u32[]{:S(2)}) collective-permute-start(bf16[832,256]{1,0:T(8,128)(2,1)S(1)} %collective-permute-done.refs_3_), channel_id=1, source_target_pairs={{0,1},{1,0},{2,3},{3,2},{4,5},{5,4},{6,7},{7,6},{8,9},{9,8},{10,11... | collective-permute-start | bytes 1277960 | tf_op jit(solution)/shard_map/ppermute | solution.py:214
  28.5 12.5 %collective-permute-start.5 = (bf16[832,256]{1,0:T(8,128)(2,1)S(1)}, bf16[832,256]{1,0:T(8,128)(2,1)S(1)}, u32[]{:S(2)}, u32[]{:S(2)}) collective-permute-start(bf16[832,256]{1,0:T(8,128)(2,1)S(1)} %collective-permute-done.3.refs_0_), channel_id=1, source_target_pairs={{0,4},{1,5},{4,8},{5,9},{8,12},{9,13},{12,14},{13,15},{14,10},{15,... | collective-permute-start | bytes 1277960 | tf_op jit(solution)/shard_map/ppermute | solution.py:211
  28.8 12.7 %collective-permute-start.14 = (bf16[832,256]{1,0:T(8,128)(2,1)S(1)}, bf16[832,256]{1,0:T(8,128)(2,1)S(1)}, u32[]{:S(2)}, u32[]{:S(2)}) collective-permute-start(bf16[832,256]{1,0:T(8,128)(2,1)S(1)} %collective-permute-done.3.refs_0_), channel_id=1, source_target_pairs={{0,1},{1,0},{2,3},{3,2},{4,5},{5,4},{6,7},{7,6},{8,9},{9,8},{10,11... | collective-permute-start | bytes 1277960 | tf_op jit(solution)/shard_map/ppermute | solution.py:214
  36.7 5.4 %collective-permute-start.15 = (bf16[832,256]{1,0:T(8,128)(2,1)S(1)}, bf16[832,256]{1,0:T(8,128)(2,1)S(1)}, u32[]{:S(2)}, u32[]{:S(2)}) collective-permute-start(bf16[832,256]{1,0:T(8,128)(2,1)S(1)} %collective-permute-done.1.refs_1_), channel_id=1, source_target_pairs={{0,1},{1,0},{2,3},{3,2},{4,5},{5,4},{6,7},{7,6},{8,9},{9,8},{10,11... | collective-permute-start | bytes 1277960 | tf_op jit(solution)/shard_map/ppermute | solution.py:214
  36.7 9.8 %collective-permute-start.13 = (bf16[576,256]{1,0:T(8,128)(2,1)S(1)}, bf16[576,256]{1,0:T(8,128)(2,1)S(1)}, u32[]{:S(2)}, u32[]{:S(2)}) collective-permute-start(bf16[576,256]{1,0:T(8,128)(2,1)S(1)} %slice.103), channel_id=1, source_target_pairs={{0,2},{1,3},{4,0},{5,1},{8,4},{9,5},{12,8},{13,9},{14,12},{15,13},... | collective-permute-start | bytes 884744 | tf_op jit(solution)/shard_map/ppermute | solution.py:211
  41.0 5.5 %collective-permute-start.12 = (bf16[256,256]{1,0:T(8,128)(2,1)S(1)}, bf16[256,256]{1,0:T(8,128)(2,1)S(1)}, u32[]{:S(2)}, u32[]{:S(2)}) collective-permute-start(bf16[256,256]{1,0:T(8,128)(2,1)S(1)} %slice.102), channel_id=1, source_target_pairs={{0,4},{1,5},{4,8},{5,9},{8,12},{9,13},{12,14},{13,15},{14,10},{15,... | collective-permute-start | bytes 393224 | tf_op jit(solution)/shard_map/ppermute | solution.py:211
  41.5 6.7 %collective-permute-start.7 = (bf16[832,256]{1,0:T(8,128)(2,1)S(1)}, bf16[832,256]{1,0:T(8,128)(2,1)S(1)}, u32[]{:S(2)}, u32[]{:S(2)}) collective-permute-start(bf16[832,256]{1,0:T(8,128)(2,1)S(1)} %collective-permute-done.5.refs_0_), channel_id=1, source_target_pairs={{0,1},{1,0},{2,3},{3,2},{4,5},{5,4},{6,7},{7,6},{8,9},{9,8},{10,11... | collective-permute-start | bytes 1277960 | tf_op jit(solution)/shard_map/ppermute | solution.py:214
  41.5 6.7 %collective-permute-start.8 = (bf16[832,256]{1,0:T(8,128)(2,1)S(1)}, bf16[832,256]{1,0:T(8,128)(2,1)S(1)}, u32[]{:S(2)}, u32[]{:S(2)}) collective-permute-start(bf16[832,256]{1,0:T(8,128)(2,1)S(1)} %collective-permute-done.6.refs_1_), channel_id=1, source_target_pairs={{0,1},{1,0},{2,3},{3,2},{4,5},{5,4},{6,7},{7,6},{8,9},{9,8},{10,11... | collective-permute-start | bytes 1277960 | tf_op jit(solution)/shard_map/ppermute | solution.py:214
  43.5 5.5 %copy-start.2 = (f32[832,448]{0,1:T(8,128)S(1)}, f32[832,448]{0,1:T(8,128)}, u32[]{:S(2)}) copy-start(f32[832,448]{0,1:T(8,128)} %param.12) | copy-start | bytes 4472836
  43.5 5.5 %copy-start.3 = (f32[832,448]{0,1:T(8,128)S(1)}, f32[832,448]{0,1:T(8,128)}, u32[]{:S(2)}) copy-start(f32[832,448]{0,1:T(8,128)} %param.9) | copy-start | bytes 4472836
  43.5 5.5 %copy-start.4 = (f32[832,448]{0,1:T(8,128)S(1)}, f32[832,448]{0,1:T(8,128)}, u32[]{:S(2)}) copy-start(f32[832,448]{0,1:T(8,128)} %param.11) | copy-start | bytes 4472836
  43.5 5.5 %copy-start.5 = (f32[832,448]{0,1:T(8,128)S(1)}, f32[832,448]{0,1:T(8,128)}, u32[]{:S(2)}) copy-start(f32[832,448]{0,1:T(8,128)} %param.10) | copy-start | bytes 4472836
  46.5 1.8 %collective-permute-start.17 = (bf16[576,256]{1,0:T(8,128)(2,1)S(1)}, bf16[576,256]{1,0:T(8,128)(2,1)S(1)}, u32[]{:S(2)}, u32[]{:S(2)}) collective-permute-start(bf16[576,256]{1,0:T(8,128)(2,1)S(1)} %collective-permute-done.13.refs_5_), channel_id=1, source_target_pairs={{0,1},{1,0},{2,3},{3,2},{4,5},{5,4},{6,7},{7,6},{8,9},{9,8},{10,11... | collective-permute-start | bytes 884744 | tf_op jit(solution)/shard_map/ppermute | solution.py:214
  46.5 1.8 %collective-permute-start.16 = (bf16[256,256]{1,0:T(8,128)(2,1)S(1)}, bf16[256,256]{1,0:T(8,128)(2,1)S(1)}, u32[]{:S(2)}, u32[]{:S(2)}) collective-permute-start(bf16[256,256]{1,0:T(8,128)(2,1)S(1)} %collective-permute-done.12.refs_4_), channel_id=1, source_target_pairs={{0,1},{1,0},{2,3},{3,2},{4,5},{5,4},{6,7},{7,6},{8,9},{9,8},{10,11... | collective-permute-start | bytes 393224 | tf_op jit(solution)/shard_map/ppermute | solution.py:214
  49.7 8.5 %collective-permute-start.20 = (f16[448,256]{1,0:T(8,128)(2,1)S(1)}, f16[448,256]{1,0:T(8,128)(2,1)S(1)}, u32[]{:S(2)}, u32[]{:S(2)}) collective-permute-start(f16[448,256]{1,0:T(8,128)(2,1)S(1)} %fusion.15), channel_id=1, source_target_pairs={{0,16},{16,0},{1,17},{17,1},{2,18},{18,2},{3,19},{19,3},{4,20},{20... | collective-permute-start | bytes 688136 | tf_op jit(solution)/shard_map/ppermute | solution.py:197
  52.5 10.5 %collective-permute-start.19 = (f16[448,256]{1,0:T(8,128)(2,1)S(1)}, f16[448,256]{1,0:T(8,128)(2,1)S(1)}, u32[]{:S(2)}, u32[]{:S(2)}) collective-permute-start(f16[448,256]{1,0:T(8,128)(2,1)S(1)} %fusion.23), channel_id=1, source_target_pairs={{0,16},{16,0},{1,17},{17,1},{2,18},{18,2},{3,19},{19,3},{4,20},{20... | collective-permute-start | bytes 688136 | tf_op jit(solution)/shard_map/ppermute | solution.py:197
  54.2 8.9 %copy-start.6 = (f32[832,448]{0,1:T(8,128)S(1)}, f32[832,448]{0,1:T(8,128)}, u32[]{:S(2)}) copy-start(f32[832,448]{0,1:T(8,128)} %param.13) | copy-start | bytes 4472836
  55.1 14.5 %collective-permute-start.18 = (f16[448,320]{1,0:T(8,128)(2,1)S(1)}, f16[448,320]{1,0:T(8,128)(2,1)S(1)}, u32[]{:S(2)}, u32[]{:S(2)}) collective-permute-start(f16[448,320]{1,0:T(8,128)(2,1)S(1)} %fusion.1), channel_id=1, source_target_pairs={{0,16},{16,0},{1,17},{17,1},{2,18},{18,2},{3,19},{19,3},{4,20},{20... | collective-permute-start | bytes 860168 | tf_op jit(solution)/shard_map/ppermute | solution.py:197

commit v3 on v2

--- a/solution.py
+++ b/solution.py
@@ -224,21 +224,20 @@
     early_others = [other_groups_sum(early16[0])]
     grad = sort_tokens(behind(mine, [first[0]]), chips)
     came = [with_other([own], to_other_core([own])), with_other(first, to_other_core(first))]
+    head = sum(came, [])
+    sums = [gradient_part(0, features, 0, grad, head)]
     newest = first
+    middle = []
     for step in range(2, half - 1):
         newest = send(newest)
-        came.append(with_other(newest, to_other_core(newest)))
-    head = sum(came[:2], [])
-    newest = send(newest, early_others)
-    sums = [gradient_part(0, features, 0, grad, head)]
-    middle = sum(came[2:], [])
+        middle += with_other(newest, to_other_core(newest))
+    newest = send(newest)
+    top = features // 2
+    final = send([newest[0][:top], newest[1][top:]], *[early_others, sums])
+    theirs = to_other_core(newest)
     sums2 = [gradient_part(0, features, len(head), grad, middle, (sums[0],))]
     skip = len(head) + len(middle)
-    top = cuts[1]
-    final = send([newest[0][:top], newest[1][top:]], sums)
-    third = [[b] for b in newest]
-    theirs = to_other_core(newest)
-    theirs_final = to_other_core(final, sums2)
+    theirs_final = to_other_core(final, *[sums2])
     tail = with_other(newest, theirs) + [(final[0], 0, 0), (final[1], top, 1), (theirs_final[0], 0, 0), (theirs_final[1], top, 1)]
     so_far = (sums2[0],)
     outs = ()

time: 71.1 us -> 66.3 us (0.932)
  waiting for transfers between devices: 38.3 us -> 33.6 us
    ppermute x4, waiting for transfers between devices: 21.2 us -> 10.8 us  [other_groups_sum(): came = lax.ppermute(value, 'replica', there).astype(jnp.float32)]
    ppermute x8, waiting for transfers between devices: 15.7 us -> 21.3 us  [send(): lax.ppermute(b, 'tensor', pairs[hop])]
  transfers between devices with their start and end apart: 21 -> 21, of which waited for: 8 -> 9; matrix products, arithmetic and copies ran while one was open for 7% -> 7% of each run, Pallas kernels for 11% -> 12%
where the time goes in v3:
time: 66.3 us; the launch traced here: 66.2 us
  waiting for transfers between devices  33.6 us (51%)
  starting transfers between devices  16.6 us (25%)
  Pallas kernels  9.4 us (14%)
  other arithmetic  5.72 us (9%)
  between operations  0.85 us (1%)
    ppermute x8, waiting for transfers between devices, send(): lax.ppermute(b, 'tensor', pairs[hop])  21.3 us
    ppermute x4, waiting for transfers between devices, other_groups_sum(): came = lax.ppermute(value, 'replica', there).astype(jnp.float32)  10.8 us
    ppermute x8, starting transfers between devices, send(): lax.ppermute(b, 'tensor', pairs[hop])  9.26 us
    pallas_call x5, Pallas kernels, gradient_part(): pl.pallas_call(functools.partial(gradient_kernel, low, skip, [b[1:] for b...  5.78 us
    ppermute x4, starting transfers between devices, other_groups_sum(): came = lax.ppermute(value, 'replica', there).astype(jnp.float32)  5.77 us
    convert_element_type x1, other arithmetic, on_device(): early16 = [early.astype(jnp.float16)]  2.82 us
    pallas_call x3, Pallas kernels, place(): pl.pallas_call(functools.partial(place_kernel, low), out_shape=tuple((jax...  2.71 us
    convert_element_type x3, other arithmetic, late_part(): return (exact - half + INNER_RATE * step).astype(jnp.float16)  2.12 us
  transfers between devices with their start and end apart: 21, of which 9 were waited for; matrix products, arithmetic and copies ran while one was open for 7% of the time, Pallas kernels for 12%

profile of v3, /device:TPU:0, one launch (start us, length us, event | category | flops | bytes accessed | tf_op | source)
XLA Modules:
  0.0 66.2 jit_solution(18321692260654153746)
XLA Ops:
  0.6 3.1 %collective-permute-start.3 = (bf16[832,256]{1,0:T(8,128)(2,1)}, bf16[832,256]{1,0:T(8,128)(2,1)S(1)}, u32[]{:S(2)}, u32[]{:S(2)}) collective-permute-start(bf16[832,256]{1,0:T(8,128)(2,1)} %bitcast.14), channel_id=1, source_target_pairs={{0,4},{1,5},{4,8},{5,9},{8,12},{9,13},{12,14},{13,15},{14,10},{15,... | collective-permute-start | bytes 1277960 | tf_op jit(solution)/shard_map/ppermute | solution.py:211
  3.7 2.8 %fusion.42 = (f16[448,832]{1,0:T(8,128)(2,1)S(1)}, f32[448,832]{1,0:T(8,128)S(1)}) fusion(f32[832,448]{0,1:T(8,128)} %param.9, f32[832,448]{0,1:T(8,128)} %param.12), kind=kLoop, calls=%fused_computation.67 | loop fusion | flops 1490944 | bytes 5218304 | tf_op jit(solution)/shard_map/convert_element_type | solution.py:223
  6.5 2.0 %collective-permute-start.6 = (f16[448,832]{1,0:T(8,128)(2,1)S(1)}, f16[448,832]{1,0:T(8,128)(2,1)S(1)}, u32[]{:S(2)}, u32[]{:S(2)}) collective-permute-start(f16[448,832]{1,0:T(8,128)(2,1)S(1)} %get-tuple-element.40), channel_id=1, source_target_pairs={{0,16},{16,0},{1,17},{17,1},{2,18},{18,2},{3,19},{19,3},{4,20},{20... | collective-permute-start | bytes 2236424 | tf_op jit(solution)/shard_map/ppermute | solution.py:197
  8.6 0.0 collective-permute-start.7
  8.6 5.1 %collective-permute-done.3.refs_2_ = bf16[832,256]{1,0:T(8,128)(2,1)S(1)} collective-permute-done((bf16[832,256]{1,0:T(8,128)(2,1)}, bf16[832,256]{1,0:T(8,128)(2,1)S(1)}, u32[]{:S(2)}, u32[]{:S(2)}) %collective-permute-start.3) | collective-permute-done | bytes 426016 | tf_op jit(solution)/shard_map/ppermute | solution.py:211
  13.7 1.8 %collective-permute-start.4 = (bf16[832,256]{1,0:T(8,128)(2,1)S(1)}, bf16[832,256]{1,0:T(8,128)(2,1)S(1)}, u32[]{:S(2)}, u32[]{:S(2)}) collective-permute-start(bf16[832,256]{1,0:T(8,128)(2,1)S(1)} %collective-permute-done.3.refs_2_), channel_id=1, source_target_pairs={{0,4},{1,5},{4,8},{5,9},{8,12},{9,13},{12,14},{13,15},{14,10},{15,... | collective-permute-start | bytes 1277960 | tf_op jit(solution)/shard_map/ppermute | solution.py:211
  15.5 0.0 collective-permute-done.refs_3_
  15.5 0.2 collective-permute-start.1
  15.7 0.5 collective-permute-start.9
  16.2 8.5 %collective-permute-done.4.refs_0_ = bf16[832,256]{1,0:T(8,128)(2,1)S(1)} collective-permute-done((bf16[832,256]{1,0:T(8,128)(2,1)S(1)}, bf16[832,256]{1,0:T(8,128)(2,1)S(1)}, u32[]{:S(2)}, u32[]{:S(2)}) %collective-permute-start.4) | collective-permute-done | bytes 426016 | tf_op jit(solution)/shard_map/ppermute | solution.py:211
  24.7 1.5 %collective-permute-start.5 = (bf16[832,256]{1,0:T(8,128)(2,1)S(1)}, bf16[832,256]{1,0:T(8,128)(2,1)S(1)}, u32[]{:S(2)}, u32[]{:S(2)}) collective-permute-start(bf16[832,256]{1,0:T(8,128)(2,1)S(1)} %collective-permute-done.4.refs_0_), channel_id=1, source_target_pairs={{0,4},{1,5},{4,8},{5,9},{8,12},{9,13},{12,14},{13,15},{14,10},{15,... | collective-permute-start | bytes 1277960 | tf_op jit(solution)/shard_map/ppermute | solution.py:211
  26.2 0.5 collective-permute-start.2
  26.7 0.0 collective-permute-done.6
  26.7 0.5 collective-permute-start.15
  27.2 0.9 %sort_tokens.1.grad_ref = bf16[448,4096]{1,0:T(8,128)(2,1)S(1)} custom-call(bf16[448,4096]{1,0:T(8,128)(2,1)S(1)} %bitcast.13), custom_call_target="tpu_custom_call" | custom-call | bytes 7340032 | tf_op jit(solution)/shard_map/sort_tokens/pallas_call | solution.py:73
  28.1 0.1 convert_element_type.43
  28.3 1.9 %gradient.5.refs_4_ = f32[448,832]{1,0:T(8,128)S(1)} custom-call(bf16[448,4096]{1,0:T(8,128)(2,1)S(1)} %sort_tokens.1.grad_ref, bf16[832,256]{1,0:T(8,128)(2,1)S(1)} %bitcast.17, bf16[832,256]{1,0:T(8,128)(2,1)S(1)} %collective-permute-done.7.refs_1_, bf16[832,256]{1,0:T(8,128)(2,1)S(1)} %collective-permute-done.3.refs_2_, ...), custom_call_target="tpu_custom_call" | custom-call | flops 1145044992 | bytes 2981888 | tf_op jit(solution)/shard_map/gradient/pallas_call | solution.py:146
  30.2 4.6 %collective-permute-done.5.refs_0_ = bf16[832,256]{1,0:T(8,128)(2,1)S(1)} collective-permute-done((bf16[832,256]{1,0:T(8,128)(2,1)S(1)}, bf16[832,256]{1,0:T(8,128)(2,1)S(1)}, u32[]{:S(2)}, u32[]{:S(2)}) %collective-permute-start.5) | collective-permute-done | bytes 426016 | tf_op jit(solution)/shard_map/ppermute | solution.py:211
  34.8 1.4 %collective-permute-start.12 = (bf16[416,256]{1,0:T(8,128)(2,1)S(1)}, bf16[416,256]{1,0:T(8,128)(2,1)S(1)}, u32[]{:S(2)}, u32[]{:S(2)}) collective-permute-start(bf16[416,256]{1,0:T(8,128)(2,1)S(1)} %slice.98), channel_id=1, source_target_pairs={{0,4},{1,5},{4,8},{5,9},{8,12},{9,13},{12,14},{13,15},{14,10},{15,... | collective-permute-start | bytes 638984 | tf_op jit(solution)/shard_map/ppermute | solution.py:211
  36.2 0.7 %collective-permute-start.13 = (bf16[416,256]{1,0:T(8,128)(2,1)S(1)}, bf16[416,256]{1,0:T(8,128)(2,1)S(1)}, u32[]{:S(2)}, u32[]{:S(2)}) collective-permute-start(bf16[416,256]{1,0:T(8,128)(2,1)S(1)} %slice.97), channel_id=1, source_target_pairs={{0,2},{1,3},{4,0},{5,1},{8,4},{9,5},{12,8},{13,9},{14,12},{15,13},... | collective-permute-start | bytes 638984 | tf_op jit(solution)/shard_map/ppermute | solution.py:211
  36.9 0.5 collective-permute-start.11
  37.4 1.4 %gradient.6.refs_8_ = f32[448,832]{1,0:T(8,128)S(1)} custom-call(bf16[448,4096]{1,0:T(8,128)(2,1)S(1)} %sort_tokens.1.grad_ref, bf16[832,256]{1,0:T(8,128)(2,1)S(1)} %collective-permute-done.4.refs_0_, bf16[832,256]{1,0:T(8,128)(2,1)S(1)} %collective-permute-done.1.refs_1_, bf16[832,256]{1,0:T(8,128)(2,1)S(1)} %collective-permute-done.14.refs_2_, ...), custom_call_target="tpu_custom_call" | custom-call | flops 763363328 | bytes 2981888 | tf_op jit(solution)/shard_map/gradient/pallas_call | solution.py:146
  38.9 0.0 copy-start.2
  38.9 0.0 copy-start.3
  38.9 0.0 copy-start.4
  38.9 0.0 copy-start.5
  38.9 1.7 %collective-permute-done.12.refs_4_ = bf16[416,256]{1,0:T(8,128)(2,1)S(1)} collective-permute-done((bf16[416,256]{1,0:T(8,128)(2,1)S(1)}, bf16[416,256]{1,0:T(8,128)(2,1)S(1)}, u32[]{:S(2)}, u32[]{:S(2)}) %collective-permute-start.12) | collective-permute-done | bytes 213024 | tf_op jit(solution)/shard_map/ppermute | solution.py:211
  40.7 1.4 %collective-permute-done.13.refs_5_ = bf16[416,256]{1,0:T(8,128)(2,1)S(1)} collective-permute-done((bf16[416,256]{1,0:T(8,128)(2,1)S(1)}, bf16[416,256]{1,0:T(8,128)(2,1)S(1)}, u32[]{:S(2)}, u32[]{:S(2)}) %collective-permute-start.13) | collective-permute-done | bytes 213024 | tf_op jit(solution)/shard_map/ppermute | solution.py:211
  42.1 0.0 collective-permute-done.16.refs_6_
  42.1 1.4 %collective-permute-done.17.refs_7_ = bf16[416,256]{1,0:T(8,128)(2,1)S(1)} collective-permute-done((bf16[416,256]{1,0:T(8,128)(2,1)S(1)}, bf16[416,256]{1,0:T(8,128)(2,1)S(1)}, u32[]{:S(2)}, u32[]{:S(2)}) %collective-permute-start.17) | collective-permute-done | bytes 213024 | tf_op jit(solution)/shard_map/ppermute | solution.py:214
  43.5 0.7 %gradient.7 = f32[448,256]{1,0:T(8,128)S(1)} custom-call(bf16[448,4096]{1,0:T(8,128)(2,1)S(1)} %sort_tokens.1.grad_ref, bf16[832,256]{1,0:T(8,128)(2,1)S(1)} %collective-permute-done.5.refs_0_, bf16[832,256]{1,0:T(8,128)(2,1)S(1)} %collective-permute-done.2.refs_1_, bf16[832,256]{1,0:T(8,128)(2,1)S(1)} %collective-permute-done.10.refs_2_, ...), custom_call_target="tpu_custom_call" | custom-call | flops 352321536 | bytes 917504 | tf_op jit(solution)/shard_map/gradient/pallas_call | solution.py:146
  44.3 0.6 fusion.15
  44.9 1.6 %collective-permute-start.20 = (f16[448,256]{1,0:T(8,128)(2,1)S(1)}, f16[448,256]{1,0:T(8,128)(2,1)S(1)}, u32[]{:S(2)}, u32[]{:S(2)}) collective-permute-start(f16[448,256]{1,0:T(8,128)(2,1)S(1)} %fusion.15), channel_id=1, source_target_pairs={{0,16},{16,0},{1,17},{17,1},{2,18},{18,2},{3,19},{19,3},{4,20},{20... | collective-permute-start | bytes 688136 | tf_op jit(solution)/shard_map/ppermute | solution.py:197
  46.5 0.7 %gradient.8 = f32[448,256]{1,0:T(8,128)S(1)} custom-call(bf16[448,4096]{1,0:T(8,128)(2,1)S(1)} %sort_tokens.1.grad_ref, bf16[832,256]{1,0:T(8,128)(2,1)S(1)} %collective-permute-done.5.refs_0_, bf16[832,256]{1,0:T(8,128)(2,1)S(1)} %collective-permute-done.2.refs_1_, bf16[832,256]{1,0:T(8,128)(2,1)S(1)} %collective-permute-done.10.refs_2_, ...), custom_call_target="tpu_custom_call" | custom-call | flops 352321536 | bytes 917504 | tf_op jit(solution)/shard_map/gradient/pallas_call | solution.py:146
  47.2 0.6 fusion.23
  47.8 0.6 collective-permute-start.19
  48.4 1.1 %gradient.9 = f32[448,320]{1,0:T(8,128)S(1)} custom-call(bf16[448,4096]{1,0:T(8,128)(2,1)S(1)} %sort_tokens.1.grad_ref, bf16[832,256]{1,0:T(8,128)(2,1)S(1)} %collective-permute-done.5.refs_0_, bf16[832,256]{1,0:T(8,128)(2,1)S(1)} %collective-permute-done.2.refs_1_, bf16[832,256]{1,0:T(8,128)(2,1)S(1)} %collective-permute-done.10.refs_2_, ...), custom_call_target="tpu_custom_call" | custom-call | flops 440401920 | bytes 1146880 | tf_op jit(solution)/shard_map/gradient/pallas_call | solution.py:146
  49.4 0.0 copy-start.6
  49.5 0.9 %fusion.1 = f16[448,320]{1,0:T(8,128)(2,1)S(1)} fusion(f32[448,320]{1,0:T(8,128)S(1)} %gradient.9, f32[448,832]{1,0:T(8,128)S(1)} %bitcast.30, f32[448,832]{1,0:T(8,128)S(1)} %bitcast.33, f32[448,832]{1,0:T(8,128)S(1)} %bitcast.25, f32[448,832]{1,0:T(8,128)S(1)} %bitcast.20), kind=kLoop, calls=%fused_computation.4 | loop fusion | flops 2580480 | bytes 3153920 | tf_op jit(solution)/shard_map/convert_element_type | solution.py:175
  50.4 1.6 %collective-permute-start.18 = (f16[448,320]{1,0:T(8,128)(2,1)S(1)}, f16[448,320]{1,0:T(8,128)(2,1)S(1)}, u32[]{:S(2)}, u32[]{:S(2)}) collective-permute-start(f16[448,320]{1,0:T(8,128)(2,1)S(1)} %fusion.1), channel_id=1, source_target_pairs={{0,16},{16,0},{1,17},{17,1},{2,18},{18,2},{3,19},{19,3},{4,20},{20... | collective-permute-start | bytes 860168 | tf_op jit(solution)/shard_map/ppermute | solution.py:197
  52.0 1.5 %collective-permute-done.20 = f16[448,256]{1,0:T(8,128)(2,1)S(1)} collective-permute-done((f16[448,256]{1,0:T(8,128)(2,1)S(1)}, f16[448,256]{1,0:T(8,128)(2,1)S(1)}, u32[]{:S(2)}, u32[]{:S(2)}) %collective-permute-start.20) | collective-permute-done | bytes 229408 | tf_op jit(solution)/shard_map/ppermute | solution.py:197
  53.4 4.9 %collective-permute-done.19 = f16[448,256]{1,0:T(8,128)(2,1)S(1)} collective-permute-done((f16[448,256]{1,0:T(8,128)(2,1)S(1)}, f16[448,256]{1,0:T(8,128)(2,1)S(1)}, u32[]{:S(2)}, u32[]{:S(2)}) %collective-permute-start.19) | collective-permute-done | bytes 229408 | tf_op jit(solution)/shard_map/ppermute | solution.py:197
  58.3 0.4 subtract_convert_fusion.1
  58.7 0.9 %place.3 = (bf16[448,832]{1,0:T(8,128)(2,1)}, f32[448,832]{1,0:T(8,128)}) custom-call(bf16[448,256]{1,0:T(8,128)(2,1)S(1)} %get-tuple-element.42.refs_0_, f32[448,256]{1,0:T(8,128)S(1)} %get-tuple-element.47.refs_1_), custom_call_target="tpu_custom_call" | custom-call | bytes 1376256 | tf_op jit(solution)/shard_map/place/pallas_call | solution.py:98
  59.6 0.9 %place.4 = (bf16[448,832]{1,0:T(8,128)(2,1)}, f32[448,832]{1,0:T(8,128)}) custom-call(bf16[448,256]{1,0:T(8,128)(2,1)S(1)} %get-tuple-element.43.refs_0_, f32[448,256]{1,0:T(8,128)S(1)} %get-tuple-element.46.refs_1_, bf16[448,832]{1,0:T(8,128)(2,1)} %get-tuple-element.34.refs_2_, ...), custom_call_target="tpu_custom_call", output_to_operand_aliasing={{0}: (2, {}), {1}: (3, {})} | custom-call | bytes 1376256 | tf_op jit(solution)/shard_map/place/pallas_call | solution.py:98
  60.5 4.4 %collective-permute-done.18 = f16[448,320]{1,0:T(8,128)(2,1)S(1)} collective-permute-done((f16[448,320]{1,0:T(8,128)(2,1)S(1)}, f16[448,320]{1,0:T(8,128)(2,1)S(1)}, u32[]{:S(2)}, u32[]{:S(2)}) %collective-permute-start.18) | collective-permute-done | bytes 286752 | tf_op jit(solution)/shard_map/ppermute | solution.py:197
  64.9 0.3 fusion.8
  65.2 1.0 %place.5 = (bf16[448,832]{1,0:T(8,128)(2,1)}, f32[448,832]{1,0:T(8,128)}) custom-call(bf16[448,320]{1,0:T(8,128)(2,1)S(1)} %get-tuple-element.45.refs_0_, f32[448,320]{1,0:T(8,128)S(1)} %get-tuple-element.44.refs_1_, bf16[448,832]{1,0:T(8,128)(2,1)} %get-tuple-element.36.refs_2_, ...), custom_call_target="tpu_custom_call", output_to_operand_aliasing={{0}: (2, {}), {1}: (3, {})} | custom-call | bytes 1720320 | tf_op jit(solution)/shard_map/place/pallas_call | solution.py:98
  (26 shorter events, 0.1 us)
Async XLA Ops:
  0.6 8.0 %copy-start.1 = (bf16[256,832]{0,1:T(8,128)(2,1)S(1)}, bf16[256,832]{0,1:T(8,128)(2,1)}, u32[]{:S(2)}) copy-start(bf16[256,832]{0,1:T(8,128)(2,1)} %param.7) | copy-start | bytes 1277956
  0.6 26.6 %copy-start = (bf16[4096,448]{0,1:T(8,128)(2,1)S(1)}, bf16[4096,448]{0,1:T(8,128)(2,1)}, u32[]{:S(2)}) copy-start(bf16[4096,448]{0,1:T(8,128)(2,1)} %param.8) | copy-start | bytes 11010052
  0.6 13.0 %collective-permute-start.3 = (bf16[832,256]{1,0:T(8,128)(2,1)}, bf16[832,256]{1,0:T(8,128)(2,1)S(1)}, u32[]{:S(2)}, u32[]{:S(2)}) collective-permute-start(bf16[832,256]{1,0:T(8,128)(2,1)} %bitcast.14), channel_id=1, source_target_pairs={{0,4},{1,5},{4,8},{5,9},{8,12},{9,13},{12,14},{13,15},{14,10},{15,... | collective-permute-start | bytes 1277960 | tf_op jit(solution)/shard_map/ppermute | solution.py:211
  3.7 11.8 %collective-permute-start = (bf16[832,256]{1,0:T(8,128)(2,1)}, bf16[832,256]{1,0:T(8,128)(2,1)S(1)}, u32[]{:S(2)}, u32[]{:S(2)}) collective-permute-start(bf16[832,256]{1,0:T(8,128)(2,1)} %bitcast.15), channel_id=1, source_target_pairs={{0,2},{1,3},{4,0},{5,1},{8,4},{9,5},{12,8},{13,9},{14,12},{15,13},... | collective-permute-start | bytes 1277960 | tf_op jit(solution)/shard_map/ppermute | solution.py:211
  6.5 20.2 %collective-permute-start.6 = (f16[448,832]{1,0:T(8,128)(2,1)S(1)}, f16[448,832]{1,0:T(8,128)(2,1)S(1)}, u32[]{:S(2)}, u32[]{:S(2)}) collective-permute-start(f16[448,832]{1,0:T(8,128)(2,1)S(1)} %get-tuple-element.40), channel_id=1, source_target_pairs={{0,16},{16,0},{1,17},{17,1},{2,18},{18,2},{3,19},{19,3},{4,20},{20... | collective-permute-start | bytes 2236424 | tf_op jit(solution)/shard_map/ppermute | solution.py:197
  8.6 7.1 %collective-permute-start.7 = (bf16[832,256]{1,0:T(8,128)(2,1)S(1)}, bf16[832,256]{1,0:T(8,128)(2,1)S(1)}, u32[]{:S(2)}, u32[]{:S(2)}) collective-permute-start(bf16[832,256]{1,0:T(8,128)(2,1)S(1)} %bitcast.16), channel_id=1, source_target_pairs={{0,1},{1,0},{2,3},{3,2},{4,5},{5,4},{6,7},{7,6},{8,9},{9,8},{10,11... | collective-permute-start | bytes 1277960 | tf_op jit(solution)/shard_map/ppermute | solution.py:214
  13.7 11.0 %collective-permute-start.4 = (bf16[832,256]{1,0:T(8,128)(2,1)S(1)}, bf16[832,256]{1,0:T(8,128)(2,1)S(1)}, u32[]{:S(2)}, u32[]{:S(2)}) collective-permute-start(bf16[832,256]{1,0:T(8,128)(2,1)S(1)} %collective-permute-done.3.refs_2_), channel_id=1, source_target_pairs={{0,4},{1,5},{4,8},{5,9},{8,12},{9,13},{12,14},{13,15},{14,10},{15,... | collective-permute-start | bytes 1277960 | tf_op jit(solution)/shard_map/ppermute | solution.py:211
  15.5 10.7 %collective-permute-start.1 = (bf16[832,256]{1,0:T(8,128)(2,1)S(1)}, bf16[832,256]{1,0:T(8,128)(2,1)S(1)}, u32[]{:S(2)}, u32[]{:S(2)}) collective-permute-start(bf16[832,256]{1,0:T(8,128)(2,1)S(1)} %collective-permute-done.refs_3_), channel_id=1, source_target_pairs={{0,2},{1,3},{4,0},{5,1},{8,4},{9,5},{12,8},{13,9},{14,12},{15,13},... | collective-permute-start | bytes 1277960 | tf_op jit(solution)/shard_map/ppermute | solution.py:211
  15.7 11.0 %collective-permute-start.8 = (bf16[832,256]{1,0:T(8,128)(2,1)S(1)}, bf16[832,256]{1,0:T(8,128)(2,1)S(1)}, u32[]{:S(2)}, u32[]{:S(2)}) collective-permute-start(bf16[832,256]{1,0:T(8,128)(2,1)S(1)} %collective-permute-done.3.refs_2_), channel_id=1, source_target_pairs={{0,1},{1,0},{2,3},{3,2},{4,5},{5,4},{6,7},{7,6},{8,9},{9,8},{10,11... | collective-permute-start | bytes 1277960 | tf_op jit(solution)/shard_map/ppermute | solution.py:214
  15.7 12.6 %collective-permute-start.9 = (bf16[832,256]{1,0:T(8,128)(2,1)S(1)}, bf16[832,256]{1,0:T(8,128)(2,1)S(1)}, u32[]{:S(2)}, u32[]{:S(2)}) collective-permute-start(bf16[832,256]{1,0:T(8,128)(2,1)S(1)} %collective-permute-done.refs_3_), channel_id=1, source_target_pairs={{0,1},{1,0},{2,3},{3,2},{4,5},{5,4},{6,7},{7,6},{8,9},{9,8},{10,11... | collective-permute-start | bytes 1277960 | tf_op jit(solution)/shard_map/ppermute | solution.py:214
  24.7 10.1 %collective-permute-start.5 = (bf16[832,256]{1,0:T(8,128)(2,1)S(1)}, bf16[832,256]{1,0:T(8,128)(2,1)S(1)}, u32[]{:S(2)}, u32[]{:S(2)}) collective-permute-start(bf16[832,256]{1,0:T(8,128)(2,1)S(1)} %collective-permute-done.4.refs_0_), channel_id=1, source_target_pairs={{0,4},{1,5},{4,8},{5,9},{8,12},{9,13},{12,14},{13,15},{14,10},{15,... | collective-permute-start | bytes 1277960 | tf_op jit(solution)/shard_map/ppermute | solution.py:211
  26.2 10.0 %collective-permute-start.2 = (bf16[832,256]{1,0:T(8,128)(2,1)S(1)}, bf16[832,256]{1,0:T(8,128)(2,1)S(1)}, u32[]{:S(2)}, u32[]{:S(2)}) collective-permute-start(bf16[832,256]{1,0:T(8,128)(2,1)S(1)} %collective-permute-done.1.refs_1_), channel_id=1, source_target_pairs={{0,2},{1,3},{4,0},{5,1},{8,4},{9,5},{12,8},{13,9},{14,12},{15,13},... | collective-permute-start | bytes 1277960 | tf_op jit(solution)/shard_map/ppermute | solution.py:211
  26.7 10.2 %collective-permute-start.14 = (bf16[832,256]{1,0:T(8,128)(2,1)S(1)}, bf16[832,256]{1,0:T(8,128)(2,1)S(1)}, u32[]{:S(2)}, u32[]{:S(2)}) collective-permute-start(bf16[832,256]{1,0:T(8,128)(2,1)S(1)} %collective-permute-done.4.refs_0_), channel_id=1, source_target_pairs={{0,1},{1,0},{2,3},{3,2},{4,5},{5,4},{6,7},{7,6},{8,9},{9,8},{10,11... | collective-permute-start | bytes 1277960 | tf_op jit(solution)/shard_map/ppermute | solution.py:214
  26.7 10.7 %collective-permute-start.15 = (bf16[832,256]{1,0:T(8,128)(2,1)S(1)}, bf16[832,256]{1,0:T(8,128)(2,1)S(1)}, u32[]{:S(2)}, u32[]{:S(2)}) collective-permute-start(bf16[832,256]{1,0:T(8,128)(2,1)S(1)} %collective-permute-done.1.refs_1_), channel_id=1, source_target_pairs={{0,1},{1,0},{2,3},{3,2},{4,5},{5,4},{6,7},{7,6},{8,9},{9,8},{10,11... | collective-permute-start | bytes 1277960 | tf_op jit(solution)/shard_map/ppermute | solution.py:214
  34.8 5.9 %collective-permute-start.12 = (bf16[416,256]{1,0:T(8,128)(2,1)S(1)}, bf16[416,256]{1,0:T(8,128)(2,1)S(1)}, u32[]{:S(2)}, u32[]{:S(2)}) collective-permute-start(bf16[416,256]{1,0:T(8,128)(2,1)S(1)} %slice.98), channel_id=1, source_target_pairs={{0,4},{1,5},{4,8},{5,9},{8,12},{9,13},{12,14},{13,15},{14,10},{15,... | collective-permute-start | bytes 638984 | tf_op jit(solution)/shard_map/ppermute | solution.py:211
  36.2 5.9 %collective-permute-start.13 = (bf16[416,256]{1,0:T(8,128)(2,1)S(1)}, bf16[416,256]{1,0:T(8,128)(2,1)S(1)}, u32[]{:S(2)}, u32[]{:S(2)}) collective-permute-start(bf16[416,256]{1,0:T(8,128)(2,1)S(1)} %slice.97), channel_id=1, source_target_pairs={{0,2},{1,3},{4,0},{5,1},{8,4},{9,5},{12,8},{13,9},{14,12},{15,13},... | collective-permute-start | bytes 638984 | tf_op jit(solution)/shard_map/ppermute | solution.py:211
  36.9 5.2 %collective-permute-start.10 = (bf16[832,256]{1,0:T(8,128)(2,1)S(1)}, bf16[832,256]{1,0:T(8,128)(2,1)S(1)}, u32[]{:S(2)}, u32[]{:S(2)}) collective-permute-start(bf16[832,256]{1,0:T(8,128)(2,1)S(1)} %collective-permute-done.5.refs_0_), channel_id=1, source_target_pairs={{0,1},{1,0},{2,3},{3,2},{4,5},{5,4},{6,7},{7,6},{8,9},{9,8},{10,11... | collective-permute-start | bytes 1277960 | tf_op jit(solution)/shard_map/ppermute | solution.py:214
  36.9 5.2 %collective-permute-start.11 = (bf16[832,256]{1,0:T(8,128)(2,1)S(1)}, bf16[832,256]{1,0:T(8,128)(2,1)S(1)}, u32[]{:S(2)}, u32[]{:S(2)}) collective-permute-start(bf16[832,256]{1,0:T(8,128)(2,1)S(1)} %collective-permute-done.2.refs_1_), channel_id=1, source_target_pairs={{0,1},{1,0},{2,3},{3,2},{4,5},{5,4},{6,7},{7,6},{8,9},{9,8},{10,11... | collective-permute-start | bytes 1277960 | tf_op jit(solution)/shard_map/ppermute | solution.py:214
  38.9 5.4 %copy-start.2 = (f32[832,448]{0,1:T(8,128)S(1)}, f32[832,448]{0,1:T(8,128)}, u32[]{:S(2)}) copy-start(f32[832,448]{0,1:T(8,128)} %param.12) | copy-start | bytes 4472836
  38.9 5.4 %copy-start.3 = (f32[832,448]{0,1:T(8,128)S(1)}, f32[832,448]{0,1:T(8,128)}, u32[]{:S(2)}) copy-start(f32[832,448]{0,1:T(8,128)} %param.9) | copy-start | bytes 4472836
  38.9 5.4 %copy-start.4 = (f32[832,448]{0,1:T(8,128)S(1)}, f32[832,448]{0,1:T(8,128)}, u32[]{:S(2)}) copy-start(f32[832,448]{0,1:T(8,128)} %param.11) | copy-start | bytes 4472836
  38.9 5.4 %copy-start.5 = (f32[832,448]{0,1:T(8,128)S(1)}, f32[832,448]{0,1:T(8,128)}, u32[]{:S(2)}) copy-start(f32[832,448]{0,1:T(8,128)} %param.10) | copy-start | bytes 4472836
  40.7 1.5 %collective-permute-start.16 = (bf16[416,256]{1,0:T(8,128)(2,1)S(1)}, bf16[416,256]{1,0:T(8,128)(2,1)S(1)}, u32[]{:S(2)}, u32[]{:S(2)}) collective-permute-start(bf16[416,256]{1,0:T(8,128)(2,1)S(1)} %collective-permute-done.12.refs_4_), channel_id=1, source_target_pairs={{0,1},{1,0},{2,3},{3,2},{4,5},{5,4},{6,7},{7,6},{8,9},{9,8},{10,11... | collective-permute-start | bytes 638984 | tf_op jit(solution)/shard_map/ppermute | solution.py:214
  42.1 1.5 %collective-permute-start.17 = (bf16[416,256]{1,0:T(8,128)(2,1)S(1)}, bf16[416,256]{1,0:T(8,128)(2,1)S(1)}, u32[]{:S(2)}, u32[]{:S(2)}) collective-permute-start(bf16[416,256]{1,0:T(8,128)(2,1)S(1)} %collective-permute-done.13.refs_5_), channel_id=1, source_target_pairs={{0,1},{1,0},{2,3},{3,2},{4,5},{5,4},{6,7},{7,6},{8,9},{9,8},{10,11... | collective-permute-start | bytes 638984 | tf_op jit(solution)/shard_map/ppermute | solution.py:214
  44.9 8.5 %collective-permute-start.20 = (f16[448,256]{1,0:T(8,128)(2,1)S(1)}, f16[448,256]{1,0:T(8,128)(2,1)S(1)}, u32[]{:S(2)}, u32[]{:S(2)}) collective-permute-start(f16[448,256]{1,0:T(8,128)(2,1)S(1)} %fusion.15), channel_id=1, source_target_pairs={{0,16},{16,0},{1,17},{17,1},{2,18},{18,2},{3,19},{19,3},{4,20},{20... | collective-permute-start | bytes 688136 | tf_op jit(solution)/shard_map/ppermute | solution.py:197
  47.8 10.5 %collective-permute-start.19 = (f16[448,256]{1,0:T(8,128)(2,1)S(1)}, f16[448,256]{1,0:T(8,128)(2,1)S(1)}, u32[]{:S(2)}, u32[]{:S(2)}) collective-permute-start(f16[448,256]{1,0:T(8,128)(2,1)S(1)} %fusion.23), channel_id=1, source_target_pairs={{0,16},{16,0},{1,17},{17,1},{2,18},{18,2},{3,19},{19,3},{4,20},{20... | collective-permute-start | bytes 688136 | tf_op jit(solution)/shard_map/ppermute | solution.py:197
  49.4 8.9 %copy-start.6 = (f32[832,448]{0,1:T(8,128)S(1)}, f32[832,448]{0,1:T(8,128)}, u32[]{:S(2)}) copy-start(f32[832,448]{0,1:T(8,128)} %param.13) | copy-start | bytes 4472836
  50.4 14.5 %collective-permute-start.18 = (f16[448,320]{1,0:T(8,128)(2,1)S(1)}, f16[448,320]{1,0:T(8,128)(2,1)S(1)}, u32[]{:S(2)}, u32[]{:S(2)}) collective-permute-start(f16[448,320]{1,0:T(8,128)(2,1)S(1)} %fusion.1), channel_id=1, source_target_pairs={{0,16},{16,0},{1,17},{17,1},{2,18},{18,2},{3,19},{19,3},{4,20},{20... | collective-permute-start | bytes 860168 | tf_op jit(solution)/shard_map/ppermute | solution.py:197

commit v4 on v3

--- a/solution.py
+++ b/solution.py
@@ -39,7 +39,8 @@
 
 def feature_cuts(features):
     tiles = features // LANES
-    return [0, tiles // 3 * LANES, 2 * (tiles // 3) * LANES, features]
+    return [0, tiles // 3 * LANES, (tiles - 1) * LANES, features]
+
 
 def in_vmem(limit):
     return pltpu.CompilerParams(vmem_limit_bytes=limit)
@@ -187,16 +188,31 @@
     own, mine = activations.T, out_grad.T
     weights, one, two = master_weights.T, first_moment.T, second_moment.T
     anchor, momentum = anchor.T, outer_momentum.T
-    cuts = feature_cuts(own.shape[0])
+    features = own.shape[0]
+    cuts = feature_cuts(features)
     spans = list(zip(cuts[:-1], cuts[1:]))
 
-    def other_groups_sum(value):
-        total = None
-        for hop in range(1, groups):
-            there = [(g, (g + hop) % groups) for g in range(groups)]
-            came = lax.ppermute(value, "replica", there).astype(jnp.float32)
-            total = came if total is None else total + came
-        return total
+    def across(value):
+        if groups != 2:
+            return lax.psum(value.astype(jnp.float32), "replica")
+        return lax.ppermute(value, "replica", [(0, 1), (1, 0)]).astype(jnp.float32)
+
+    def total(value, came):
+        return value + came if groups == 2 else came
+
+    def across_packed(value):
+        rows, count = value.shape
+        spare = count % LANES
+        if groups != 2 or 2 * spare != LANES or rows % 32:
+            return across(value)
+        tiles = [value[:, at : at + LANES] for at in range(0, count - spare, LANES)]
+        rest = value[:, count - spare :]
+        tiles.append(jnp.concatenate([rest[: rows // 2], rest[rows // 2 :]], axis=1))
+        other = across(jnp.concatenate(tiles))
+        parts = [other[at * rows : (at + 1) * rows] for at in range(len(tiles) - 1)]
+        rest = other[(len(tiles) - 1) * rows :]
+        parts.append(jnp.concatenate([rest[:, :spare], rest[:, spare:]]))
+        return jnp.concatenate(parts, axis=1)
 
     def behind(value, *boxes):
         if not boxes:
@@ -207,53 +223,48 @@
         return value
 
     def send(blocks, *boxes):
-        blocks = [behind(b, *boxes) for b in blocks] if boxes else blocks
+        blocks = [behind(b, *boxes) for b in blocks]
         return [lax.ppermute(b, "tensor", pairs[hop]) for b, hop in zip(blocks, (1, -1))]
 
-    def to_other_core(blocks, *boxes):
-        return [lax.ppermute(behind(b, *boxes) if boxes else b, "tensor", swap) for b in blocks]
-
-    def with_other(mine, theirs):
-        return [(b, 0, 1) for b in mine + theirs]
-
-
-    features = own.shape[0]
+    def with_other_core(blocks, *boxes):
+        return blocks + [lax.ppermute(behind(b, *boxes), "tensor", swap) for b in blocks]
+
+    def whole(blocks):
+        return [(b, 0, 1) for b in blocks]
+
     first = send([own, own])
     early = start_to_half(anchor, weights)[1]
-    early16 = [early.astype(jnp.float16)]
-    early_others = [other_groups_sum(early16[0])]
+    early_came = [across(early.astype(jnp.float16))]
     grad = sort_tokens(behind(mine, [first[0]]), chips)
-    came = [with_other([own], to_other_core([own])), with_other(first, to_other_core(first))]
-    head = sum(came, [])
-    sums = [gradient_part(0, features, 0, grad, head)]
-    newest = first
-    middle = []
+    head = whole(with_other_core([own]) + with_other_core(first))
+    head_sum = [gradient_part(0, features, 0, grad, head)]
+    newest, middle = first, []
     for step in range(2, half - 1):
         newest = send(newest)
-        middle += with_other(newest, to_other_core(newest))
+        middle += whole(with_other_core(newest))
     newest = send(newest)
     top = features // 2
-    final = send([newest[0][:top], newest[1][top:]], *[early_others, sums])
-    theirs = to_other_core(newest)
-    sums2 = [gradient_part(0, features, len(head), grad, middle, (sums[0],))]
+    opposite = send([newest[0][:top], newest[1][top:]], early_came, head_sum)
+    third = whole(with_other_core(newest))
+    so_far = [gradient_part(0, features, len(head), grad, middle, (head_sum[0],))]
     skip = len(head) + len(middle)
-    theirs_final = to_other_core(final, *[sums2])
-    tail = with_other(newest, theirs) + [(final[0], 0, 0), (final[1], top, 1), (theirs_final[0], 0, 0), (theirs_final[1], top, 1)]
-    so_far = (sums2[0],)
-    outs = ()
-    rest = []
+    ends = [(0, 0), (top, 1)] * CORES
+    tail = third + [(b, *end) for b, end in zip(with_other_core(opposite, so_far), ends)]
+
+    lates, came, outs = [], [], ()
     for low, high in spans:
-        tied = [behind(b[0], *rest) for b in tail]
-        tail = [(t, *b[1:]) for t, b in zip(tied, tail)]
-        gradient = gradient_part(low, high, skip, grad, tail, so_far)
+        ties = lates[-1:] + came[-2:-1]
+        tail = [(behind(b[0], *ties), *b[1:]) for b in tail]
+        gradient = gradient_part(low, high, skip, grad, tail, (so_far[0],))
+        late = late_part(gradient, *[x[:, low:high] for x in (one, two, weights, anchor)])
+        lates.append([late])
+        came.append([across_packed(late)])
+    for (low, high), (late,), (other,) in zip(spans, lates, came):
         here = lambda x: x[:, low:high]
-        late = late_part(gradient, *map(here, (one, two, weights, anchor)))
-        late_others = other_groups_sum(late)
-        rest = [[late]] if True else []
-        mean = ((here(early) + here(early_others[0])) + (late.astype(jnp.float32) + late_others)) / groups
+        mean = (total(here(early), here(early_came[0])) + total(late.astype(jnp.float32), other)) / groups
         moved = NESTEROV * here(momentum) + mean
         weight = here(anchor) - OUTER_RATE * (mean + NESTEROV * moved)
-        outs = place(low, cuts[-1], (weight.astype(jnp.bfloat16), moved), outs)
+        outs = place(low, features, (weight.astype(jnp.bfloat16), moved), outs)
     rebuilt, new_momentum = outs
     return rebuilt.T, new_momentum.T
 

time: 66.3 us -> 65.1 us (0.982)
  waiting for transfers between devices: 33.6 us -> 31.8 us
    ppermute x13, waiting for transfers between devices: 12.3 us -> 10.5 us  [the longest x4 9.04 us: across(): return lax.ppermute(value, 'replica', [(0, 1), (1, 0)]).astype(jnp.float32)]
    convert_element_type x3 -> x6, other arithmetic: 3.31 us -> 3.22 us  [the longest x1 2.82 us: on_device(): early_came = [across(early.astype(jnp.float16))]]
  transfers between devices with their start and end apart: 21 -> 21, of which waited for: 9 -> 9; matrix products, arithmetic and copies ran while one was open for 7% -> 8% of each run, Pallas kernels for 12% -> 12%
where the time goes in v4:
time: 65.1 us; the launch traced here: 65 us
  waiting for transfers between devices  31.8 us (49%)
  starting transfers between devices  16.6 us (25%)
  Pallas kernels  9.4 us (14%)
  other arithmetic  6.12 us (9%)
  between operations  0.88 us (1%)
    ppermute x8, waiting for transfers between devices, send(): lax.ppermute(b, 'tensor', pairs[hop])  21.3 us
    ppermute x8, starting transfers between devices, send(): lax.ppermute(b, 'tensor', pairs[hop])  9.26 us
    ppermute x4, waiting for transfers between devices, across(): return lax.ppermute(value, 'replica', [(0, 1), (1, 0)]).astype(jnp.float32)  9.04 us
    ppermute x4, starting transfers between devices, across(): return lax.ppermute(value, 'replica', [(0, 1), (1, 0)]).astype(jnp.float32)  5.77 us
    pallas_call x5, Pallas kernels, gradient_part(): pl.pallas_call(functools.partial(gradient_kernel, low, skip, [b[1:] for b...  5.77 us
    convert_element_type x1, other arithmetic, on_device(): early_came = [across(early.astype(jnp.float16))]  2.82 us
    pallas_call x3, Pallas kernels, place(): pl.pallas_call(functools.partial(place_kernel, low), out_shape=tuple((jax...  2.71 us
    convert_element_type x3, other arithmetic, late_part(): return (exact - half + INNER_RATE * step).astype(jnp.float16)  2.14 us
  transfers between devices with their start and end apart: 21, of which 9 were waited for; matrix products, arithmetic and copies ran while one was open for 8% of the time, Pallas kernels for 12%

profile of v4, /device:TPU:0, one launch (start us, length us, event | category | flops | bytes accessed | tf_op | source)
XLA Modules:
  0.0 65.0 jit_solution(6619080370331005347)
XLA Ops:
  0.6 3.1 %collective-permute-start.3 = (bf16[832,256]{1,0:T(8,128)(2,1)}, bf16[832,256]{1,0:T(8,128)(2,1)S(1)}, u32[]{:S(2)}, u32[]{:S(2)}) collective-permute-start(bf16[832,256]{1,0:T(8,128)(2,1)} %bitcast.14), channel_id=1, source_target_pairs={{0,4},{1,5},{4,8},{5,9},{8,12},{9,13},{12,14},{13,15},{14,10},{15,... | collective-permute-start | bytes 1277960 | tf_op jit(solution)/shard_map/ppermute | solution.py:227
  3.7 2.8 %fusion.44 = (f16[448,832]{1,0:T(8,128)(2,1)S(1)}, f32[448,832]{1,0:T(8,128)S(1)}) fusion(f32[832,448]{0,1:T(8,128)} %param.9, f32[832,448]{0,1:T(8,128)} %param.12), kind=kLoop, calls=%fused_computation.69 | loop fusion | flops 1490944 | bytes 5218304 | tf_op jit(solution)/shard_map/convert_element_type | solution.py:237
  6.5 2.0 %collective-permute-start.6 = (f16[448,832]{1,0:T(8,128)(2,1)S(1)}, f16[448,832]{1,0:T(8,128)(2,1)S(1)}, u32[]{:S(2)}, u32[]{:S(2)}) collective-permute-start(f16[448,832]{1,0:T(8,128)(2,1)S(1)} %get-tuple-element.120), channel_id=1, source_target_pairs={{0,16},{16,0},{1,17},{17,1},{2,18},{18,2},{3,19},{19,3},{4,20},{20... | collective-permute-start | bytes 2236424 | tf_op jit(solution)/shard_map/ppermute | solution.py:198
  8.6 5.1 %collective-permute-done.3.refs_2_ = bf16[832,256]{1,0:T(8,128)(2,1)S(1)} collective-permute-done((bf16[832,256]{1,0:T(8,128)(2,1)}, bf16[832,256]{1,0:T(8,128)(2,1)S(1)}, u32[]{:S(2)}, u32[]{:S(2)}) %collective-permute-start.3) | collective-permute-done | bytes 426016 | tf_op jit(solution)/shard_map/ppermute | solution.py:227
  13.7 1.8 %collective-permute-start.4 = (bf16[832,256]{1,0:T(8,128)(2,1)S(1)}, bf16[832,256]{1,0:T(8,128)(2,1)S(1)}, u32[]{:S(2)}, u32[]{:S(2)}) collective-permute-start(bf16[832,256]{1,0:T(8,128)(2,1)S(1)} %collective-permute-done.3.refs_2_), channel_id=1, source_target_pairs={{0,4},{1,5},{4,8},{5,9},{8,12},{9,13},{12,14},{13,15},{14,10},{15,... | collective-permute-start | bytes 1277960 | tf_op jit(solution)/shard_map/ppermute | solution.py:227
  15.5 0.2 collective-permute-start.1
  15.7 0.5 collective-permute-start.9
  16.2 8.5 %collective-permute-done.4.refs_0_ = bf16[832,256]{1,0:T(8,128)(2,1)S(1)} collective-permute-done((bf16[832,256]{1,0:T(8,128)(2,1)S(1)}, bf16[832,256]{1,0:T(8,128)(2,1)S(1)}, u32[]{:S(2)}, u32[]{:S(2)}) %collective-permute-start.4) | collective-permute-done | bytes 426016 | tf_op jit(solution)/shard_map/ppermute | solution.py:227
  24.7 1.5 %collective-permute-start.5 = (bf16[832,256]{1,0:T(8,128)(2,1)S(1)}, bf16[832,256]{1,0:T(8,128)(2,1)S(1)}, u32[]{:S(2)}, u32[]{:S(2)}) collective-permute-start(bf16[832,256]{1,0:T(8,128)(2,1)S(1)} %collective-permute-done.4.refs_0_), channel_id=1, source_target_pairs={{0,4},{1,5},{4,8},{5,9},{8,12},{9,13},{12,14},{13,15},{14,10},{15,... | collective-permute-start | bytes 1277960 | tf_op jit(solution)/shard_map/ppermute | solution.py:227
  26.2 0.5 collective-permute-start.2
  26.7 0.5 collective-permute-start.15
  27.2 0.9 %sort_tokens.1.grad_ref = bf16[448,4096]{1,0:T(8,128)(2,1)S(1)} custom-call(bf16[448,4096]{1,0:T(8,128)(2,1)S(1)} %bitcast.13), custom_call_target="tpu_custom_call" | custom-call | bytes 7340032 | tf_op jit(solution)/shard_map/sort_tokens/pallas_call | solution.py:74
  28.1 0.1 convert_element_type.43
  28.3 1.9 %gradient.5.refs_4_ = f32[448,832]{1,0:T(8,128)S(1)} custom-call(bf16[448,4096]{1,0:T(8,128)(2,1)S(1)} %sort_tokens.1.grad_ref, bf16[832,256]{1,0:T(8,128)(2,1)S(1)} %bitcast.17, bf16[832,256]{1,0:T(8,128)(2,1)S(1)} %collective-permute-done.7.refs_1_, bf16[832,256]{1,0:T(8,128)(2,1)S(1)} %collective-permute-done.3.refs_2_, ...), custom_call_target="tpu_custom_call" | custom-call | flops 1145044992 | bytes 2981888 | tf_op jit(solution)/shard_map/gradient/pallas_call | solution.py:147
  30.2 4.6 %collective-permute-done.5.refs_0_ = bf16[832,256]{1,0:T(8,128)(2,1)S(1)} collective-permute-done((bf16[832,256]{1,0:T(8,128)(2,1)S(1)}, bf16[832,256]{1,0:T(8,128)(2,1)S(1)}, u32[]{:S(2)}, u32[]{:S(2)}) %collective-permute-start.5) | collective-permute-done | bytes 426016 | tf_op jit(solution)/shard_map/ppermute | solution.py:227
  34.8 1.4 %collective-permute-start.12 = (bf16[416,256]{1,0:T(8,128)(2,1)S(1)}, bf16[416,256]{1,0:T(8,128)(2,1)S(1)}, u32[]{:S(2)}, u32[]{:S(2)}) collective-permute-start(bf16[416,256]{1,0:T(8,128)(2,1)S(1)} %slice.128), channel_id=1, source_target_pairs={{0,4},{1,5},{4,8},{5,9},{8,12},{9,13},{12,14},{13,15},{14,10},{15,... | collective-permute-start | bytes 638984 | tf_op jit(solution)/shard_map/ppermute | solution.py:227
  36.2 0.7 %collective-permute-start.13 = (bf16[416,256]{1,0:T(8,128)(2,1)S(1)}, bf16[416,256]{1,0:T(8,128)(2,1)S(1)}, u32[]{:S(2)}, u32[]{:S(2)}) collective-permute-start(bf16[416,256]{1,0:T(8,128)(2,1)S(1)} %slice.127), channel_id=1, source_target_pairs={{0,2},{1,3},{4,0},{5,1},{8,4},{9,5},{12,8},{13,9},{14,12},{15,13},... | collective-permute-start | bytes 638984 | tf_op jit(solution)/shard_map/ppermute | solution.py:227
  36.9 0.5 collective-permute-start.11
  37.4 1.4 %gradient.6.refs_8_ = f32[448,832]{1,0:T(8,128)S(1)} custom-call(bf16[448,4096]{1,0:T(8,128)(2,1)S(1)} %sort_tokens.1.grad_ref, bf16[832,256]{1,0:T(8,128)(2,1)S(1)} %collective-permute-done.4.refs_0_, bf16[832,256]{1,0:T(8,128)(2,1)S(1)} %collective-permute-done.1.refs_1_, bf16[832,256]{1,0:T(8,128)(2,1)S(1)} %collective-permute-done.14.refs_2_, ...), custom_call_target="tpu_custom_call" | custom-call | flops 763363328 | bytes 2981888 | tf_op jit(solution)/shard_map/gradient/pallas_call | solution.py:147
  38.9 0.0 copy-start.2
  38.9 0.0 copy-start.3
  38.9 0.0 copy-start.5
  38.9 1.7 %collective-permute-done.12.refs_4_ = bf16[416,256]{1,0:T(8,128)(2,1)S(1)} collective-permute-done((bf16[416,256]{1,0:T(8,128)(2,1)S(1)}, bf16[416,256]{1,0:T(8,128)(2,1)S(1)}, u32[]{:S(2)}, u32[]{:S(2)}) %collective-permute-start.12) | collective-permute-done | bytes 213024 | tf_op jit(solution)/shard_map/ppermute | solution.py:227
  40.7 1.4 %collective-permute-done.13.refs_5_ = bf16[416,256]{1,0:T(8,128)(2,1)S(1)} collective-permute-done((bf16[416,256]{1,0:T(8,128)(2,1)S(1)}, bf16[416,256]{1,0:T(8,128)(2,1)S(1)}, u32[]{:S(2)}, u32[]{:S(2)}) %collective-permute-start.13) | collective-permute-done | bytes 213024 | tf_op jit(solution)/shard_map/ppermute | solution.py:227
  42.1 0.0 collective-permute-done.16.refs_6_
  42.1 1.4 %collective-permute-done.17.refs_7_ = bf16[416,256]{1,0:T(8,128)(2,1)S(1)} collective-permute-done((bf16[416,256]{1,0:T(8,128)(2,1)S(1)}, bf16[416,256]{1,0:T(8,128)(2,1)S(1)}, u32[]{:S(2)}, u32[]{:S(2)}) %collective-permute-start.17) | collective-permute-done | bytes 213024 | tf_op jit(solution)/shard_map/ppermute | solution.py:230
  43.5 0.7 %gradient.7 = f32[448,256]{1,0:T(8,128)S(1)} custom-call(bf16[448,4096]{1,0:T(8,128)(2,1)S(1)} %sort_tokens.1.grad_ref, bf16[832,256]{1,0:T(8,128)(2,1)S(1)} %collective-permute-done.5.refs_0_, bf16[832,256]{1,0:T(8,128)(2,1)S(1)} %collective-permute-done.2.refs_1_, bf16[832,256]{1,0:T(8,128)(2,1)S(1)} %collective-permute-done.10.refs_2_, ...), custom_call_target="tpu_custom_call" | custom-call | flops 352321536 | bytes 917504 | tf_op jit(solution)/shard_map/gradient/pallas_call | solution.py:147
  44.3 0.6 fusion.17
  44.9 1.6 %collective-permute-start.18 = (f16[448,256]{1,0:T(8,128)(2,1)S(1)}, f16[448,256]{1,0:T(8,128)(2,1)S(1)}, u32[]{:S(2)}, u32[]{:S(2)}) collective-permute-start(f16[448,256]{1,0:T(8,128)(2,1)S(1)} %fusion.17), channel_id=1, source_target_pairs={{0,16},{16,0},{1,17},{17,1},{2,18},{18,2},{3,19},{19,3},{4,20},{20... | collective-permute-start | bytes 688136 | tf_op jit(solution)/shard_map/ppermute | solution.py:198
  46.5 1.1 %gradient.8 = f32[448,384]{1,0:T(8,128)S(1)} custom-call(bf16[448,4096]{1,0:T(8,128)(2,1)S(1)} %sort_tokens.1.grad_ref, bf16[832,256]{1,0:T(8,128)(2,1)S(1)} %collective-permute-done.5.refs_0_, bf16[832,256]{1,0:T(8,128)(2,1)S(1)} %collective-permute-done.2.refs_1_, bf16[832,256]{1,0:T(8,128)(2,1)S(1)} %collective-permute-done.10.refs_2_, ...), custom_call_target="tpu_custom_call" | custom-call | flops 528482304 | bytes 1376256 | tf_op jit(solution)/shard_map/gradient/pallas_call | solution.py:147
  47.6 0.9 %fusion.1 = f16[448,384]{1,0:T(8,128)(2,1)S(1)} fusion(f32[448,384]{1,0:T(8,128)S(1)} %gradient.8, f32[448,832]{1,0:T(8,128)S(1)} %bitcast.35, f32[448,832]{1,0:T(8,128)S(1)} %bitcast.38, f32[448,832]{1,0:T(8,128)S(1)} %bitcast.25, f32[448,832]{1,0:T(8,128)S(1)} %bitcast.19), kind=kLoop, calls=%fused_computation.4 | loop fusion | flops 3096576 | bytes 3784704 | tf_op jit(solution)/shard_map/convert_element_type | solution.py:176
  48.5 0.6 collective-permute-start.20
  49.1 4.4 %collective-permute-done.18 = f16[448,256]{1,0:T(8,128)(2,1)S(1)} collective-permute-done((f16[448,256]{1,0:T(8,128)(2,1)S(1)}, f16[448,256]{1,0:T(8,128)(2,1)S(1)}, u32[]{:S(2)}, u32[]{:S(2)}) %collective-permute-start.18) | collective-permute-done | bytes 229408 | tf_op jit(solution)/shard_map/ppermute | solution.py:198
  53.5 0.7 %gradient.9 = f32[448,192]{1,0:T(8,128)S(1)} custom-call(bf16[448,4096]{1,0:T(8,128)(2,1)S(1)} %sort_tokens.1.grad_ref, bf16[832,256]{1,0:T(8,128)(2,1)S(1)} %collective-permute-done.5.refs_0_, bf16[832,256]{1,0:T(8,128)(2,1)S(1)} %collective-permute-done.2.refs_1_, bf16[832,256]{1,0:T(8,128)(2,1)S(1)} %collective-permute-done.10.refs_2_, ...), custom_call_target="tpu_custom_call" | custom-call | flops 264241152 | bytes 688128 | tf_op jit(solution)/shard_map/gradient/pallas_call | solution.py:147
  54.1 0.6 fusion.15
  54.8 0.1 maximum_maximum_fusion
  54.9 1.6 %collective-permute-start.19 = (f16[672,128]{1,0:T(8,128)(2,1)S(1)}, f16[672,128]{1,0:T(8,128)(2,1)S(1)}, u32[]{:S(2)}, u32[]{:S(2)}) collective-permute-start(f16[672,128]{1,0:T(8,128)(2,1)S(1)} %maximum_maximum_fusion), channel_id=1, source_target_pairs={{0,16},{16,0},{1,17},{17,1},{2,18},{18,2},{3,19},{19,3},{4,20},{20... | collective-permute-start | bytes 516104 | tf_op jit(solution)/shard_map/ppermute | solution.py:198
  56.5 0.1 fusion.30
  56.7 0.1 subtract_convert_fusion.1.refs_0_
  56.8 0.9 %place.3 = (bf16[448,832]{1,0:T(8,128)(2,1)}, f32[448,832]{1,0:T(8,128)}) custom-call(bf16[448,256]{1,0:T(8,128)(2,1)S(1)} %subtract_convert_fusion.1.refs_0_, f32[448,256]{1,0:T(8,128)S(1)} %get-tuple-element.116.refs_1_), custom_call_target="tpu_custom_call" | custom-call | bytes 1376256 | tf_op jit(solution)/shard_map/place/pallas_call | solution.py:99
  57.7 3.1 %collective-permute-done.20 = f16[448,384]{1,0:T(8,128)(2,1)S(1)} collective-permute-done((f16[448,384]{1,0:T(8,128)(2,1)S(1)}, f16[448,384]{1,0:T(8,128)(2,1)S(1)}, u32[]{:S(2)}, u32[]{:S(2)}) %collective-permute-start.20) | collective-permute-done | bytes 344096 | tf_op jit(solution)/shard_map/ppermute | solution.py:198
  60.8 0.3 fusion.8
  61.1 1.0 %place.4 = (bf16[448,832]{1,0:T(8,128)(2,1)}, f32[448,832]{1,0:T(8,128)}) custom-call(bf16[448,384]{1,0:T(8,128)(2,1)S(1)} %get-tuple-element.123.refs_0_, f32[448,384]{1,0:T(8,128)S(1)} %get-tuple-element.122.refs_1_, bf16[448,832]{1,0:T(8,128)(2,1)} %get-tuple-element.110.refs_2_, ...), custom_call_target="tpu_custom_call", output_to_operand_aliasing={{0}: (2, {}), {1}: (3, {})} | custom-call | bytes 2064384 | tf_op jit(solution)/shard_map/place/pallas_call | solution.py:99
  62.1 1.6 %collective-permute-done.19 = f16[672,128]{1,0:T(8,128)(2,1)S(1)} collective-permute-done((f16[672,128]{1,0:T(8,128)(2,1)S(1)}, f16[672,128]{1,0:T(8,128)(2,1)S(1)}, u32[]{:S(2)}, u32[]{:S(2)}) %collective-permute-start.19) | collective-permute-done | bytes 172064 | tf_op jit(solution)/shard_map/ppermute | solution.py:198
  63.7 0.1 fusion.45
  63.8 0.2 fusion.33
  64.0 0.1 subtract_convert_fusion.2.refs_0_
  64.1 0.9 %place.5 = (bf16[448,832]{1,0:T(8,128)(2,1)}, f32[448,832]{1,0:T(8,128)}) custom-call(bf16[448,192]{1,0:T(8,128)(2,1)S(1)} %subtract_convert_fusion.2.refs_0_, f32[448,192]{1,0:T(8,128)S(1)} %get-tuple-element.118.refs_1_, bf16[448,832]{1,0:T(8,128)(2,1)} %get-tuple-element.112.refs_2_, ...), custom_call_target="tpu_custom_call", output_to_operand_aliasing={{0}: (2, {}), {1}: (3, {})} | custom-call | bytes 1032192 | tf_op jit(solution)/shard_map/place/pallas_call | solution.py:99
  (36 shorter events, 0.2 us)
Async XLA Ops:
  0.6 8.0 %copy-start.1 = (bf16[256,832]{0,1:T(8,128)(2,1)S(1)}, bf16[256,832]{0,1:T(8,128)(2,1)}, u32[]{:S(2)}) copy-start(bf16[256,832]{0,1:T(8,128)(2,1)} %param.7) | copy-start | bytes 1277956
  0.6 26.6 %copy-start = (bf16[4096,448]{0,1:T(8,128)(2,1)S(1)}, bf16[4096,448]{0,1:T(8,128)(2,1)}, u32[]{:S(2)}) copy-start(bf16[4096,448]{0,1:T(8,128)(2,1)} %param.8) | copy-start | bytes 11010052
  0.6 13.0 %collective-permute-start.3 = (bf16[832,256]{1,0:T(8,128)(2,1)}, bf16[832,256]{1,0:T(8,128)(2,1)S(1)}, u32[]{:S(2)}, u32[]{:S(2)}) collective-permute-start(bf16[832,256]{1,0:T(8,128)(2,1)} %bitcast.14), channel_id=1, source_target_pairs={{0,4},{1,5},{4,8},{5,9},{8,12},{9,13},{12,14},{13,15},{14,10},{15,... | collective-permute-start | bytes 1277960 | tf_op jit(solution)/shard_map/ppermute | solution.py:227
  3.7 11.8 %collective-permute-start = (bf16[832,256]{1,0:T(8,128)(2,1)}, bf16[832,256]{1,0:T(8,128)(2,1)S(1)}, u32[]{:S(2)}, u32[]{:S(2)}) collective-permute-start(bf16[832,256]{1,0:T(8,128)(2,1)} %bitcast.15), channel_id=1, source_target_pairs={{0,2},{1,3},{4,0},{5,1},{8,4},{9,5},{12,8},{13,9},{14,12},{15,13},... | collective-permute-start | bytes 1277960 | tf_op jit(solution)/shard_map/ppermute | solution.py:227
  6.5 20.2 %collective-permute-start.6 = (f16[448,832]{1,0:T(8,128)(2,1)S(1)}, f16[448,832]{1,0:T(8,128)(2,1)S(1)}, u32[]{:S(2)}, u32[]{:S(2)}) collective-permute-start(f16[448,832]{1,0:T(8,128)(2,1)S(1)} %get-tuple-element.120), channel_id=1, source_target_pairs={{0,16},{16,0},{1,17},{17,1},{2,18},{18,2},{3,19},{19,3},{4,20},{20... | collective-permute-start | bytes 2236424 | tf_op jit(solution)/shard_map/ppermute | solution.py:198
  8.6 7.1 %collective-permute-start.7 = (bf16[832,256]{1,0:T(8,128)(2,1)S(1)}, bf16[832,256]{1,0:T(8,128)(2,1)S(1)}, u32[]{:S(2)}, u32[]{:S(2)}) collective-permute-start(bf16[832,256]{1,0:T(8,128)(2,1)S(1)} %bitcast.16), channel_id=1, source_target_pairs={{0,1},{1,0},{2,3},{3,2},{4,5},{5,4},{6,7},{7,6},{8,9},{9,8},{10,11... | collective-permute-start | bytes 1277960 | tf_op jit(solution)/shard_map/ppermute | solution.py:230
  13.7 11.0 %collective-permute-start.4 = (bf16[832,256]{1,0:T(8,128)(2,1)S(1)}, bf16[832,256]{1,0:T(8,128)(2,1)S(1)}, u32[]{:S(2)}, u32[]{:S(2)}) collective-permute-start(bf16[832,256]{1,0:T(8,128)(2,1)S(1)} %collective-permute-done.3.refs_2_), channel_id=1, source_target_pairs={{0,4},{1,5},{4,8},{5,9},{8,12},{9,13},{12,14},{13,15},{14,10},{15,... | collective-permute-start | bytes 1277960 | tf_op jit(solution)/shard_map/ppermute | solution.py:227
  15.5 10.7 %collective-permute-start.1 = (bf16[832,256]{1,0:T(8,128)(2,1)S(1)}, bf16[832,256]{1,0:T(8,128)(2,1)S(1)}, u32[]{:S(2)}, u32[]{:S(2)}) collective-permute-start(bf16[832,256]{1,0:T(8,128)(2,1)S(1)} %collective-permute-done.refs_3_), channel_id=1, source_target_pairs={{0,2},{1,3},{4,0},{5,1},{8,4},{9,5},{12,8},{13,9},{14,12},{15,13},... | collective-permute-start | bytes 1277960 | tf_op jit(solution)/shard_map/ppermute | solution.py:227
  15.7 11.0 %collective-permute-start.8 = (bf16[832,256]{1,0:T(8,128)(2,1)S(1)}, bf16[832,256]{1,0:T(8,128)(2,1)S(1)}, u32[]{:S(2)}, u32[]{:S(2)}) collective-permute-start(bf16[832,256]{1,0:T(8,128)(2,1)S(1)} %collective-permute-done.3.refs_2_), channel_id=1, source_target_pairs={{0,1},{1,0},{2,3},{3,2},{4,5},{5,4},{6,7},{7,6},{8,9},{9,8},{10,11... | collective-permute-start | bytes 1277960 | tf_op jit(solution)/shard_map/ppermute | solution.py:230
  15.7 12.6 %collective-permute-start.9 = (bf16[832,256]{1,0:T(8,128)(2,1)S(1)}, bf16[832,256]{1,0:T(8,128)(2,1)S(1)}, u32[]{:S(2)}, u32[]{:S(2)}) collective-permute-start(bf16[832,256]{1,0:T(8,128)(2,1)S(1)} %collective-permute-done.refs_3_), channel_id=1, source_target_pairs={{0,1},{1,0},{2,3},{3,2},{4,5},{5,4},{6,7},{7,6},{8,9},{9,8},{10,11... | collective-permute-start | bytes 1277960 | tf_op jit(solution)/shard_map/ppermute | solution.py:230
  24.7 10.1 %collective-permute-start.5 = (bf16[832,256]{1,0:T(8,128)(2,1)S(1)}, bf16[832,256]{1,0:T(8,128)(2,1)S(1)}, u32[]{:S(2)}, u32[]{:S(2)}) collective-permute-start(bf16[832,256]{1,0:T(8,128)(2,1)S(1)} %collective-permute-done.4.refs_0_), channel_id=1, source_target_pairs={{0,4},{1,5},{4,8},{5,9},{8,12},{9,13},{12,14},{13,15},{14,10},{15,... | collective-permute-start | bytes 1277960 | tf_op jit(solution)/shard_map/ppermute | solution.py:227
  26.2 10.0 %collective-permute-start.2 = (bf16[832,256]{1,0:T(8,128)(2,1)S(1)}, bf16[832,256]{1,0:T(8,128)(2,1)S(1)}, u32[]{:S(2)}, u32[]{:S(2)}) collective-permute-start(bf16[832,256]{1,0:T(8,128)(2,1)S(1)} %collective-permute-done.1.refs_1_), channel_id=1, source_target_pairs={{0,2},{1,3},{4,0},{5,1},{8,4},{9,5},{12,8},{13,9},{14,12},{15,13},... | collective-permute-start | bytes 1277960 | tf_op jit(solution)/shard_map/ppermute | solution.py:227
  26.7 10.2 %collective-permute-start.14 = (bf16[832,256]{1,0:T(8,128)(2,1)S(1)}, bf16[832,256]{1,0:T(8,128)(2,1)S(1)}, u32[]{:S(2)}, u32[]{:S(2)}) collective-permute-start(bf16[832,256]{1,0:T(8,128)(2,1)S(1)} %collective-permute-done.4.refs_0_), channel_id=1, source_target_pairs={{0,1},{1,0},{2,3},{3,2},{4,5},{5,4},{6,7},{7,6},{8,9},{9,8},{10,11... | collective-permute-start | bytes 1277960 | tf_op jit(solution)/shard_map/ppermute | solution.py:230
  26.7 10.7 %collective-permute-start.15 = (bf16[832,256]{1,0:T(8,128)(2,1)S(1)}, bf16[832,256]{1,0:T(8,128)(2,1)S(1)}, u32[]{:S(2)}, u32[]{:S(2)}) collective-permute-start(bf16[832,256]{1,0:T(8,128)(2,1)S(1)} %collective-permute-done.1.refs_1_), channel_id=1, source_target_pairs={{0,1},{1,0},{2,3},{3,2},{4,5},{5,4},{6,7},{7,6},{8,9},{9,8},{10,11... | collective-permute-start | bytes 1277960 | tf_op jit(solution)/shard_map/ppermute | solution.py:230
  34.8 5.9 %collective-permute-start.12 = (bf16[416,256]{1,0:T(8,128)(2,1)S(1)}, bf16[416,256]{1,0:T(8,128)(2,1)S(1)}, u32[]{:S(2)}, u32[]{:S(2)}) collective-permute-start(bf16[416,256]{1,0:T(8,128)(2,1)S(1)} %slice.128), channel_id=1, source_target_pairs={{0,4},{1,5},{4,8},{5,9},{8,12},{9,13},{12,14},{13,15},{14,10},{15,... | collective-permute-start | bytes 638984 | tf_op jit(solution)/shard_map/ppermute | solution.py:227
  36.2 5.9 %collective-permute-start.13 = (bf16[416,256]{1,0:T(8,128)(2,1)S(1)}, bf16[416,256]{1,0:T(8,128)(2,1)S(1)}, u32[]{:S(2)}, u32[]{:S(2)}) collective-permute-start(bf16[416,256]{1,0:T(8,128)(2,1)S(1)} %slice.127), channel_id=1, source_target_pairs={{0,2},{1,3},{4,0},{5,1},{8,4},{9,5},{12,8},{13,9},{14,12},{15,13},... | collective-permute-start | bytes 638984 | tf_op jit(solution)/shard_map/ppermute | solution.py:227
  36.9 5.2 %collective-permute-start.10 = (bf16[832,256]{1,0:T(8,128)(2,1)S(1)}, bf16[832,256]{1,0:T(8,128)(2,1)S(1)}, u32[]{:S(2)}, u32[]{:S(2)}) collective-permute-start(bf16[832,256]{1,0:T(8,128)(2,1)S(1)} %collective-permute-done.5.refs_0_), channel_id=1, source_target_pairs={{0,1},{1,0},{2,3},{3,2},{4,5},{5,4},{6,7},{7,6},{8,9},{9,8},{10,11... | collective-permute-start | bytes 1277960 | tf_op jit(solution)/shard_map/ppermute | solution.py:230
  36.9 5.2 %collective-permute-start.11 = (bf16[832,256]{1,0:T(8,128)(2,1)S(1)}, bf16[832,256]{1,0:T(8,128)(2,1)S(1)}, u32[]{:S(2)}, u32[]{:S(2)}) collective-permute-start(bf16[832,256]{1,0:T(8,128)(2,1)S(1)} %collective-permute-done.2.refs_1_), channel_id=1, source_target_pairs={{0,1},{1,0},{2,3},{3,2},{4,5},{5,4},{6,7},{7,6},{8,9},{9,8},{10,11... | collective-permute-start | bytes 1277960 | tf_op jit(solution)/shard_map/ppermute | solution.py:230
  38.9 5.4 %copy-start.2 = (f32[832,448]{0,1:T(8,128)S(1)}, f32[832,448]{0,1:T(8,128)}, u32[]{:S(2)}) copy-start(f32[832,448]{0,1:T(8,128)} %param.12) | copy-start | bytes 4472836
  38.9 5.4 %copy-start.3 = (f32[832,448]{0,1:T(8,128)S(1)}, f32[832,448]{0,1:T(8,128)}, u32[]{:S(2)}) copy-start(f32[832,448]{0,1:T(8,128)} %param.9) | copy-start | bytes 4472836
  38.9 5.4 %copy-start.5 = (f32[832,448]{0,1:T(8,128)S(1)}, f32[832,448]{0,1:T(8,128)}, u32[]{:S(2)}) copy-start(f32[832,448]{0,1:T(8,128)} %param.11) | copy-start | bytes 4472836
  38.9 5.4 %copy-start.6 = (f32[832,448]{0,1:T(8,128)S(1)}, f32[832,448]{0,1:T(8,128)}, u32[]{:S(2)}) copy-start(f32[832,448]{0,1:T(8,128)} %param.10) | copy-start | bytes 4472836
  40.7 1.5 %collective-permute-start.16 = (bf16[416,256]{1,0:T(8,128)(2,1)S(1)}, bf16[416,256]{1,0:T(8,128)(2,1)S(1)}, u32[]{:S(2)}, u32[]{:S(2)}) collective-permute-start(bf16[416,256]{1,0:T(8,128)(2,1)S(1)} %collective-permute-done.12.refs_4_), channel_id=1, source_target_pairs={{0,1},{1,0},{2,3},{3,2},{4,5},{5,4},{6,7},{7,6},{8,9},{9,8},{10,11... | collective-permute-start | bytes 638984 | tf_op jit(solution)/shard_map/ppermute | solution.py:230
  42.1 1.5 %collective-permute-start.17 = (bf16[416,256]{1,0:T(8,128)(2,1)S(1)}, bf16[416,256]{1,0:T(8,128)(2,1)S(1)}, u32[]{:S(2)}, u32[]{:S(2)}) collective-permute-start(bf16[416,256]{1,0:T(8,128)(2,1)S(1)} %collective-permute-done.13.refs_5_), channel_id=1, source_target_pairs={{0,1},{1,0},{2,3},{3,2},{4,5},{5,4},{6,7},{7,6},{8,9},{9,8},{10,11... | collective-permute-start | bytes 638984 | tf_op jit(solution)/shard_map/ppermute | solution.py:230
  44.9 8.5 %collective-permute-start.18 = (f16[448,256]{1,0:T(8,128)(2,1)S(1)}, f16[448,256]{1,0:T(8,128)(2,1)S(1)}, u32[]{:S(2)}, u32[]{:S(2)}) collective-permute-start(f16[448,256]{1,0:T(8,128)(2,1)S(1)} %fusion.17), channel_id=1, source_target_pairs={{0,16},{16,0},{1,17},{17,1},{2,18},{18,2},{3,19},{19,3},{4,20},{20... | collective-permute-start | bytes 688136 | tf_op jit(solution)/shard_map/ppermute | solution.py:198
  48.5 12.3 %collective-permute-start.20 = (f16[448,384]{1,0:T(8,128)(2,1)S(1)}, f16[448,384]{1,0:T(8,128)(2,1)S(1)}, u32[]{:S(2)}, u32[]{:S(2)}) collective-permute-start(f16[448,384]{1,0:T(8,128)(2,1)S(1)} %fusion.1), channel_id=1, source_target_pairs={{0,16},{16,0},{1,17},{17,1},{2,18},{18,2},{3,19},{19,3},{4,20},{20... | collective-permute-start | bytes 1032200 | tf_op jit(solution)/shard_map/ppermute | solution.py:198
  54.1 2.4 %copy-start.4 = (f32[832,448]{0,1:T(8,128)S(1)}, f32[832,448]{0,1:T(8,128)}, u32[]{:S(2)}) copy-start(f32[832,448]{0,1:T(8,128)} %param.13) | copy-start | bytes 4472836
  54.9 8.7 %collective-permute-start.19 = (f16[672,128]{1,0:T(8,128)(2,1)S(1)}, f16[672,128]{1,0:T(8,128)(2,1)S(1)}, u32[]{:S(2)}, u32[]{:S(2)}) collective-permute-start(f16[672,128]{1,0:T(8,128)(2,1)S(1)} %maximum_maximum_fusion), channel_id=1, source_target_pairs={{0,16},{16,0},{1,17},{17,1},{2,18},{18,2},{3,19},{19,3},{4,20},{20... | collective-permute-start | bytes 516104 | tf_op jit(solution)/shard_map/ppermute | solution.py:198

commit v5 on v4

--- a/solution.py
+++ b/solution.py
@@ -235,7 +235,7 @@
     first = send([own, own])
     early = start_to_half(anchor, weights)[1]
     early_came = [across(early.astype(jnp.float16))]
-    grad = sort_tokens(behind(mine, [first[0]]), chips)
+    grad = sort_tokens(mine, chips)
     head = whole(with_other_core([own]) + with_other_core(first))
     head_sum = [gradient_part(0, features, 0, grad, head)]
     newest, middle = first, []

time: 65.1 us -> 65.1 us (level)
  no operation moved by 1% of the time
where the time goes in v5:
time: 65.1 us; the launch traced here: 65 us
  waiting for transfers between devices  31.8 us (49%)
  starting transfers between devices  16.6 us (25%)
  Pallas kernels  9.4 us (14%)
  other arithmetic  6.12 us (9%)
  between operations  0.88 us (1%)
    ppermute x8, waiting for transfers between devices, send(): lax.ppermute(b, 'tensor', pairs[hop])  21.3 us
    ppermute x8, starting transfers between devices, send(): lax.ppermute(b, 'tensor', pairs[hop])  9.26 us
    ppermute x4, waiting for transfers between devices, across(): return lax.ppermute(value, 'replica', [(0, 1), (1, 0)]).astype(jnp.float32)  9.04 us
    ppermute x4, starting transfers between devices, across(): return lax.ppermute(value, 'replica', [(0, 1), (1, 0)]).astype(jnp.float32)  5.77 us
    pallas_call x5, Pallas kernels, gradient_part(): pl.pallas_call(functools.partial(gradient_kernel, low, skip, [b[1:] for b...  5.77 us
    convert_element_type x1, other arithmetic, on_device(): early_came = [across(early.astype(jnp.float16))]  2.82 us
    pallas_call x3, Pallas kernels, place(): pl.pallas_call(functools.partial(place_kernel, low), out_shape=tuple((jax...  2.71 us
    convert_element_type x3, other arithmetic, late_part(): return (exact - half + INNER_RATE * step).astype(jnp.float16)  2.14 us
  transfers between devices with their start and end apart: 21, of which 9 were waited for; matrix products, arithmetic and copies ran while one was open for 8% of the time, Pallas kernels for 12%

profile of v5, /device:TPU:0, one launch (start us, length us, event | category | flops | bytes accessed | tf_op | source)
XLA Modules:
  0.0 65.0 jit_solution(6619080370331005347)
XLA Ops:
  0.6 3.1 %collective-permute-start.3 = (bf16[832,256]{1,0:T(8,128)(2,1)}, bf16[832,256]{1,0:T(8,128)(2,1)S(1)}, u32[]{:S(2)}, u32[]{:S(2)}) collective-permute-start(bf16[832,256]{1,0:T(8,128)(2,1)} %bitcast.14), channel_id=1, source_target_pairs={{0,4},{1,5},{4,8},{5,9},{8,12},{9,13},{12,14},{13,15},{14,10},{15,... | collective-permute-start | bytes 1277960 | tf_op jit(solution)/shard_map/ppermute | solution.py:227
  3.7 2.8 %fusion.44 = (f16[448,832]{1,0:T(8,128)(2,1)S(1)}, f32[448,832]{1,0:T(8,128)S(1)}) fusion(f32[832,448]{0,1:T(8,128)} %param.9, f32[832,448]{0,1:T(8,128)} %param.12), kind=kLoop, calls=%fused_computation.69 | loop fusion | flops 1490944 | bytes 5218304 | tf_op jit(solution)/shard_map/convert_element_type | solution.py:237
  6.5 2.0 %collective-permute-start.6 = (f16[448,832]{1,0:T(8,128)(2,1)S(1)}, f16[448,832]{1,0:T(8,128)(2,1)S(1)}, u32[]{:S(2)}, u32[]{:S(2)}) collective-permute-start(f16[448,832]{1,0:T(8,128)(2,1)S(1)} %get-tuple-element.118), channel_id=1, source_target_pairs={{0,16},{16,0},{1,17},{17,1},{2,18},{18,2},{3,19},{19,3},{4,20},{20... | collective-permute-start | bytes 2236424 | tf_op jit(solution)/shard_map/ppermute | solution.py:198
  8.6 5.1 %collective-permute-done.3.refs_2_ = bf16[832,256]{1,0:T(8,128)(2,1)S(1)} collective-permute-done((bf16[832,256]{1,0:T(8,128)(2,1)}, bf16[832,256]{1,0:T(8,128)(2,1)S(1)}, u32[]{:S(2)}, u32[]{:S(2)}) %collective-permute-start.3) | collective-permute-done | bytes 426016 | tf_op jit(solution)/shard_map/ppermute | solution.py:227
  13.7 1.8 %collective-permute-start.4 = (bf16[832,256]{1,0:T(8,128)(2,1)S(1)}, bf16[832,256]{1,0:T(8,128)(2,1)S(1)}, u32[]{:S(2)}, u32[]{:S(2)}) collective-permute-start(bf16[832,256]{1,0:T(8,128)(2,1)S(1)} %collective-permute-done.3.refs_2_), channel_id=1, source_target_pairs={{0,4},{1,5},{4,8},{5,9},{8,12},{9,13},{12,14},{13,15},{14,10},{15,... | collective-permute-start | bytes 1277960 | tf_op jit(solution)/shard_map/ppermute | solution.py:227
  15.5 0.2 collective-permute-start.1
  15.7 0.5 collective-permute-start.9
  16.2 8.5 %collective-permute-done.4.refs_0_ = bf16[832,256]{1,0:T(8,128)(2,1)S(1)} collective-permute-done((bf16[832,256]{1,0:T(8,128)(2,1)S(1)}, bf16[832,256]{1,0:T(8,128)(2,1)S(1)}, u32[]{:S(2)}, u32[]{:S(2)}) %collective-permute-start.4) | collective-permute-done | bytes 426016 | tf_op jit(solution)/shard_map/ppermute | solution.py:227
  24.7 1.5 %collective-permute-start.5 = (bf16[832,256]{1,0:T(8,128)(2,1)S(1)}, bf16[832,256]{1,0:T(8,128)(2,1)S(1)}, u32[]{:S(2)}, u32[]{:S(2)}) collective-permute-start(bf16[832,256]{1,0:T(8,128)(2,1)S(1)} %collective-permute-done.4.refs_0_), channel_id=1, source_target_pairs={{0,4},{1,5},{4,8},{5,9},{8,12},{9,13},{12,14},{13,15},{14,10},{15,... | collective-permute-start | bytes 1277960 | tf_op jit(solution)/shard_map/ppermute | solution.py:227
  26.2 0.5 collective-permute-start.2
  26.7 0.5 collective-permute-start.15
  27.2 0.9 %sort_tokens.1.grad_ref = bf16[448,4096]{1,0:T(8,128)(2,1)S(1)} custom-call(bf16[448,4096]{1,0:T(8,128)(2,1)S(1)} %bitcast.13), custom_call_target="tpu_custom_call" | custom-call | bytes 7340032 | tf_op jit(solution)/shard_map/sort_tokens/pallas_call | solution.py:74
  28.1 0.1 convert_element_type.43
  28.3 1.9 %gradient.5.refs_4_ = f32[448,832]{1,0:T(8,128)S(1)} custom-call(bf16[448,4096]{1,0:T(8,128)(2,1)S(1)} %sort_tokens.1.grad_ref, bf16[832,256]{1,0:T(8,128)(2,1)S(1)} %bitcast.17, bf16[832,256]{1,0:T(8,128)(2,1)S(1)} %collective-permute-done.7.refs_1_, bf16[832,256]{1,0:T(8,128)(2,1)S(1)} %collective-permute-done.3.refs_2_, ...), custom_call_target="tpu_custom_call" | custom-call | flops 1145044992 | bytes 2981888 | tf_op jit(solution)/shard_map/gradient/pallas_call | solution.py:147
  30.2 4.6 %collective-permute-done.5.refs_0_ = bf16[832,256]{1,0:T(8,128)(2,1)S(1)} collective-permute-done((bf16[832,256]{1,0:T(8,128)(2,1)S(1)}, bf16[832,256]{1,0:T(8,128)(2,1)S(1)}, u32[]{:S(2)}, u32[]{:S(2)}) %collective-permute-start.5) | collective-permute-done | bytes 426016 | tf_op jit(solution)/shard_map/ppermute | solution.py:227
  34.8 1.4 %collective-permute-start.12 = (bf16[416,256]{1,0:T(8,128)(2,1)S(1)}, bf16[416,256]{1,0:T(8,128)(2,1)S(1)}, u32[]{:S(2)}, u32[]{:S(2)}) collective-permute-start(bf16[416,256]{1,0:T(8,128)(2,1)S(1)} %slice.128), channel_id=1, source_target_pairs={{0,4},{1,5},{4,8},{5,9},{8,12},{9,13},{12,14},{13,15},{14,10},{15,... | collective-permute-start | bytes 638984 | tf_op jit(solution)/shard_map/ppermute | solution.py:227
  36.2 0.7 %collective-permute-start.13 = (bf16[416,256]{1,0:T(8,128)(2,1)S(1)}, bf16[416,256]{1,0:T(8,128)(2,1)S(1)}, u32[]{:S(2)}, u32[]{:S(2)}) collective-permute-start(bf16[416,256]{1,0:T(8,128)(2,1)S(1)} %slice.127), channel_id=1, source_target_pairs={{0,2},{1,3},{4,0},{5,1},{8,4},{9,5},{12,8},{13,9},{14,12},{15,13},... | collective-permute-start | bytes 638984 | tf_op jit(solution)/shard_map/ppermute | solution.py:227
  36.9 0.5 collective-permute-start.11
  37.4 1.4 %gradient.6.refs_8_ = f32[448,832]{1,0:T(8,128)S(1)} custom-call(bf16[448,4096]{1,0:T(8,128)(2,1)S(1)} %sort_tokens.1.grad_ref, bf16[832,256]{1,0:T(8,128)(2,1)S(1)} %collective-permute-done.4.refs_0_, bf16[832,256]{1,0:T(8,128)(2,1)S(1)} %collective-permute-done.1.refs_1_, bf16[832,256]{1,0:T(8,128)(2,1)S(1)} %collective-permute-done.14.refs_2_, ...), custom_call_target="tpu_custom_call" | custom-call | flops 763363328 | bytes 2981888 | tf_op jit(solution)/shard_map/gradient/pallas_call | solution.py:147
  38.9 0.0 copy-start.2
  38.9 0.0 copy-start.3
  38.9 0.0 copy-start.5
  38.9 1.7 %collective-permute-done.12.refs_4_ = bf16[416,256]{1,0:T(8,128)(2,1)S(1)} collective-permute-done((bf16[416,256]{1,0:T(8,128)(2,1)S(1)}, bf16[416,256]{1,0:T(8,128)(2,1)S(1)}, u32[]{:S(2)}, u32[]{:S(2)}) %collective-permute-start.12) | collective-permute-done | bytes 213024 | tf_op jit(solution)/shard_map/ppermute | solution.py:227
  40.7 1.4 %collective-permute-done.13.refs_5_ = bf16[416,256]{1,0:T(8,128)(2,1)S(1)} collective-permute-done((bf16[416,256]{1,0:T(8,128)(2,1)S(1)}, bf16[416,256]{1,0:T(8,128)(2,1)S(1)}, u32[]{:S(2)}, u32[]{:S(2)}) %collective-permute-start.13) | collective-permute-done | bytes 213024 | tf_op jit(solution)/shard_map/ppermute | solution.py:227
  42.1 0.0 collective-permute-done.16.refs_6_
  42.1 1.4 %collective-permute-done.17.refs_7_ = bf16[416,256]{1,0:T(8,128)(2,1)S(1)} collective-permute-done((bf16[416,256]{1,0:T(8,128)(2,1)S(1)}, bf16[416,256]{1,0:T(8,128)(2,1)S(1)}, u32[]{:S(2)}, u32[]{:S(2)}) %collective-permute-start.17) | collective-permute-done | bytes 213024 | tf_op jit(solution)/shard_map/ppermute | solution.py:230
  43.5 0.7 %gradient.7 = f32[448,256]{1,0:T(8,128)S(1)} custom-call(bf16[448,4096]{1,0:T(8,128)(2,1)S(1)} %sort_tokens.1.grad_ref, bf16[832,256]{1,0:T(8,128)(2,1)S(1)} %collective-permute-done.5.refs_0_, bf16[832,256]{1,0:T(8,128)(2,1)S(1)} %collective-permute-done.2.refs_1_, bf16[832,256]{1,0:T(8,128)(2,1)S(1)} %collective-permute-done.10.refs_2_, ...), custom_call_target="tpu_custom_call" | custom-call | flops 352321536 | bytes 917504 | tf_op jit(solution)/shard_map/gradient/pallas_call | solution.py:147
  44.3 0.6 fusion.17
  44.9 1.6 %collective-permute-start.18 = (f16[448,256]{1,0:T(8,128)(2,1)S(1)}, f16[448,256]{1,0:T(8,128)(2,1)S(1)}, u32[]{:S(2)}, u32[]{:S(2)}) collective-permute-start(f16[448,256]{1,0:T(8,128)(2,1)S(1)} %fusion.17), channel_id=1, source_target_pairs={{0,16},{16,0},{1,17},{17,1},{2,18},{18,2},{3,19},{19,3},{4,20},{20... | collective-permute-start | bytes 688136 | tf_op jit(solution)/shard_map/ppermute | solution.py:198
  46.5 1.1 %gradient.8 = f32[448,384]{1,0:T(8,128)S(1)} custom-call(bf16[448,4096]{1,0:T(8,128)(2,1)S(1)} %sort_tokens.1.grad_ref, bf16[832,256]{1,0:T(8,128)(2,1)S(1)} %collective-permute-done.5.refs_0_, bf16[832,256]{1,0:T(8,128)(2,1)S(1)} %collective-permute-done.2.refs_1_, bf16[832,256]{1,0:T(8,128)(2,1)S(1)} %collective-permute-done.10.refs_2_, ...), custom_call_target="tpu_custom_call" | custom-call | flops 528482304 | bytes 1376256 | tf_op jit(solution)/shard_map/gradient/pallas_call | solution.py:147
  47.6 0.9 %fusion.1 = f16[448,384]{1,0:T(8,128)(2,1)S(1)} fusion(f32[448,384]{1,0:T(8,128)S(1)} %gradient.8, f32[448,832]{1,0:T(8,128)S(1)} %bitcast.35, f32[448,832]{1,0:T(8,128)S(1)} %bitcast.38, f32[448,832]{1,0:T(8,128)S(1)} %bitcast.25, f32[448,832]{1,0:T(8,128)S(1)} %bitcast.19), kind=kLoop, calls=%fused_computation.4 | loop fusion | flops 3096576 | bytes 3784704 | tf_op jit(solution)/shard_map/convert_element_type | solution.py:176
  48.5 0.6 collective-permute-start.20
  49.1 4.4 %collective-permute-done.18 = f16[448,256]{1,0:T(8,128)(2,1)S(1)} collective-permute-done((f16[448,256]{1,0:T(8,128)(2,1)S(1)}, f16[448,256]{1,0:T(8,128)(2,1)S(1)}, u32[]{:S(2)}, u32[]{:S(2)}) %collective-permute-start.18) | collective-permute-done | bytes 229408 | tf_op jit(solution)/shard_map/ppermute | solution.py:198
  53.5 0.7 %gradient.9 = f32[448,192]{1,0:T(8,128)S(1)} custom-call(bf16[448,4096]{1,0:T(8,128)(2,1)S(1)} %sort_tokens.1.grad_ref, bf16[832,256]{1,0:T(8,128)(2,1)S(1)} %collective-permute-done.5.refs_0_, bf16[832,256]{1,0:T(8,128)(2,1)S(1)} %collective-permute-done.2.refs_1_, bf16[832,256]{1,0:T(8,128)(2,1)S(1)} %collective-permute-done.10.refs_2_, ...), custom_call_target="tpu_custom_call" | custom-call | flops 264241152 | bytes 688128 | tf_op jit(solution)/shard_map/gradient/pallas_call | solution.py:147
  54.1 0.6 fusion.15
  54.8 0.1 maximum_maximum_fusion
  54.9 1.6 %collective-permute-start.19 = (f16[672,128]{1,0:T(8,128)(2,1)S(1)}, f16[672,128]{1,0:T(8,128)(2,1)S(1)}, u32[]{:S(2)}, u32[]{:S(2)}) collective-permute-start(f16[672,128]{1,0:T(8,128)(2,1)S(1)} %maximum_maximum_fusion), channel_id=1, source_target_pairs={{0,16},{16,0},{1,17},{17,1},{2,18},{18,2},{3,19},{19,3},{4,20},{20... | collective-permute-start | bytes 516104 | tf_op jit(solution)/shard_map/ppermute | solution.py:198
  56.5 0.1 fusion.30
  56.7 0.1 subtract_convert_fusion.1.refs_0_
  56.8 0.9 %place.3 = (bf16[448,832]{1,0:T(8,128)(2,1)}, f32[448,832]{1,0:T(8,128)}) custom-call(bf16[448,256]{1,0:T(8,128)(2,1)S(1)} %subtract_convert_fusion.1.refs_0_, f32[448,256]{1,0:T(8,128)S(1)} %get-tuple-element.114.refs_1_), custom_call_target="tpu_custom_call" | custom-call | bytes 1376256 | tf_op jit(solution)/shard_map/place/pallas_call | solution.py:99
  57.7 3.1 %collective-permute-done.20 = f16[448,384]{1,0:T(8,128)(2,1)S(1)} collective-permute-done((f16[448,384]{1,0:T(8,128)(2,1)S(1)}, f16[448,384]{1,0:T(8,128)(2,1)S(1)}, u32[]{:S(2)}, u32[]{:S(2)}) %collective-permute-start.20) | collective-permute-done | bytes 344096 | tf_op jit(solution)/shard_map/ppermute | solution.py:198
  60.8 0.3 fusion.8
  61.1 1.0 %place.4 = (bf16[448,832]{1,0:T(8,128)(2,1)}, f32[448,832]{1,0:T(8,128)}) custom-call(bf16[448,384]{1,0:T(8,128)(2,1)S(1)} %get-tuple-element.121.refs_0_, f32[448,384]{1,0:T(8,128)S(1)} %get-tuple-element.120.refs_1_, bf16[448,832]{1,0:T(8,128)(2,1)} %get-tuple-element.108.refs_2_, ...), custom_call_target="tpu_custom_call", output_to_operand_aliasing={{0}: (2, {}), {1}: (3, {})} | custom-call | bytes 2064384 | tf_op jit(solution)/shard_map/place/pallas_call | solution.py:99
  62.1 1.6 %collective-permute-done.19 = f16[672,128]{1,0:T(8,128)(2,1)S(1)} collective-permute-done((f16[672,128]{1,0:T(8,128)(2,1)S(1)}, f16[672,128]{1,0:T(8,128)(2,1)S(1)}, u32[]{:S(2)}, u32[]{:S(2)}) %collective-permute-start.19) | collective-permute-done | bytes 172064 | tf_op jit(solution)/shard_map/ppermute | solution.py:198
  63.7 0.1 fusion.45
  63.8 0.2 fusion.33
  64.0 0.1 subtract_convert_fusion.2.refs_0_
  64.1 0.9 %place.5 = (bf16[448,832]{1,0:T(8,128)(2,1)}, f32[448,832]{1,0:T(8,128)}) custom-call(bf16[448,192]{1,0:T(8,128)(2,1)S(1)} %subtract_convert_fusion.2.refs_0_, f32[448,192]{1,0:T(8,128)S(1)} %get-tuple-element.116.refs_1_, bf16[448,832]{1,0:T(8,128)(2,1)} %get-tuple-element.110.refs_2_, ...), custom_call_target="tpu_custom_call", output_to_operand_aliasing={{0}: (2, {}), {1}: (3, {})} | custom-call | bytes 1032192 | tf_op jit(solution)/shard_map/place/pallas_call | solution.py:99
  (36 shorter events, 0.2 us)
Async XLA Ops:
  0.6 8.0 %copy-start.1 = (bf16[256,832]{0,1:T(8,128)(2,1)S(1)}, bf16[256,832]{0,1:T(8,128)(2,1)}, u32[]{:S(2)}) copy-start(bf16[256,832]{0,1:T(8,128)(2,1)} %param.7) | copy-start | bytes 1277956
  0.6 26.6 %copy-start = (bf16[4096,448]{0,1:T(8,128)(2,1)S(1)}, bf16[4096,448]{0,1:T(8,128)(2,1)}, u32[]{:S(2)}) copy-start(bf16[4096,448]{0,1:T(8,128)(2,1)} %param.8) | copy-start | bytes 11010052
  0.6 13.0 %collective-permute-start.3 = (bf16[832,256]{1,0:T(8,128)(2,1)}, bf16[832,256]{1,0:T(8,128)(2,1)S(1)}, u32[]{:S(2)}, u32[]{:S(2)}) collective-permute-start(bf16[832,256]{1,0:T(8,128)(2,1)} %bitcast.14), channel_id=1, source_target_pairs={{0,4},{1,5},{4,8},{5,9},{8,12},{9,13},{12,14},{13,15},{14,10},{15,... | collective-permute-start | bytes 1277960 | tf_op jit(solution)/shard_map/ppermute | solution.py:227
  3.7 11.8 %collective-permute-start = (bf16[832,256]{1,0:T(8,128)(2,1)}, bf16[832,256]{1,0:T(8,128)(2,1)S(1)}, u32[]{:S(2)}, u32[]{:S(2)}) collective-permute-start(bf16[832,256]{1,0:T(8,128)(2,1)} %bitcast.15), channel_id=1, source_target_pairs={{0,2},{1,3},{4,0},{5,1},{8,4},{9,5},{12,8},{13,9},{14,12},{15,13},... | collective-permute-start | bytes 1277960 | tf_op jit(solution)/shard_map/ppermute | solution.py:227
  6.5 20.2 %collective-permute-start.6 = (f16[448,832]{1,0:T(8,128)(2,1)S(1)}, f16[448,832]{1,0:T(8,128)(2,1)S(1)}, u32[]{:S(2)}, u32[]{:S(2)}) collective-permute-start(f16[448,832]{1,0:T(8,128)(2,1)S(1)} %get-tuple-element.118), channel_id=1, source_target_pairs={{0,16},{16,0},{1,17},{17,1},{2,18},{18,2},{3,19},{19,3},{4,20},{20... | collective-permute-start | bytes 2236424 | tf_op jit(solution)/shard_map/ppermute | solution.py:198
  8.6 7.1 %collective-permute-start.7 = (bf16[832,256]{1,0:T(8,128)(2,1)S(1)}, bf16[832,256]{1,0:T(8,128)(2,1)S(1)}, u32[]{:S(2)}, u32[]{:S(2)}) collective-permute-start(bf16[832,256]{1,0:T(8,128)(2,1)S(1)} %bitcast.16), channel_id=1, source_target_pairs={{0,1},{1,0},{2,3},{3,2},{4,5},{5,4},{6,7},{7,6},{8,9},{9,8},{10,11... | collective-permute-start | bytes 1277960 | tf_op jit(solution)/shard_map/ppermute | solution.py:230
  13.7 11.0 %collective-permute-start.4 = (bf16[832,256]{1,0:T(8,128)(2,1)S(1)}, bf16[832,256]{1,0:T(8,128)(2,1)S(1)}, u32[]{:S(2)}, u32[]{:S(2)}) collective-permute-start(bf16[832,256]{1,0:T(8,128)(2,1)S(1)} %collective-permute-done.3.refs_2_), channel_id=1, source_target_pairs={{0,4},{1,5},{4,8},{5,9},{8,12},{9,13},{12,14},{13,15},{14,10},{15,... | collective-permute-start | bytes 1277960 | tf_op jit(solution)/shard_map/ppermute | solution.py:227
  15.5 10.7 %collective-permute-start.1 = (bf16[832,256]{1,0:T(8,128)(2,1)S(1)}, bf16[832,256]{1,0:T(8,128)(2,1)S(1)}, u32[]{:S(2)}, u32[]{:S(2)}) collective-permute-start(bf16[832,256]{1,0:T(8,128)(2,1)S(1)} %collective-permute-done.refs_3_), channel_id=1, source_target_pairs={{0,2},{1,3},{4,0},{5,1},{8,4},{9,5},{12,8},{13,9},{14,12},{15,13},... | collective-permute-start | bytes 1277960 | tf_op jit(solution)/shard_map/ppermute | solution.py:227
  15.7 11.0 %collective-permute-start.8 = (bf16[832,256]{1,0:T(8,128)(2,1)S(1)}, bf16[832,256]{1,0:T(8,128)(2,1)S(1)}, u32[]{:S(2)}, u32[]{:S(2)}) collective-permute-start(bf16[832,256]{1,0:T(8,128)(2,1)S(1)} %collective-permute-done.3.refs_2_), channel_id=1, source_target_pairs={{0,1},{1,0},{2,3},{3,2},{4,5},{5,4},{6,7},{7,6},{8,9},{9,8},{10,11... | collective-permute-start | bytes 1277960 | tf_op jit(solution)/shard_map/ppermute | solution.py:230
  15.7 12.6 %collective-permute-start.9 = (bf16[832,256]{1,0:T(8,128)(2,1)S(1)}, bf16[832,256]{1,0:T(8,128)(2,1)S(1)}, u32[]{:S(2)}, u32[]{:S(2)}) collective-permute-start(bf16[832,256]{1,0:T(8,128)(2,1)S(1)} %collective-permute-done.refs_3_), channel_id=1, source_target_pairs={{0,1},{1,0},{2,3},{3,2},{4,5},{5,4},{6,7},{7,6},{8,9},{9,8},{10,11... | collective-permute-start | bytes 1277960 | tf_op jit(solution)/shard_map/ppermute | solution.py:230
  24.7 10.1 %collective-permute-start.5 = (bf16[832,256]{1,0:T(8,128)(2,1)S(1)}, bf16[832,256]{1,0:T(8,128)(2,1)S(1)}, u32[]{:S(2)}, u32[]{:S(2)}) collective-permute-start(bf16[832,256]{1,0:T(8,128)(2,1)S(1)} %collective-permute-done.4.refs_0_), channel_id=1, source_target_pairs={{0,4},{1,5},{4,8},{5,9},{8,12},{9,13},{12,14},{13,15},{14,10},{15,... | collective-permute-start | bytes 1277960 | tf_op jit(solution)/shard_map/ppermute | solution.py:227
  26.2 10.0 %collective-permute-start.2 = (bf16[832,256]{1,0:T(8,128)(2,1)S(1)}, bf16[832,256]{1,0:T(8,128)(2,1)S(1)}, u32[]{:S(2)}, u32[]{:S(2)}) collective-permute-start(bf16[832,256]{1,0:T(8,128)(2,1)S(1)} %collective-permute-done.1.refs_1_), channel_id=1, source_target_pairs={{0,2},{1,3},{4,0},{5,1},{8,4},{9,5},{12,8},{13,9},{14,12},{15,13},... | collective-permute-start | bytes 1277960 | tf_op jit(solution)/shard_map/ppermute | solution.py:227
  26.7 10.2 %collective-permute-start.14 = (bf16[832,256]{1,0:T(8,128)(2,1)S(1)}, bf16[832,256]{1,0:T(8,128)(2,1)S(1)}, u32[]{:S(2)}, u32[]{:S(2)}) collective-permute-start(bf16[832,256]{1,0:T(8,128)(2,1)S(1)} %collective-permute-done.4.refs_0_), channel_id=1, source_target_pairs={{0,1},{1,0},{2,3},{3,2},{4,5},{5,4},{6,7},{7,6},{8,9},{9,8},{10,11... | collective-permute-start | bytes 1277960 | tf_op jit(solution)/shard_map/ppermute | solution.py:230
  26.7 10.7 %collective-permute-start.15 = (bf16[832,256]{1,0:T(8,128)(2,1)S(1)}, bf16[832,256]{1,0:T(8,128)(2,1)S(1)}, u32[]{:S(2)}, u32[]{:S(2)}) collective-permute-start(bf16[832,256]{1,0:T(8,128)(2,1)S(1)} %collective-permute-done.1.refs_1_), channel_id=1, source_target_pairs={{0,1},{1,0},{2,3},{3,2},{4,5},{5,4},{6,7},{7,6},{8,9},{9,8},{10,11... | collective-permute-start | bytes 1277960 | tf_op jit(solution)/shard_map/ppermute | solution.py:230
  34.8 5.9 %collective-permute-start.12 = (bf16[416,256]{1,0:T(8,128)(2,1)S(1)}, bf16[416,256]{1,0:T(8,128)(2,1)S(1)}, u32[]{:S(2)}, u32[]{:S(2)}) collective-permute-start(bf16[416,256]{1,0:T(8,128)(2,1)S(1)} %slice.128), channel_id=1, source_target_pairs={{0,4},{1,5},{4,8},{5,9},{8,12},{9,13},{12,14},{13,15},{14,10},{15,... | collective-permute-start | bytes 638984 | tf_op jit(solution)/shard_map/ppermute | solution.py:227
  36.2 5.9 %collective-permute-start.13 = (bf16[416,256]{1,0:T(8,128)(2,1)S(1)}, bf16[416,256]{1,0:T(8,128)(2,1)S(1)}, u32[]{:S(2)}, u32[]{:S(2)}) collective-permute-start(bf16[416,256]{1,0:T(8,128)(2,1)S(1)} %slice.127), channel_id=1, source_target_pairs={{0,2},{1,3},{4,0},{5,1},{8,4},{9,5},{12,8},{13,9},{14,12},{15,13},... | collective-permute-start | bytes 638984 | tf_op jit(solution)/shard_map/ppermute | solution.py:227
  36.9 5.2 %collective-permute-start.10 = (bf16[832,256]{1,0:T(8,128)(2,1)S(1)}, bf16[832,256]{1,0:T(8,128)(2,1)S(1)}, u32[]{:S(2)}, u32[]{:S(2)}) collective-permute-start(bf16[832,256]{1,0:T(8,128)(2,1)S(1)} %collective-permute-done.5.refs_0_), channel_id=1, source_target_pairs={{0,1},{1,0},{2,3},{3,2},{4,5},{5,4},{6,7},{7,6},{8,9},{9,8},{10,11... | collective-permute-start | bytes 1277960 | tf_op jit(solution)/shard_map/ppermute | solution.py:230
  36.9 5.2 %collective-permute-start.11 = (bf16[832,256]{1,0:T(8,128)(2,1)S(1)}, bf16[832,256]{1,0:T(8,128)(2,1)S(1)}, u32[]{:S(2)}, u32[]{:S(2)}) collective-permute-start(bf16[832,256]{1,0:T(8,128)(2,1)S(1)} %collective-permute-done.2.refs_1_), channel_id=1, source_target_pairs={{0,1},{1,0},{2,3},{3,2},{4,5},{5,4},{6,7},{7,6},{8,9},{9,8},{10,11... | collective-permute-start | bytes 1277960 | tf_op jit(solution)/shard_map/ppermute | solution.py:230
  38.9 5.4 %copy-start.2 = (f32[832,448]{0,1:T(8,128)S(1)}, f32[832,448]{0,1:T(8,128)}, u32[]{:S(2)}) copy-start(f32[832,448]{0,1:T(8,128)} %param.12) | copy-start | bytes 4472836
  38.9 5.4 %copy-start.3 = (f32[832,448]{0,1:T(8,128)S(1)}, f32[832,448]{0,1:T(8,128)}, u32[]{:S(2)}) copy-start(f32[832,448]{0,1:T(8,128)} %param.9) | copy-start | bytes 4472836
  38.9 5.4 %copy-start.5 = (f32[832,448]{0,1:T(8,128)S(1)}, f32[832,448]{0,1:T(8,128)}, u32[]{:S(2)}) copy-start(f32[832,448]{0,1:T(8,128)} %param.11) | copy-start | bytes 4472836
  38.9 5.4 %copy-start.6 = (f32[832,448]{0,1:T(8,128)S(1)}, f32[832,448]{0,1:T(8,128)}, u32[]{:S(2)}) copy-start(f32[832,448]{0,1:T(8,128)} %param.10) | copy-start | bytes 4472836
  40.7 1.5 %collective-permute-start.16 = (bf16[416,256]{1,0:T(8,128)(2,1)S(1)}, bf16[416,256]{1,0:T(8,128)(2,1)S(1)}, u32[]{:S(2)}, u32[]{:S(2)}) collective-permute-start(bf16[416,256]{1,0:T(8,128)(2,1)S(1)} %collective-permute-done.12.refs_4_), channel_id=1, source_target_pairs={{0,1},{1,0},{2,3},{3,2},{4,5},{5,4},{6,7},{7,6},{8,9},{9,8},{10,11... | collective-permute-start | bytes 638984 | tf_op jit(solution)/shard_map/ppermute | solution.py:230
  42.1 1.5 %collective-permute-start.17 = (bf16[416,256]{1,0:T(8,128)(2,1)S(1)}, bf16[416,256]{1,0:T(8,128)(2,1)S(1)}, u32[]{:S(2)}, u32[]{:S(2)}) collective-permute-start(bf16[416,256]{1,0:T(8,128)(2,1)S(1)} %collective-permute-done.13.refs_5_), channel_id=1, source_target_pairs={{0,1},{1,0},{2,3},{3,2},{4,5},{5,4},{6,7},{7,6},{8,9},{9,8},{10,11... | collective-permute-start | bytes 638984 | tf_op jit(solution)/shard_map/ppermute | solution.py:230
  44.9 8.5 %collective-permute-start.18 = (f16[448,256]{1,0:T(8,128)(2,1)S(1)}, f16[448,256]{1,0:T(8,128)(2,1)S(1)}, u32[]{:S(2)}, u32[]{:S(2)}) collective-permute-start(f16[448,256]{1,0:T(8,128)(2,1)S(1)} %fusion.17), channel_id=1, source_target_pairs={{0,16},{16,0},{1,17},{17,1},{2,18},{18,2},{3,19},{19,3},{4,20},{20... | collective-permute-start | bytes 688136 | tf_op jit(solution)/shard_map/ppermute | solution.py:198
  48.5 12.3 %collective-permute-start.20 = (f16[448,384]{1,0:T(8,128)(2,1)S(1)}, f16[448,384]{1,0:T(8,128)(2,1)S(1)}, u32[]{:S(2)}, u32[]{:S(2)}) collective-permute-start(f16[448,384]{1,0:T(8,128)(2,1)S(1)} %fusion.1), channel_id=1, source_target_pairs={{0,16},{16,0},{1,17},{17,1},{2,18},{18,2},{3,19},{19,3},{4,20},{20... | collective-permute-start | bytes 1032200 | tf_op jit(solution)/shard_map/ppermute | solution.py:198
  54.1 2.4 %copy-start.4 = (f32[832,448]{0,1:T(8,128)S(1)}, f32[832,448]{0,1:T(8,128)}, u32[]{:S(2)}) copy-start(f32[832,448]{0,1:T(8,128)} %param.13) | copy-start | bytes 4472836
  54.9 8.7 %collective-permute-start.19 = (f16[672,128]{1,0:T(8,128)(2,1)S(1)}, f16[672,128]{1,0:T(8,128)(2,1)S(1)}, u32[]{:S(2)}, u32[]{:S(2)}) collective-permute-start(f16[672,128]{1,0:T(8,128)(2,1)S(1)} %maximum_maximum_fusion), channel_id=1, source_target_pairs={{0,16},{16,0},{1,17},{17,1},{2,18},{18,2},{3,19},{19,3},{4,20},{20... | collective-permute-start | bytes 516104 | tf_op jit(solution)/shard_map/ppermute | solution.py:198
